TPU v7x, 32 devices: a whole 2x2x4 slice. The times are simulated.
32 devices in a mesh: dp: 32 (over z, y, x, core).
Axes of the slice: x: 2, y: 2, z: 4, core: 2. Of those that a mesh axis runs over, the one named last changes fastest.
Arguments:
- tokens: bfloat16 [32768, 1024], P('dp'), may hold values from -6 to 6
- w_query: bfloat16 [1024, 1024], P('dp'), may hold values from -0.1875 to 0.1875
- w_key: bfloat16 [1024, 1024], P('dp'), may hold values from -0.1875 to 0.1875
- w_value: bfloat16 [1024, 1024], P('dp'), may hold values from -0.1875 to 0.1875
- w_out: bfloat16 [1024, 1024], P('dp'), may hold values from -0.75 to 0.75
- w_up: bfloat16 [1024, 4096], P('dp'), may hold values from -0.1875 to 0.1875
- w_down: bfloat16 [4096, 1024], P('dp'), may hold values from -0.09375 to 0.09375
- b_query: bfloat16 [1024], P('dp'), may hold values from -3 to 3
- b_value: bfloat16 [1024], P('dp'), may hold values from -3 to 3
- b_out: bfloat16 [1024], P('dp'), may hold values from -3 to 3
- b_up: bfloat16 [4096], P('dp'), may hold values from -3 to 3
- b_down: bfloat16 [1024], P('dp'), may hold values from -3 to 3
- gain_attn: bfloat16 [1024], P('dp'), may hold values from 0.25 to 1.75
- shift_attn: bfloat16 [1024], P('dp'), may hold values from -3 to 3
- gain_ffn: bfloat16 [1024], P('dp'), may hold values from 0.25 to 1.75
- shift_ffn: bfloat16 [1024], P('dp'), may hold values from -3 to 3
- cotangent: bfloat16 [32768, 1024], P('dp'), may hold values from -6 to 6
Outputs:
- layer_out: bfloat16 [32768, 1024], P('dp')
- grad_tokens: bfloat16 [32768, 1024], P('dp')
- grad_w_query: float32 [1024, 1024], P('dp')
- grad_w_key: float32 [1024, 1024], P('dp')
- grad_w_value: float32 [1024, 1024], P('dp')
- grad_w_out: float32 [1024, 1024], P('dp')
- grad_w_up: float32 [1024, 4096], P('dp')
- grad_w_down: float32 [4096, 1024], P('dp')
- grad_b_query: float32 [1024], P('dp')
- grad_b_value: float32 [1024], P('dp')
- grad_b_out: float32 [1024], P('dp')
- grad_b_up: float32 [4096], P('dp')
- grad_b_down: float32 [1024], P('dp')
- grad_gain_attn: float32 [1024], P('dp')
- grad_shift_attn: float32 [1024], P('dp')
- grad_gain_ffn: float32 [1024], P('dp')
- grad_shift_ffn: float32 [1024], P('dp')
All inputs are finite; a program needn't handle non-finite values.
Results may differ from a plain program's by a relative error of at most 0.015.
Values may be sent and summed in bfloat16 or wider, within the bound.
No kernel may reach another device: no remote copies, remote signals or barrier semaphores. Data moves between devices by JAX's collectives and lax.ppermute only.
A program may use at most 256 MiB of HBM per device.

v0:
```python
import jax
import jax.numpy as jnp
from jax import lax
from jax.sharding import PartitionSpec as P

D = 1024
HEADS = 16
LEN = 512
MICRO = 2


EPS = 1e-12


def matmul(left_side, right_side):
    return jnp.dot(left_side, right_side, preferred_element_type=jnp.float32)


def layer_norm(summed, gain_vec, shift_vec):
    centre = jnp.mean(summed, axis=-1, keepdims=True)
    centered = summed - centre
    spread = jnp.mean(centered * centered, axis=-1, keepdims=True)
    inverse = lax.rsqrt(spread + EPS)
    normed = centered * inverse
    return (normed * gain_vec + shift_vec, normed, inverse)


def norm_back(upstream, gain_vec, normed, inverse):
    scaled = upstream * gain_vec
    mean_grad = jnp.mean(scaled, axis=-1, keepdims=True)
    mean_cross = jnp.mean(scaled * normed, axis=-1, keepdims=True)
    return inverse * (scaled - mean_grad - normed * mean_cross)


def exact_gelu(point):
    return jax.nn.gelu(point, approximate=False)


def column_sum(grad_rows):
    return jnp.sum(grad_rows.astype(jnp.float32), axis=0)


def forward_pass(rows_in, gathered):
    (
        w_query,
        w_key,
        w_value,
        w_out,
        w_up,
        w_down,
        b_query,
        b_value,
        b_out,
        b_up,
        b_down,
        gain_attn,
        shift_attn,
        gain_ffn,
        shift_ffn,
    ) = gathered
    row_count = rows_in.shape[0]
    seq_count = row_count // LEN
    head_dim = D // HEADS
    score_scale = head_dim ** (-0.5)
    head_shape = (seq_count, LEN, HEADS, head_dim)
    queries = (matmul(rows_in, w_query) + b_query.astype(jnp.float32)).astype(jnp.bfloat16)
    key_rows = matmul(rows_in, w_key).astype(jnp.bfloat16)
    values = (matmul(rows_in, w_value) + b_value.astype(jnp.float32)).astype(jnp.bfloat16)
    scores = score_scale * jnp.einsum(
        "sqhe,skhe->shqk",
        queries.reshape(head_shape),
        key_rows.reshape(head_shape),
        preferred_element_type=jnp.float32,
    )
    maxima = jnp.max(scores, axis=-1, keepdims=True)
    exponent = jnp.exp(scores - maxima)
    row_totals = jnp.sum(exponent, axis=-1, keepdims=True)
    attn_probs = exponent / row_totals
    logsum = maxima + jnp.log(row_totals)
    mixed = jnp.einsum(
        "shqk,skhe->sqhe",
        attn_probs.astype(jnp.bfloat16),
        values.reshape(head_shape),
        preferred_element_type=jnp.float32,
    )
    attn_rows = mixed.reshape(row_count, D).astype(jnp.bfloat16)
    branch = matmul(attn_rows, w_out) + b_out.astype(jnp.float32)
    first_out, first_normed, first_inverse = layer_norm(
        rows_in.astype(jnp.float32) + branch,
        gain_attn.astype(jnp.float32),
        shift_attn.astype(jnp.float32),
    )
    first_low = first_out.astype(jnp.bfloat16)
    pre_act = matmul(first_low, w_up) + b_up.astype(jnp.float32)
    hidden = exact_gelu(pre_act).astype(jnp.bfloat16)
    ffn_out = matmul(hidden, w_down) + b_down.astype(jnp.float32)
    result, second_normed, second_inverse = layer_norm(
        first_out + ffn_out, gain_ffn.astype(jnp.float32), shift_ffn.astype(jnp.float32)
    )
    stored = (
        queries,
        key_rows,
        values,
        logsum,
        attn_rows,
        first_normed,
        first_inverse,
        first_low,
        pre_act,
        hidden,
        second_normed,
        second_inverse,
    )
    return (result, stored)


def backward_pass(rows_in, cot_rows, gathered, stored):
    (
        w_query,
        w_key,
        w_value,
        w_out,
        w_up,
        w_down,
        b_query,
        b_value,
        b_out,
        b_up,
        b_down,
        gain_attn,
        shift_attn,
        gain_ffn,
        shift_ffn,
    ) = gathered
    (
        queries,
        key_rows,
        values,
        logsum,
        attn_rows,
        first_normed,
        first_inverse,
        first_low,
        pre_act,
        hidden,
        second_normed,
        second_inverse,
    ) = stored
    row_count = rows_in.shape[0]
    seq_count = row_count // LEN
    head_dim = D // HEADS
    score_scale = head_dim ** (-0.5)
    head_shape = (seq_count, LEN, HEADS, head_dim)
    upstream = cot_rows.astype(jnp.float32)
    d_gain_ffn = jnp.sum(upstream * second_normed, axis=0)
    d_shift_ffn = jnp.sum(upstream, axis=0)
    d_second = norm_back(upstream, gain_ffn.astype(jnp.float32), second_normed, second_inverse)
    d_ffn = d_second.astype(jnp.bfloat16)
    d_b_down = column_sum(d_ffn)
    d_w_down = jnp.einsum("tf,td->fd", hidden, d_ffn, preferred_element_type=jnp.float32)
    d_hidden = jnp.einsum("td,fd->tf", d_ffn, w_down, preferred_element_type=jnp.float32)
    gelu_pull = jax.vjp(exact_gelu, pre_act)[1]
    d_pre = gelu_pull(d_hidden)[0].astype(jnp.bfloat16)
    d_b_up = column_sum(d_pre)
    d_w_up = jnp.einsum("td,tf->df", first_low, d_pre, preferred_element_type=jnp.float32)
    d_first = d_second + jnp.einsum("tf,df->td", d_pre, w_up, preferred_element_type=jnp.float32)
    d_gain_attn = jnp.sum(d_first * first_normed, axis=0)
    d_shift_attn = jnp.sum(d_first, axis=0)
    d_resid = norm_back(d_first, gain_attn.astype(jnp.float32), first_normed, first_inverse)
    d_branch = d_resid.astype(jnp.bfloat16)
    d_b_out = column_sum(d_branch)
    d_w_out = jnp.einsum("ti,to->io", attn_rows, d_branch, preferred_element_type=jnp.float32)
    d_attn = jnp.einsum("to,io->ti", d_branch, w_out, preferred_element_type=jnp.float32).astype(
        jnp.bfloat16
    )
    query_heads = queries.reshape(head_shape)
    key_heads = key_rows.reshape(head_shape)
    value_heads = values.reshape(head_shape)
    grad_heads = d_attn.reshape(head_shape)
    scores = score_scale * jnp.einsum(
        "sqhe,skhe->shqk", query_heads, key_heads, preferred_element_type=jnp.float32
    )
    attn_probs = jnp.exp(scores - logsum)
    d_probs = jnp.einsum(
        "sqhe,skhe->shqk", grad_heads, value_heads, preferred_element_type=jnp.float32
    )
    d_probs = lax.optimization_barrier(d_probs.astype(jnp.bfloat16)).astype(jnp.float32)
    d_values = (
        jnp.einsum(
            "shqk,sqhe->skhe",
            attn_probs.astype(jnp.bfloat16),
            grad_heads,
            preferred_element_type=jnp.float32,
        )
        .reshape(row_count, D)
        .astype(jnp.bfloat16)
    )
    d_scores = (
        attn_probs * (d_probs - jnp.sum(d_probs * attn_probs, axis=-1, keepdims=True))
    ).astype(jnp.bfloat16)
    d_queries = (
        (
            score_scale
            * jnp.einsum("shqk,skhe->sqhe", d_scores, key_heads, preferred_element_type=jnp.float32)
        )
        .reshape(row_count, D)
        .astype(jnp.bfloat16)
    )
    d_keys = (
        (
            score_scale
            * jnp.einsum(
                "shqk,sqhe->skhe", d_scores, query_heads, preferred_element_type=jnp.float32
            )
        )
        .reshape(row_count, D)
        .astype(jnp.bfloat16)
    )
    d_b_query = column_sum(d_queries)
    d_b_value = column_sum(d_values)
    d_w_query = jnp.einsum("ti,to->io", rows_in, d_queries, preferred_element_type=jnp.float32)
    d_w_key = jnp.einsum("ti,to->io", rows_in, d_keys, preferred_element_type=jnp.float32)
    d_w_value = jnp.einsum("ti,to->io", rows_in, d_values, preferred_element_type=jnp.float32)
    grad_rows = d_resid + jnp.einsum(
        "to,io->ti", d_queries, w_query, preferred_element_type=jnp.float32
    )
    grad_rows = grad_rows + jnp.einsum(
        "to,io->ti", d_keys, w_key, preferred_element_type=jnp.float32
    )
    grad_rows = grad_rows + jnp.einsum(
        "to,io->ti", d_values, w_value, preferred_element_type=jnp.float32
    )
    gradients = (
        d_w_query,
        d_w_key,
        d_w_value,
        d_w_out,
        d_w_up,
        d_w_down,
        d_b_query,
        d_b_value,
        d_b_out,
        d_b_up,
        d_b_down,
        d_gain_attn,
        d_shift_attn,
        d_gain_ffn,
        d_shift_ffn,
    )
    return (gradients, grad_rows)


def local(
    tokens,
    w_query,
    w_key,
    w_value,
    w_out,
    w_up,
    w_down,
    b_query,
    b_value,
    b_out,
    b_up,
    b_down,
    gain_attn,
    shift_attn,
    gain_ffn,
    shift_ffn,
    cotangent,
):
    micro_rows = tokens.shape[0] // MICRO
    outputs = []
    input_grads = []
    running = None
    for micro_step in range(MICRO):
        rows_in = lax.slice_in_dim(
            tokens, micro_step * micro_rows, (micro_step + 1) * micro_rows, axis=0
        )
        cot_rows = lax.slice_in_dim(
            cotangent, micro_step * micro_rows, (micro_step + 1) * micro_rows, axis=0
        )
        gathered = (
            lax.all_gather(w_query, "dp", axis=0, tiled=True),
            lax.all_gather(w_key, "dp", axis=0, tiled=True),
            lax.all_gather(w_value, "dp", axis=0, tiled=True),
            lax.all_gather(w_out, "dp", axis=0, tiled=True),
            lax.all_gather(w_up, "dp", axis=0, tiled=True),
            lax.all_gather(w_down, "dp", axis=0, tiled=True),
            lax.all_gather(b_query, "dp", axis=0, tiled=True),
            lax.all_gather(b_value, "dp", axis=0, tiled=True),
            lax.all_gather(b_out, "dp", axis=0, tiled=True),
            lax.all_gather(b_up, "dp", axis=0, tiled=True),
            lax.all_gather(b_down, "dp", axis=0, tiled=True),
            lax.all_gather(gain_attn, "dp", axis=0, tiled=True),
            lax.all_gather(shift_attn, "dp", axis=0, tiled=True),
            lax.all_gather(gain_ffn, "dp", axis=0, tiled=True),
            lax.all_gather(shift_ffn, "dp", axis=0, tiled=True),
        )
        result, stored = forward_pass(rows_in, gathered)
        outputs.append(result.astype(jnp.bfloat16))
        gathered = (
            lax.all_gather(w_query, "dp", axis=0, tiled=True),
            lax.all_gather(w_key, "dp", axis=0, tiled=True),
            lax.all_gather(w_value, "dp", axis=0, tiled=True),
            lax.all_gather(w_out, "dp", axis=0, tiled=True),
            lax.all_gather(w_up, "dp", axis=0, tiled=True),
            lax.all_gather(w_down, "dp", axis=0, tiled=True),
            lax.all_gather(b_query, "dp", axis=0, tiled=True),
            lax.all_gather(b_value, "dp", axis=0, tiled=True),
            lax.all_gather(b_out, "dp", axis=0, tiled=True),
            lax.all_gather(b_up, "dp", axis=0, tiled=True),
            lax.all_gather(b_down, "dp", axis=0, tiled=True),
            lax.all_gather(gain_attn, "dp", axis=0, tiled=True),
            lax.all_gather(shift_attn, "dp", axis=0, tiled=True),
            lax.all_gather(gain_ffn, "dp", axis=0, tiled=True),
            lax.all_gather(shift_ffn, "dp", axis=0, tiled=True),
        )
        gradients, grad_rows = backward_pass(rows_in, cot_rows, gathered, stored)
        input_grads.append(grad_rows.astype(jnp.bfloat16))
        if running is None:
            running = tuple(gradients)
        else:
            running = tuple(jax.tree.map(jnp.add, running, tuple(gradients)))
    running = (
        lax.psum_scatter(running[0], "dp", scatter_dimension=0, tiled=True),
        lax.psum_scatter(running[1], "dp", scatter_dimension=0, tiled=True),
        lax.psum_scatter(running[2], "dp", scatter_dimension=0, tiled=True),
        lax.psum_scatter(running[3], "dp", scatter_dimension=0, tiled=True),
        lax.psum_scatter(running[4], "dp", scatter_dimension=0, tiled=True),
        lax.psum_scatter(running[5], "dp", scatter_dimension=0, tiled=True),
        lax.psum_scatter(running[6], "dp", scatter_dimension=0, tiled=True),
        lax.psum_scatter(running[7], "dp", scatter_dimension=0, tiled=True),
        lax.psum_scatter(running[8], "dp", scatter_dimension=0, tiled=True),
        lax.psum_scatter(running[9], "dp", scatter_dimension=0, tiled=True),
        lax.psum_scatter(running[10], "dp", scatter_dimension=0, tiled=True),
        lax.psum_scatter(running[11], "dp", scatter_dimension=0, tiled=True),
        lax.psum_scatter(running[12], "dp", scatter_dimension=0, tiled=True),
        lax.psum_scatter(running[13], "dp", scatter_dimension=0, tiled=True),
        lax.psum_scatter(running[14], "dp", scatter_dimension=0, tiled=True),
    )
    return (jnp.concatenate(outputs, axis=0), jnp.concatenate(input_grads, axis=0)) + tuple(running)


def solution(mesh):
    placed = (
        P("dp", None),
        P("dp", None),
        P("dp", None),
        P("dp", None),
        P("dp", None),
        P("dp", None),
        P("dp", None),
        P("dp"),
        P("dp"),
        P("dp"),
        P("dp"),
        P("dp"),
        P("dp"),
        P("dp"),
        P("dp"),
        P("dp"),
        P("dp", None),
    )
    return jax.shard_map(
        local,
        mesh=mesh,
        in_specs=placed,
        out_specs=(
            P("dp", None),
            P("dp", None),
            P("dp", None),
            P("dp", None),
            P("dp", None),
            P("dp", None),
            P("dp", None),
            P("dp", None),
            P("dp"),
            P("dp"),
            P("dp"),
            P("dp"),
            P("dp"),
            P("dp"),
            P("dp"),
            P("dp"),
            P("dp"),
        ),
        check_vma=False,
    )
```

profile of v0, /device:TPU:0, one launch (start us, length us, event | category | flops | bytes accessed | tf_op | source)
XLA Modules:
  0.0 1424.2 jit_solution(1529392509229781152)
XLA Ops:
  17.9 42.3 %all-reduce.18 = (bf16[1024]{0:T(1024)(128)(2,1)S(1)}, bf16[1024]{0:T(1024)(128)(2,1)S(1)}, bf16[1024]{0:T(1024)(128)(2,1)S(1)}, bf16[1024]{0:T(1024)(128)(2,1)S...) all-reduce(bf16[1024]{0:T(1024)(128)(2,1)S(1)} %dynamic-update-slic, ...), channel_id=1, replica_groups=mesh['dp'=32] {'dp'}, use_global_device_ids=true, to_apply=%add | all-reduce | flops 8192 | bytes 32768
  62.1 40.3 %all-gather = bf16[32,1,128]{2,1,0:T(2,128)(2,1)S(1)} all-gather(bf16[1,1,128]{2,1,0:T(2,128)(2,1)} %bitcast.184), channel_id=1, replica_groups=mesh['dp'=32] {'dp'}, dimensions={0}, use_global_device_ids=true | all-gather | bytes 8448 | tf_op jit(solution)/shard_map/all_gather | solution.py:293
  111.8 16.7 %all-gather.8.cloned.1.call-done = bf16[1024,1024]{1,0:T(8,128)(2,1)} async-done(((bf16[32,1024]{1,0:T(8,128)(2,1)}), bf16[1024,1024]{1,0:T(8,128)(2,1)}) %all-gather.8.cloned.1.call-update) | async-done | bytes 2097168 | tf_op jit(solution)/shard_map/all_gather | solution.py:286
  136.8 49.8 %all-gather.12.cloned.1.call-done = bf16[1024,1024]{1,0:T(8,128)(2,1)} async-done(((bf16[32,1024]{1,0:T(8,128)(2,1)}), bf16[1024,1024]{1,0:T(8,128)(2,1)}) %all-gather.12.cloned.1.call-update) | async-done | bytes 2097168 | tf_op jit(solution)/shard_map/all_gather | solution.py:285
  225.1 19.4 %all-gather.14.cloned.1.call-done = bf16[1024,1024]{1,0:T(8,128)(2,1)} async-done(((bf16[32,1024]{1,0:T(8,128)(2,1)}), bf16[1024,1024]{1,0:T(8,128)(2,1)}) %all-gather.14.cloned.1.call-update) | async-done | bytes 2097168 | tf_op jit(solution)/shard_map/all_gather | solution.py:287
  276.3 47.3 %all-gather.16.cloned.1.call-done = bf16[1024,4096]{1,0:T(8,128)(2,1)} async-done(((bf16[32,4096]{1,0:T(8,128)(2,1)}), bf16[1024,4096]{1,0:T(8,128)(2,1)}) %all-gather.16.cloned.1.call-update) | async-done | bytes 8388624 | tf_op jit(solution)/shard_map/all_gather | solution.py:288
  334.3 49.1 %multiply_convert_fusion.1 = (bf16[512,4096]{1,0:T(8,128)(2,1)}, f32[512,4096]{1,0:T(8,128)}, bf16[512,4096]{1,0:T(8,128)(2,1)}, f32[512,4096]{1,0:T(8,128)}, f32[512,4096]{1,0:T(8,128)}) fusion(f32[4096]{0:T(1024)S(1)} %bitcast.181, f32[512,4096]{1,0:T(8,128)S(1)} %fusion.94, bf16[1024,4096]{1,0:T(8,128)(2,1)S(1)} %copy-done.82, ...), kind=kOutput, calls=%fused_computation.51 | convolution fusion | flops 4574412800 | bytes 52457472 | tf_op jit(solution)/shard_map/dot_general | solution.py:16
  383.3 19.1 %all-gather.18.cloned.1.call-done = bf16[4096,1024]{1,0:T(8,128)(2,1)} async-done(((bf16[128,1024]{1,0:T(8,128)(2,1)}), bf16[4096,1024]{1,0:T(8,128)(2,1)}) %all-gather.18.cloned.1.call-update) | async-done | bytes 8388624 | tf_op jit(solution)/shard_map/all_gather | solution.py:289
  424.4 17.2 %convert_reduce_fusion.1 = (f32[4096]{0:T(1024)}, bf16[512,4096]{1,0:T(8,128)(2,1)}) fusion(f32[512,4096]{1,0:T(8,128)} %get-tuple-element.118, bf16[4096,1024]{1,0:T(8,128)(2,1)} %all-gather.18.cloned.1.call-done, f32[512,1024]{1,0:T(8,128)S(1)} %get-tuple-element.125, f32[512,4096]{1,0:T(8,128)} %get-tuple-element.140, f32[4096]{0:T(1024)S(1)} %bitcast.182), kind=kOutput, calls=%fused_computation.31 | convolution fusion | flops 4331139072 | bytes 31490048 | tf_op jit(solution)/shard_map/td,fd->tf/dot_general | solution.py:161
  441.5 11.6 multiply_reduce_fusion.3
  453.1 15.6 %convert_reduce_fusion = (f32[4096]{0:T(1024)}, bf16[512,4096]{1,0:T(8,128)(2,1)}) fusion(f32[512,4096]{1,0:T(8,128)} %get-tuple-element.127, bf16[4096,1024]{1,0:T(8,128)(2,1)} %all-gather.18.cloned.1.call-done, f32[512,1024]{1,0:T(8,128)S(1)} %get-tuple-element.110, f32[512,4096]{1,0:T(8,128)} %copy-done.86, f32[4096]{0:T(1024)S(1)} %bitcast.183), kind=kOutput, calls=%fused_computation.30 | convolution fusion | flops 4331139072 | bytes 31490048 | tf_op jit(solution)/shard_map/td,fd->tf/dot_general | solution.py:161
  468.7 12.7 convert_reduce_fusion.7
  541.5 10.1 fusion
  551.6 10.8 fusion.17
  619.2 13.5 fusion.96
  632.7 11.8 convolution_add_fusion
  645.0 13.3 fusion.83
  658.4 11.7 convolution_add_fusion.1
  671.0 40.6 %all-reduce.17 = (f32[1024]{0:T(1024)S(1)}, f32[1024]{0:T(1024)S(1)}, f32[1024]{0:T(1024)S(1)}, f32[4096]{0:T(1024)S(1)}, f32[1024]{0:T(1024)S(1)}, /*index=5*/f...) all-reduce(f32[1024]{0:T(1024)S(1)} %add.321, ...), channel_id=8, replica_groups=mesh['dp'=32] {'dp'}, use_global_device_ids=true, to_apply=%region_30.0.clone | all-reduce | flops 12288 | bytes 98304
  730.1 39.2 %reduce-scatter.23.cloned.1.call-done = f32[32,1024]{1,0:T(8,128)} async-done(((f32[1024,1024]{1,0:T(8,128)}), f32[32,1024]{1,0:T(8,128)}) %reduce-scatter.23.cloned.1.call-update) | async-done | bytes 131088
  769.3 139.6 %reduce-scatter.19.cloned.1.call-done = f32[32,1024]{1,0:T(8,128)} async-done(((f32[1024,1024]{1,0:T(8,128)}), f32[32,1024]{1,0:T(8,128)}) %reduce-scatter.19.cloned.1.call-update) | async-done | bytes 131088
  908.9 139.4 %reduce-scatter.21.cloned.1.call-done = f32[32,1024]{1,0:T(8,128)} async-done(((f32[1024,1024]{1,0:T(8,128)}), f32[32,1024]{1,0:T(8,128)}) %reduce-scatter.21.cloned.1.call-update) | async-done | bytes 131088
  1048.3 181.5 %reduce-scatter.15.cloned.1.call-done = f32[32,4096]{1,0:T(8,128)} async-done(((f32[1024,4096]{1,0:T(8,128)}), f32[32,4096]{1,0:T(8,128)}) %reduce-scatter.15.cloned.1.call-update) | async-done | bytes 524304 | tf_op jit(solution)/shard_map/reduce_scatter | solution.py:330
  1229.9 187.4 %reduce-scatter.17.cloned.1.call-done = f32[128,1024]{1,0:T(8,128)} async-done(((f32[4096,1024]{1,0:T(8,128)}), f32[128,1024]{1,0:T(8,128)}) %reduce-scatter.17.cloned.1.call-update) | async-done | bytes 524304 | tf_op jit(solution)/shard_map/reduce_scatter | solution.py:331
  (338 shorter events, 268.8 us)
Async XLA Ops:
  7.2 95.3 %all-gather.10.cloned.1.call-start = ((), (), s32[]{:S(2)}) async-start(), calls=%async_computation.7 | async-start | bytes 2162688 | tf_op jit(solution)/shard_map/all_gather | solution.py:284
  7.9 120.5 %all-gather.8.cloned.1.call-start = ((), (), s32[]{:S(2)}) async-start(), calls=%async_computation.6 | async-start | bytes 2162688 | tf_op jit(solution)/shard_map/all_gather | solution.py:286
  8.7 177.9 %all-gather.12.cloned.1.call-start = ((), (), s32[]{:S(2)}) async-start(), calls=%async_computation.8 | async-start | bytes 2162688 | tf_op jit(solution)/shard_map/all_gather | solution.py:285
  9.4 235.1 %all-gather.14.cloned.1.call-start = ((), (), s32[]{:S(2)}) async-start(), calls=%async_computation.9 | async-start | bytes 2162688 | tf_op jit(solution)/shard_map/all_gather | solution.py:287
  10.0 313.6 %all-gather.16.cloned.1.call-start = ((), (), s32[]{:S(2)}) async-start(), calls=%async_computation.10 | async-start | bytes 8650752 | tf_op jit(solution)/shard_map/all_gather | solution.py:288
  10.6 391.9 %all-gather.18.cloned.1.call-start = ((), (), s32[]{:S(2)}) async-start(), calls=%async_computation.11 | async-start | bytes 8650752 | tf_op jit(solution)/shard_map/all_gather | solution.py:289
  11.1 718.9 %reduce-scatter.13.cloned.1.call-start = ((), (), s32[]{:S(2)}) async-start(), calls=%async_computation.12 | async-start | bytes 4325376 | tf_op jit(solution)/shard_map/reduce_scatter | solution.py:329
  60.2 352.6 %copy-start.63 = (f32[1024]{0:T(1024)}, f32[1024]{0:T(1024)S(1)}, u32[]{:S(2)}) copy-start(f32[1024]{0:T(1024)S(1)} %convert_element_type.321) | copy-start | bytes 12292
  191.9 57.7 %copy-start.7 = (bf16[512,1024]{0,1:T(8,128)(2,1)}, bf16[512,1024]{0,1:T(8,128)(2,1)S(1)}, u32[]{:S(2)}) copy-start(bf16[512,1024]{0,1:T(8,128)(2,1)S(1)} %copy.90) | copy-start | bytes 3145732
  216.0 28.5 %copy-start.12 = (bf16[1024,1024]{1,0:T(8,128)(2,1)S(1)}, bf16[1024,1024]{1,0:T(8,128)(2,1)}, u32[]{:S(2)}) copy-start(bf16[1024,1024]{1,0:T(8,128)(2,1)} %param.17) | copy-start | bytes 6291460
  276.0 206.8 %copy-start.2 = (f32[512,1024]{1,0:T(8,128)}, f32[512,1024]{1,0:T(8,128)S(1)}, u32[]{:S(2)}) copy-start(f32[512,1024]{1,0:T(8,128)S(1)} %get-tuple-element.139) | copy-start | bytes 6291460
  334.3 68.2 %copy-start.81 = (f32[1024]{0:T(1024)S(1)}, f32[1024]{0:T(1024)}, u32[]{:S(2)}) copy-start(f32[1024]{0:T(1024)} %convert_element_type.325) | copy-start | bytes 12292
  424.4 44.4 %copy-start.32 = (f32[512,1024]{1,0:T(8,128)}, f32[512,1024]{1,0:T(8,128)S(1)}, u32[]{:S(2)}) copy-start(f32[512,1024]{1,0:T(8,128)S(1)} %get-tuple-element.110) | copy-start | bytes 6291460
  489.7 279.5 %reduce-scatter.23.cloned.1.call-start = ((), (), s32[]{:S(2)}) async-start(), calls=%async_computation.17 | async-start | bytes 4325376
  541.4 367.5 %reduce-scatter.19.cloned.1.call-start = ((), (), s32[]{:S(2)}) async-start(), calls=%async_computation.15 | async-start | bytes 4325376
  541.5 30.1 %slice-start.4 = ((s8[8388608]{0:T(1024)(128)(4,1)}), s8[4194304]{0:T(1024)(128)(4,1)S(1)}, s32[]{:S(2)}) async-start(s8[8388608]{0:T(1024)(128)(4,1)} %bitcast.147), calls=%async_computation.22 | async-start | bytes 8388608
  551.6 20.0 %slice-start = ((s8[16777216]{0:T(1024)(128)(4,1)}), s8[4194304]{0:T(1024)(128)(4,1)S(1)}, s32[]{:S(2)}) async-start(s8[16777216]{0:T(1024)(128)(4,1)} %bitcast.145), calls=%async_computation.18 | async-start | bytes 8388608
  551.6 20.0 %slice-start.1 = ((s8[16777216]{0:T(1024)(128)(4,1)}), s8[4194304]{0:T(1024)(128)(4,1)S(1)}, s32[]{:S(2)}) async-start(s8[16777216]{0:T(1024)(128)(4,1)} %bitcast.145), calls=%async_computation.19 | async-start | bytes 8388608
  551.6 20.0 %slice-start.2 = ((s8[16777216]{0:T(1024)(128)(4,1)}), s8[4194304]{0:T(1024)(128)(4,1)S(1)}, s32[]{:S(2)}) async-start(s8[16777216]{0:T(1024)(128)(4,1)} %bitcast.145), calls=%async_computation.20 | async-start | bytes 8388608
  595.0 453.3 %reduce-scatter.21.cloned.1.call-start = ((), (), s32[]{:S(2)}) async-start(), calls=%async_computation.16 | async-start | bytes 4325376
  618.6 611.3 %reduce-scatter.15.cloned.1.call-start = ((), (), s32[]{:S(2)}) async-start(), calls=%async_computation.13 | async-start | bytes 17301504 | tf_op jit(solution)/shard_map/reduce_scatter | solution.py:330
  644.6 772.6 %reduce-scatter.17.cloned.1.call-start = ((), (), s32[]{:S(2)}) async-start(), calls=%async_computation.14 | async-start | bytes 17301504 | tf_op jit(solution)/shard_map/reduce_scatter | solution.py:331
  670.2 46.6 %copy-start.45 = (bf16[512,1024]{1,0:T(8,128)(2,1)S(1)}, bf16[512,1024]{1,0:T(8,128)(2,1)}, u32[]{:S(2)}) copy-start(bf16[512,1024]{1,0:T(8,128)(2,1)} %get-tuple-element.122) | copy-start | bytes 3145732
  670.2 46.6 %copy-start.46 = (bf16[512,1024]{1,0:T(8,128)(2,1)S(1)}, bf16[512,1024]{1,0:T(8,128)(2,1)}, u32[]{:S(2)}) copy-start(bf16[512,1024]{1,0:T(8,128)(2,1)} %get-tuple-element.123) | copy-start | bytes 3145732
  (81 other events, 413.3 us)
Sparse Core Ops, SparseCore 0:
  10.9 59.4 all-gather.9
  73.2 55.2 all-gather.7
  131.3 55.2 all-gather.11
  189.3 55.2 all-gather.13
  247.3 76.2 all-gather.15
  326.3 76.0 all-gather.17
  489.9 139.4 reduce-scatter.12
  632.2 137.0 reduce-scatter.22
  772.2 136.7 reduce-scatter.18
  911.6 136.6 reduce-scatter.20
  1051.2 178.5 reduce-scatter.14
  1232.6 184.5 reduce-scatter.16
where the time goes:
time: 1430 us; the launch traced here: 1420 us
  waiting for transfers between devices  843 us (59%)
  matrix products  318 us (22%)
  blocking collectives  123 us (9%)
  local copies, waits for them, and re-layouts  63 us (4%)
  other arithmetic  60.7 us (4%)
  between operations  15.6 us (1%)
    unnamed x15, waiting for transfers between devices  322 us
    reduce_scatter x1, waiting for transfers between devices, local(): lax.psum_scatter(running[5], 'dp', scatter_dimension=0, tiled=True)  187 us
    reduce_scatter x1, waiting for transfers between devices, local(): lax.psum_scatter(running[4], 'dp', scatter_dimension=0, tiled=True)  182 us
    dot_general x12, matrix products, matmul(): return jnp.dot(left_side, right_side, preferred_element_type=jnp.float32)  95.9 us
    unnamed x2, blocking collectives  82.9 us
    unnamed x214, local copies, waits for them, and re-layouts  50.7 us
    all_gather x1, waiting for transfers between devices, local(): lax.all_gather(w_key, 'dp', axis=0, tiled=True)  49.8 us
    all_gather x1, waiting for transfers between devices, local(): lax.all_gather(w_up, 'dp', axis=0, tiled=True)  47.3 us
  transfers between devices with their start and end apart: 12, of which 10 were waited for; matrix products, arithmetic and copies ran while one was open for 23% of the time, Pallas kernels for 0%

commit v1 on v0

--- a/solution.py
+++ b/solution.py
@@ -6,7 +6,7 @@
 D = 1024
 HEADS = 16
 LEN = 512
-MICRO = 2
+SPLIT = 640
 
 
 EPS = 1e-12
@@ -250,6 +250,100 @@
     return (gradients, grad_rows)
 
 
+def ring_pairs(count):
+    return [(place, (place + 8) % count) for place in range(count)]
+
+
+def flip_pairs(count, bit):
+    return [(place, place ^ bit) for place in range(count)]
+
+
+FLIPS = {"c": 1, "x": 2, "y": 4}
+
+
+def gather_part(shard, order, count):
+    stack = shard[None]
+    for dim in order + "c":
+        if dim == "z":
+            pieces = [stack]
+            for _ in range(count // 8 - 1):
+                pieces.append(lax.ppermute(pieces[-1], "dp", ring_pairs(count)))
+        else:
+            pieces = [stack, lax.ppermute(stack, "dp", flip_pairs(count, FLIPS[dim]))]
+        stack = jnp.concatenate(pieces, axis=0)
+    return stack
+
+
+def add_low(left_side, right_side):
+    return (left_side.astype(jnp.float32) + right_side.astype(jnp.float32)).astype(jnp.bfloat16)
+
+
+def scatter_part(stack, order, count):
+    for dim in "c" + order[::-1]:
+        last = dim == order[0]
+        if dim == "z":
+            ring = count // 8
+            blocks = stack.reshape((ring, stack.shape[0] // ring) + stack.shape[1:])
+            moving = blocks[1]
+            for step in range(2, ring):
+                moving = add_low(lax.ppermute(moving, "dp", ring_pairs(count)), blocks[step])
+            moving = lax.ppermute(moving, "dp", ring_pairs(count))
+            kept = blocks[0]
+        else:
+            half = stack.shape[0] // 2
+            moving = lax.ppermute(stack[half:], "dp", flip_pairs(count, FLIPS[dim]))
+            kept = stack[:half]
+        if last:
+            return (kept.astype(jnp.float32) + moving.astype(jnp.float32))[0]
+        stack = add_low(kept, moving)
+
+
+def places(order, count):
+    me = lax.axis_index("dp")
+    other = jnp.arange(count, dtype=jnp.int32)
+    digits = {
+        "z": lax.rem(me // 8 - other // 8 + count // 8, count // 8),
+        "y": (me // 4 % 2) ^ (other // 4 % 2),
+        "x": (me // 2 % 2) ^ (other // 2 % 2),
+        "c": (me % 2) ^ (other % 2),
+    }
+    weight, position = 1, jnp.zeros_like(other)
+    for dim in order + "c":
+        position = position + weight * digits[dim]
+        weight = weight * (count // 8 if dim == "z" else 2)
+    return position
+
+
+ORDERS = ("zyx", "xzy")
+
+
+def gather_rows(shard, count):
+    sides = (shard[:, :SPLIT], shard[:, SPLIT:])
+    stacks = [gather_part(side, order, count) for side, order in zip(sides, ORDERS)]
+    ordered = [
+        jnp.take(stack, places(order, count), axis=0) for stack, order in zip(stacks, ORDERS)
+    ]
+    return jnp.concatenate(ordered, axis=-1)
+
+
+def scatter_rows(blocks, count):
+    me_sides = (blocks[..., :SPLIT], blocks[..., SPLIT:])
+    sums = []
+    for side, order in zip(me_sides, ORDERS):
+        position = places(order, count)
+        relative = jnp.take(side, jnp.argsort(position), axis=0)
+        sums.append(scatter_part(relative, order, count))
+    return jnp.concatenate(sums, axis=-1)
+
+
+def vector_rows(vectors, rows):
+    flat = jnp.concatenate(vectors, axis=-1)
+    width = flat.shape[-1]
+    lead = flat.shape[:-1]
+    flat = jnp.pad(flat, [(0, 0)] * len(lead) + [(0, rows * D - width)])
+    return flat.reshape(lead + (rows, D))
+
+
 def local(
     tokens,
     w_query,
@@ -269,77 +363,62 @@
     shift_ffn,
     cotangent,
 ):
-    micro_rows = tokens.shape[0] // MICRO
-    outputs = []
-    input_grads = []
-    running = None
-    for micro_step in range(MICRO):
-        rows_in = lax.slice_in_dim(
-            tokens, micro_step * micro_rows, (micro_step + 1) * micro_rows, axis=0
-        )
-        cot_rows = lax.slice_in_dim(
-            cotangent, micro_step * micro_rows, (micro_step + 1) * micro_rows, axis=0
-        )
-        gathered = (
-            lax.all_gather(w_query, "dp", axis=0, tiled=True),
-            lax.all_gather(w_key, "dp", axis=0, tiled=True),
-            lax.all_gather(w_value, "dp", axis=0, tiled=True),
-            lax.all_gather(w_out, "dp", axis=0, tiled=True),
-            lax.all_gather(w_up, "dp", axis=0, tiled=True),
-            lax.all_gather(w_down, "dp", axis=0, tiled=True),
-            lax.all_gather(b_query, "dp", axis=0, tiled=True),
-            lax.all_gather(b_value, "dp", axis=0, tiled=True),
-            lax.all_gather(b_out, "dp", axis=0, tiled=True),
-            lax.all_gather(b_up, "dp", axis=0, tiled=True),
-            lax.all_gather(b_down, "dp", axis=0, tiled=True),
-            lax.all_gather(gain_attn, "dp", axis=0, tiled=True),
-            lax.all_gather(shift_attn, "dp", axis=0, tiled=True),
-            lax.all_gather(gain_ffn, "dp", axis=0, tiled=True),
-            lax.all_gather(shift_ffn, "dp", axis=0, tiled=True),
-        )
-        result, stored = forward_pass(rows_in, gathered)
-        outputs.append(result.astype(jnp.bfloat16))
-        gathered = (
-            lax.all_gather(w_query, "dp", axis=0, tiled=True),
-            lax.all_gather(w_key, "dp", axis=0, tiled=True),
-            lax.all_gather(w_value, "dp", axis=0, tiled=True),
-            lax.all_gather(w_out, "dp", axis=0, tiled=True),
-            lax.all_gather(w_up, "dp", axis=0, tiled=True),
-            lax.all_gather(w_down, "dp", axis=0, tiled=True),
-            lax.all_gather(b_query, "dp", axis=0, tiled=True),
-            lax.all_gather(b_value, "dp", axis=0, tiled=True),
-            lax.all_gather(b_out, "dp", axis=0, tiled=True),
-            lax.all_gather(b_up, "dp", axis=0, tiled=True),
-            lax.all_gather(b_down, "dp", axis=0, tiled=True),
-            lax.all_gather(gain_attn, "dp", axis=0, tiled=True),
-            lax.all_gather(shift_attn, "dp", axis=0, tiled=True),
-            lax.all_gather(gain_ffn, "dp", axis=0, tiled=True),
-            lax.all_gather(shift_ffn, "dp", axis=0, tiled=True),
-        )
-        gradients, grad_rows = backward_pass(rows_in, cot_rows, gathered, stored)
-        input_grads.append(grad_rows.astype(jnp.bfloat16))
-        if running is None:
-            running = tuple(gradients)
-        else:
-            running = tuple(jax.tree.map(jnp.add, running, tuple(gradients)))
-    running = (
-        lax.psum_scatter(running[0], "dp", scatter_dimension=0, tiled=True),
-        lax.psum_scatter(running[1], "dp", scatter_dimension=0, tiled=True),
-        lax.psum_scatter(running[2], "dp", scatter_dimension=0, tiled=True),
-        lax.psum_scatter(running[3], "dp", scatter_dimension=0, tiled=True),
-        lax.psum_scatter(running[4], "dp", scatter_dimension=0, tiled=True),
-        lax.psum_scatter(running[5], "dp", scatter_dimension=0, tiled=True),
-        lax.psum_scatter(running[6], "dp", scatter_dimension=0, tiled=True),
-        lax.psum_scatter(running[7], "dp", scatter_dimension=0, tiled=True),
-        lax.psum_scatter(running[8], "dp", scatter_dimension=0, tiled=True),
-        lax.psum_scatter(running[9], "dp", scatter_dimension=0, tiled=True),
-        lax.psum_scatter(running[10], "dp", scatter_dimension=0, tiled=True),
-        lax.psum_scatter(running[11], "dp", scatter_dimension=0, tiled=True),
-        lax.psum_scatter(running[12], "dp", scatter_dimension=0, tiled=True),
-        lax.psum_scatter(running[13], "dp", scatter_dimension=0, tiled=True),
-        lax.psum_scatter(running[14], "dp", scatter_dimension=0, tiled=True),
-    )
-    return (jnp.concatenate(outputs, axis=0), jnp.concatenate(input_grads, axis=0)) + tuple(running)
+    count = D // w_query.shape[0]
+    part = D // count
+    vectors = (
+        b_query, b_value, b_out, b_down, gain_attn, shift_attn, gain_ffn, shift_ffn, b_up,
+    )
+    up_cols = w_up.shape[1] // D
+    first = jnp.concatenate([w_query, w_key, w_value, vector_rows(vectors, 16)], axis=0)
+    second = jnp.concatenate([w_out] + [w_up[:, D * col : D * col + D] for col in range(up_cols)], axis=0)
+    first = gather_rows(first, count)
+    second = gather_rows(second, count)
+    third = gather_rows(w_down, count)
+    weight = lambda col: first[:, part * col : part * col + part].reshape(D, D)
+    flat = first[:, 3 * part :].reshape(count, -1)
+    vec = lambda col: flat[:, part * col : part * col + part].reshape(D)
+    ff_part = b_up.shape[0]
+    full = (
+        weight(0), weight(1), weight(2),
+        second[:, :part].reshape(D, D),
+        second[:, part:].reshape(count, up_cols, part, D).transpose(0, 2, 1, 3).reshape(D, up_cols * D),
+        third.reshape(-1, D),
+        vec(0), vec(1), vec(2),
+        flat[:, 8 * part : 8 * part + ff_part].reshape(-1),
+        vec(3), vec(4), vec(5), vec(6), vec(7),
+    )
+    result, stored = forward_pass(tokens, full)
+    gradients, grad_rows = backward_pass(tokens, cotangent, full, stored)
+    (
+        d_w_query, d_w_key, d_w_value, d_w_out, d_w_up, d_w_down,
+        d_b_query, d_b_value, d_b_out, d_b_up, d_b_down,
+        d_gain_attn, d_shift_attn, d_gain_ffn, d_shift_ffn,
+    ) = gradients
+    low = lambda grad: grad.astype(jnp.bfloat16)
+    blocks = lambda grad: low(grad).reshape(count, -1, D)
+    third = scatter_rows(blocks(d_w_down), count)
+    up_blocks = low(d_w_up).reshape(count, part, up_cols, D).transpose(0, 2, 1, 3).reshape(count, -1, D)
+    second = scatter_rows(jnp.concatenate([blocks(d_w_out), up_blocks], axis=1), count)
+    vectors = (
+        d_b_query, d_b_value, d_b_out, d_b_down, d_gain_attn, d_shift_attn, d_gain_ffn, d_shift_ffn, d_b_up,
+    )
+    packed = vector_rows([low(vector).reshape(count, -1) for vector in vectors], 16)
+    first = scatter_rows(
+        jnp.concatenate([blocks(d_w_query), blocks(d_w_key), blocks(d_w_value), packed], axis=1), count
+    )
+    flat = first[3 * part :].reshape(-1)
+    vec = lambda col: flat[part * col : part * col + part]
+    return (
+        result.astype(jnp.bfloat16),
+        grad_rows.astype(jnp.bfloat16),
+        first[:part], first[part : 2 * part], first[2 * part : 3 * part],
+        second[:part],
+        second[part:].reshape(up_cols, part, D).transpose(1, 0, 2).reshape(part, up_cols * D),
+        third,
+        vec(0), vec(1), vec(2),
+        flat[8 * part : 8 * part + ff_part],
+        vec(3), vec(4), vec(5), vec(6), vec(7),
+    )
 
 
 def solution(mesh):

time: 1430 us -> 1010 us (0.71)
  waiting for transfers between devices: 843 us -> 241 us
  local copies, waits for them, and re-layouts: 63 us -> 290 us
  blocking collectives: 123 us -> 0 us
  other arithmetic: 60.7 us -> 162 us
  matrix products: 318 us -> 253 us
  starting transfers between devices: 1.09 us -> 55.9 us
    reduce_scatter x3 -> x0, waiting for transfers between devices: 369 us -> none  [the longest x1 187 us: local(): lax.psum_scatter(running[5], 'dp', scatter_dimension=0, tiled=True)]
    unnamed x15 -> x0, waiting for transfers between devices: 322 us -> none
    ppermute x0 -> x72, waiting for transfers between devices: none -> 241 us  [the longest x18 74.1 us: scatter_part(): moving = lax.ppermute(stack[half:], 'dp', flip_pairs(count, FLIPS[dim]))]
    all_gather x6 -> x0, waiting for transfers between devices: 152 us -> none  [the longest x1 49.8 us: local(): lax.all_gather(w_key, 'dp', axis=0, tiled=True)]
    unnamed x2 -> x0, blocking collectives: 82.9 us -> none
    gather x0 -> x12, local copies, waits for them, and re-layouts: none -> 62 us  [the longest x6 31.5 us: scatter_rows(): relative = jnp.take(side, jnp.argsort(position), axis=0)]
    ppermute x0 -> x72, starting transfers between devices: none -> 55.9 us  [the longest x18 16.3 us: gather_part(): pieces = [stack, lax.ppermute(stack, 'dp', flip_pairs(count, FLIPS[dim]))]]
    reshape x0 -> x15, local copies, waits for them, and re-layouts: none -> 55.7 us  [the longest x2 24.9 us: local(): low(d_w_up).reshape(count, part, up_cols, D).transpose(0, 2, 1, 3)]
  transfers between devices with their start and end apart: 12 -> 72, of which waited for: 10 -> 32; matrix products, arithmetic and copies ran while one was open for 23% -> 30% of each run, Pallas kernels for 0% -> 0%
where the time goes in v1:
time: 1010 us; the launch traced here: 1000 us
  local copies, waits for them, and re-layouts  290 us (29%)
  matrix products  253 us (25%)
  waiting for transfers between devices  241 us (24%)
  other arithmetic  162 us (16%)
  starting transfers between devices  55.9 us (6%)
    unnamed x199, local copies, waits for them, and re-layouts  99.3 us
    dot_general x6, matrix products, matmul(): return jnp.dot(left_side, right_side, preferred_element_type=jnp.float32)  87.9 us
    ppermute x18, waiting for transfers between devices, scatter_part(): moving = lax.ppermute(stack[half:], 'dp', flip_pairs(count, FLIPS[dim]))  74.1 us
    ppermute x18, waiting for transfers between devices, gather_part(): pieces = [stack, lax.ppermute(stack, 'dp', flip_pairs(count, FLIPS[dim]))]  68.7 us
    ppermute x12, waiting for transfers between devices, scatter_part(): lax.ppermute(moving, 'dp', ring_pairs(count))  42.4 us
    ppermute x18, waiting for transfers between devices, gather_part(): pieces.append(lax.ppermute(pieces[-1], 'dp', ring_pairs(count)))  35 us
    gather x6, local copies, waits for them, and re-layouts, scatter_rows(): relative = jnp.take(side, jnp.argsort(position), axis=0)  31.5 us
    gather x6, local copies, waits for them, and re-layouts, gather_rows(): jnp.take(stack, places(order, count), axis=0)  30.5 us
  transfers between devices with their start and end apart: 72, of which 32 were waited for; matrix products, arithmetic and copies ran while one was open for 30% of the time, Pallas kernels for 0%

profile of v1, /device:TPU:0, one launch (start us, length us, event | category | flops | bytes accessed | tf_op | source)
XLA Modules:
  0.0 1003.9 jit_solution(14441643662280347204)
XLA Ops:
  134.7 14.2 %collective-permute-done.34 = bf16[8,128,384]{2,1,0:T(8,128)(2,1)S(1)} collective-permute-done((bf16[8,128,384]{2,1,0:T(8,128)(2,1)S(1)}, bf16[8,128,384]{2,1,0:T(8,128)(2,1)S(1)}, u32[]{:S(2)}, u32[]{:S(2)}) %collective-permute-start.34) | collective-permute-done | bytes 786464 | tf_op jit(solution)/shard_map/ppermute | solution.py:272
  151.2 18.8 %collective-permute-done.22 = bf16[8,160,384]{2,1,0:T(8,128)(2,1)S(1)} collective-permute-done((bf16[8,160,384]{2,1,0:T(8,128)(2,1)S(1)}, bf16[8,160,384]{2,1,0:T(8,128)(2,1)S(1)}, u32[]{:S(2)}, u32[]{:S(2)}) %collective-permute-start.22) | collective-permute-done | bytes 983072 | tf_op jit(solution)/shard_map/ppermute | solution.py:272
  172.5 10.0 collective-permute-done.15
  205.1 17.5 %collective-permute-done.16 = bf16[8,160,640]{2,1,0:T(8,128)(2,1)} collective-permute-done((bf16[8,160,640]{2,1,0:T(8,128)(2,1)}, bf16[8,160,640]{2,1,0:T(8,128)(2,1)}, u32[]{:S(2)}, u32[]{:S(2)}) %collective-permute-start.16) | collective-permute-done | bytes 1638432 | tf_op jit(solution)/shard_map/ppermute | solution.py:272
  285.3 15.2 %multiply_reduce_fusion = (f32[2,16,512]{2,1,0:T(8,128)S(1)}, f32[2,16,512,512]{2,3,1,0:T(8,128)}) fusion(bf16[2,512,16,64]{1,0,3,2:T(2,128)(2,1)S(1)} %reshape.384, bf16[2,512,16,64]{1,0,3,2:T(2,128)(2,1)} %reshape.382), kind=kOutput, calls=%fused_computation.21 | convolution fusion | flops 1090502656 | bytes 37814272 | tf_op jit(solution)/shard_map/sqhe,skhe->shqk/dot_general | solution.py:69
  300.4 13.8 %fusion.3 = f32[2,16,512]{2,1,0:T(8,128)S(1)} fusion(f32[2,16,512,512]{2,3,1,0:T(8,128)} %get-tuple-element.206, f32[2,16,512]{2,1,0:T(8,128)S(1)} %get-tuple-element.205), kind=kLoop, calls=%fused_computation.20 | loop fusion | flops 25149440 | bytes 33685504 | tf_op jit(solution)/shard_map/reduce_sum | solution.py:77
  314.2 15.8 %convert_bitcast_fusion.1 = bf16[2,512,16,64]{1,3,2,0:T(8,128)(2,1)} fusion(f32[2,16,512,512]{2,3,1,0:T(8,128)} %get-tuple-element.206, f32[2,16,512]{2,1,0:T(8,128)S(1)} %fusion.3, f32[2,16,512]{2,1,0:T(8,128)S(1)} %get-tuple-element.205, bf16[2,512,16,64]{1,0,3,2:T(2,128)(2,1)S(1)} %copy-done.13), kind=kOutput, calls=%fused_computation.116 | convolution fusion | flops 1108344832 | bytes 37879808 | tf_op jit(solution)/shard_map/shqk,skhe->sqhe/dot_general | solution.py:80
  402.0 12.2 %copy.102 = bf16[128,8,4,1024]{3,1,2,0:T(8,128)(2,1)} copy(bf16[128,8,4,1024]{3,2,1,0:T(4,128)(2,1)} %bitcast.185) | data formatting | bytes 16777216
  414.9 48.2 %multiply_convert_fusion = (bf16[1024,4096]{1,0:T(8,128)(2,1)}, f32[1024,4096]{1,0:T(8,128)}, f32[1024,4096]{1,0:T(8,128)}) fusion(f32[4096]{0:T(1024)S(1)} %fusion.50, bf16[1024,4096]{1,0:T(8,128)(2,1)} %bitcast.206, bf16[1024,1024]{0,1:T(8,128)(2,1)S(1)} %fusion.67.clone.4), kind=kOutput, calls=%fused_computation.28 | convolution fusion | flops 8866758656 | bytes 52445184 | tf_op jit(solution)/shard_map/dot_general | solution.py:16
  463.0 15.7 %fusion.74 = (f32[1024]{0:T(1024)S(1)}, f32[1024,1024]{0,1:T(8,128)}) fusion(f32[1024]{0:T(1024)S(1)} %copy-done.59, bf16[1024,4096]{1,0:T(8,128)(2,1)} %get-tuple-element.74, bf16[4096,1024]{1,0:T(8,128)(2,1)} %bitcast.204, f32[1024]{0:T(1024)S(1)} %reshape.411, f32[1024]{0:T(1024)S(1)} %reshape.410, f32[1024]{0:T(1024)S(1)} %add_rsqrt_fusion.1, ...), kind=kOutput, calls=%fused_computation.377 | convolution fusion | flops 8597273600 | bytes 25190400 | tf_op jit(solution)/shard_map/dot_general | solution.py:16
  489.9 23.6 %fusion.68 = (bf16[4096]{0:T(1024)(128)(2,1)S(1)}, bf16[1024,4096]{1,0:T(8,128)(2,1)}) fusion(f32[1024,4096]{1,0:T(8,128)} %get-tuple-element.75, f32[1024,4096]{1,0:T(8,128)} %get-tuple-element.209, f32[4096]{0:T(1024)S(1)} %fusion.50, bf16[1024,1024]{0,1:T(8,128)(2,1)} %get-tuple-element.71, bf16[4096,1024]{1,0:T(8,128)(2,1)} %bitcast.205), kind=kOutput, calls=%fused_computation.373 | convolution fusion | flops 8657039360 | bytes 52453376 | tf_op jit(solution)/shard_map/td,fd->tf/dot_general | solution.py:161
  513.5 16.9 %multiply_reduce_fusion.1 = (bf16[1024]{0:T(1024)(128)(2,1)S(1)}, f32[1024]{0:T(1024)S(1)}, f32[1024]{0:T(1024)S(1)}, bf16[1024]{0:T(1024)(128)(2,1)S(1)}, f32[1024,1024]{0,1:T(8,128)S(1)}) fusion(f32[1024,1024]{0,1:T(8,128)S(1)} %get-tuple-element.208, f32[1024]{0:T(1024)S(1)} %add_rsqrt_fusion.1, f32[1024]{0:T(1024)S(1)} %broadcast_multiply_fusion.5, ...), kind=kOutput, calls=%fused_computation.77 | convolution fusion | flops 8608804864 | bytes 31502336 | tf_op jit(solution)/shard_map/tf,df->td/dot_general | solution.py:166
  544.8 10.4 %convolution_convert_fusion = bf16[2,16,512,512]{2,3,1,0:T(8,128)(2,1)} fusion(bf16[2,512,16,64]{1,3,2,0:T(8,128)(2,1)S(1)} %copy.68, bf16[2,512,16,64]{1,0,3,2:T(2,128)(2,1)} %reshape.380), kind=kOutput, calls=%fused_computation.44 | convolution fusion | flops 1082130432 | bytes 20971520 | tf_op jit(solution)/shard_map/sqhe,skhe->shqk/dot_general | solution.py:184
  555.2 15.3 %fusion.76 = (bf16[16,64]{1,0:T(8,128)(2,1)S(1)}, bf16[2,512,16,64]{1,3,2,0:T(8,128)(2,1)}) fusion(bf16[2,512,16,64]{1,3,2,0:T(8,128)(2,1)S(1)} %copy.68, f32[2,16,512,512]{2,3,1,0:T(8,128)} %get-tuple-element.206, f32[2,16,512]{2,1,0:T(8,128)S(1)} %copy-done.45), kind=kOutput, calls=%fused_computation.379 | convolution fusion | flops 1101003776 | bytes 37816320 | tf_op jit(solution)/shard_map/shqk,sqhe->skhe/dot_general | solution.py:189
  570.5 17.9 %fusion = f32[2,16,512]{2,1,0:T(8,128)S(1)} fusion(bf16[2,16,512,512]{2,3,1,0:T(8,128)(2,1)} %convolution_convert_fusion, f32[2,16,512,512]{2,3,1,0:T(8,128)} %get-tuple-element.206, f32[2,16,512]{2,1,0:T(8,128)S(1)} %copy-done.45), kind=kLoop, calls=%fused_computation.14 | loop fusion | flops 41926656 | bytes 50462720 | tf_op jit(solution)/shard_map/reduce_sum | solution.py:199
  590.7 15.1 %fusion.2 = bf16[2,16,512,512]{2,3,1,0:T(8,128)(2,1)S(1)} fusion(bf16[2,16,512,512]{2,3,1,0:T(8,128)(2,1)S(1)} %copy-done, f32[2,16,512,512]{2,3,1,0:T(8,128)} %get-tuple-element.206, f32[2,16,512]{2,1,0:T(8,128)S(1)} %fusion, f32[2,16,512]{2,1,0:T(8,128)S(1)} %copy-done.45), kind=kLoop, calls=%fused_computation.16 | loop fusion | flops 50331648 | bytes 67239936 | tf_op jit(solution)/shard_map/convert_element_type | solution.py:200
  617.5 12.9 %fusion.41 = bf16[2,512,16,64]{1,3,2,0:T(8,128)(2,1)} fusion(bf16[2,16,512,512]{2,3,1,0:T(8,128)(2,1)} %copy-done.1, bf16[2,512,16,64]{1,0,3,2:T(2,128)(2,1)} %reshape.382), kind=kOutput, calls=%fused_computation.134 | convolution fusion | flops 1075838976 | bytes 20971520 | tf_op jit(solution)/shard_map/shqk,sqhe->skhe/dot_general | solution.py:212
  657.0 10.4 %convolution_convert_fusion.1 = bf16[4096,1024]{1,0:T(8,128)(2,1)S(1)} fusion(bf16[1024,4096]{1,0:T(8,128)(2,1)S(1)} %bitcast.240, bf16[1024,1024]{0,1:T(8,128)(2,1)S(1)} %copy-done.43), kind=kOutput, calls=%fused_computation.55 | convolution fusion | flops 8594128896 | bytes 18874368 | tf_op jit(solution)/shard_map/tf,td->fd/dot_general | solution.py:160
  678.4 11.7 %convolution_convert_fusion.2 = bf16[1024,4096]{1,0:T(8,128)(2,1)} fusion(bf16[1024,4096]{1,0:T(8,128)(2,1)S(1)} %bitcast.242, f32[1024,1024]{0,1:T(8,128)S(1)} %copy-done.6, f32[1024]{0:T(1024)S(1)} %copy-done.51, f32[1024]{0:T(1024)S(1)} %reshape.410, f32[1024]{0:T(1024)S(1)} %add_rsqrt_fusion.1, f32[1024]{0:T(1024)S(1)} %broadcast_multiply_fusion.5), kind=kOutput, calls=%fused_computation.56 | convolution fusion | flops 8599371776 | bytes 20987904 | tf_op jit(solution)/shard_map/td,tf->df/dot_general | solution.py:165
  690.1 14.5 %reshape.401 = bf16[32,32,4,1024]{3,2,1,0:T(4,128)(2,1)} reshape(bf16[1024,4096]{1,0:T(8,128)(2,1)} %convolution_convert_fusion.2) | data formatting | bytes 16777216 | tf_op jit(solution)/shard_map/reshape | solution.py:400
  704.6 10.4 %copy.83 = bf16[32,32,4,1024]{3,1,2,0:T(8,128)(2,1)} copy(bf16[32,32,4,1024]{3,2,1,0:T(4,128)(2,1)} %reshape.401) | data formatting | bytes 16777216 | tf_op jit(solution)/shard_map/reshape | solution.py:400
  895.6 12.2 %collective-permute-done.71 = bf16[1,128,384]{2,1,0:T(8,128)(2,1)S(1)} collective-permute-done((bf16[1,128,384]{2,1,0:T(8,128)(2,1)S(1)}, bf16[1,128,384]{2,1,0:T(8,128)(2,1)S(1)}, u32[]{:S(2)}, u32[]{:S(2)}) %collective-permute-start.71) | collective-permute-done | bytes 98336 | tf_op jit(solution)/shard_map/ppermute | solution.py:294
  909.1 35.1 %collective-permute-done.59 = bf16[1,160,384]{2,1,0:T(8,128)(2,1)S(1)} collective-permute-done((bf16[1,160,384]{2,1,0:T(8,128)(2,1)S(1)}, bf16[1,160,384]{2,1,0:T(8,128)(2,1)S(1)}, u32[]{:S(2)}, u32[]{:S(2)}) %collective-permute-start.59) | collective-permute-done | bytes 122912 | tf_op jit(solution)/shard_map/ppermute | solution.py:294
  963.8 14.0 %collective-permute-done.50 = bf16[4,160,640]{2,1,0:T(8,128)(2,1)S(1)} collective-permute-done((bf16[4,160,640]{2,1,0:T(8,128)(2,1)S(1)}, bf16[4,160,640]{2,1,0:T(8,128)(2,1)S(1)}, u32[]{:S(2)}, u32[]{:S(2)}) %collective-permute-start.50) | collective-permute-done | bytes 819232 | tf_op jit(solution)/shard_map/ppermute | solution.py:294
  (548 shorter events, 599.8 us)
Async XLA Ops:
  13.7 41.6 %collective-permute-start = (bf16[1,112,640]{2,1,0:T(8,128)(2,1)}, bf16[1,112,640]{2,1,0:T(8,128)(2,1)}, u32[]{:S(2)}, u32[]{:S(2)}) collective-permute-start(bf16[1,112,640]{2,1,0:T(8,128)(2,1)} %slice_bitcast_fusion.2), channel_id=1, source_target_pairs={{0,8},{1,9},{2,10},{3,11},{4,12},{5,13},{6,14},{7,15},{8,16},{9,17... | collective-permute-start | bytes 430088 | tf_op jit(solution)/shard_map/ppermute | solution.py:270
  16.2 42.4 %collective-permute-start.24 = (bf16[1,128,640]{2,1,0:T(8,128)(2,1)S(1)}, bf16[1,128,640]{2,1,0:T(8,128)(2,1)S(1)}, u32[]{:S(2)}, u32[]{:S(2)}) collective-permute-start(bf16[1,128,640]{2,1,0:T(8,128)(2,1)S(1)} %slice_bitcast_fusion.1), channel_id=1, source_target_pairs={{0,8},{1,9},{2,10},{3,11},{4,12},{5,13},{6,14},{7,15},{8,16},{9,17... | collective-permute-start | bytes 491528 | tf_op jit(solution)/shard_map/ppermute | solution.py:270
  24.2 36.9 %collective-permute-start.12 = (bf16[1,160,640]{2,1,0:T(8,128)(2,1)S(1)}, bf16[1,160,640]{2,1,0:T(8,128)(2,1)S(1)}, u32[]{:S(2)}, u32[]{:S(2)}) collective-permute-start(bf16[1,160,640]{2,1,0:T(8,128)(2,1)S(1)} %slice_bitcast_fusion), channel_id=1, source_target_pairs={{0,8},{1,9},{2,10},{3,11},{4,12},{5,13},{6,14},{7,15},{8,16},{9,17... | collective-permute-start | bytes 614408 | tf_op jit(solution)/shard_map/ppermute | solution.py:270
  85.4 36.9 %collective-permute-start.14 = (bf16[1,160,640]{2,1,0:T(8,128)(2,1)S(1)}, bf16[1,160,640]{2,1,0:T(8,128)(2,1)S(1)}, u32[]{:S(2)}, u32[]{:S(2)}) collective-permute-start(bf16[1,160,640]{2,1,0:T(8,128)(2,1)S(1)} %collective-permute-done.13), channel_id=1, source_target_pairs={{0,8},{1,9},{2,10},{3,11},{4,12},{5,13},{6,14},{7,15},{8,16},{9,17... | collective-permute-start | bytes 614408 | tf_op jit(solution)/shard_map/ppermute | solution.py:270
  118.7 51.3 %collective-permute-start.22 = (bf16[8,160,384]{2,1,0:T(8,128)(2,1)S(1)}, bf16[8,160,384]{2,1,0:T(8,128)(2,1)S(1)}, u32[]{:S(2)}, u32[]{:S(2)}) collective-permute-start(bf16[8,160,384]{2,1,0:T(8,128)(2,1)S(1)} %get-tuple-element.130), channel_id=1, source_target_pairs={{0,4},{1,5},{2,6},{3,7},{4,0},{5,1},{6,2},{7,3},{8,12},{9,13},{10,... | collective-permute-start | bytes 2949128 | tf_op jit(solution)/shard_map/ppermute | solution.py:272
  120.4 63.7 %collective-permute-start.4 = (bf16[8,112,640]{2,1,0:T(8,128)(2,1)S(1)}, bf16[8,112,640]{2,1,0:T(8,128)(2,1)S(1)}, u32[]{:S(2)}, u32[]{:S(2)}) collective-permute-start(bf16[8,112,640]{2,1,0:T(8,128)(2,1)S(1)} %get-tuple-element.112), channel_id=1, source_target_pairs={{0,2},{1,3},{2,0},{3,1},{4,6},{5,7},{6,4},{7,5},{8,10},{9,11},{10,... | collective-permute-start | bytes 3440648 | tf_op jit(solution)/shard_map/ppermute | solution.py:272
  122.3 63.9 %collective-permute-start.28 = (bf16[8,128,640]{2,1,0:T(8,128)(2,1)S(1)}, bf16[8,128,640]{2,1,0:T(8,128)(2,1)S(1)}, u32[]{:S(2)}, u32[]{:S(2)}) collective-permute-start(bf16[8,128,640]{2,1,0:T(8,128)(2,1)S(1)} %get-tuple-element.109), channel_id=1, source_target_pairs={{0,2},{1,3},{2,0},{3,1},{4,6},{5,7},{6,4},{7,5},{8,10},{9,11},{10,... | collective-permute-start | bytes 3932168 | tf_op jit(solution)/shard_map/ppermute | solution.py:272
  132.1 50.3 %collective-permute-start.15 = (bf16[4,160,640]{2,1,0:T(8,128)(2,1)S(1)}, bf16[4,160,640]{2,1,0:T(8,128)(2,1)S(1)}, u32[]{:S(2)}, u32[]{:S(2)}) collective-permute-start(bf16[4,160,640]{2,1,0:T(8,128)(2,1)S(1)} %pad_maximum_fusion.7), channel_id=1, source_target_pairs={{0,4},{1,5},{2,6},{3,7},{4,0},{5,1},{6,2},{7,3},{8,12},{9,13},{10,... | collective-permute-start | bytes 2457608 | tf_op jit(solution)/shard_map/ppermute | solution.py:272
  149.0 39.8 %collective-permute-start.11 = (bf16[16,112,384]{2,1,0:T(8,128)(2,1)S(1)}, bf16[16,112,384]{2,1,0:T(8,128)(2,1)S(1)}, u32[]{:S(2)}, u32[]{:S(2)}) collective-permute-start(bf16[16,112,384]{2,1,0:T(8,128)(2,1)S(1)} %get-tuple-element.105), channel_id=1, source_target_pairs={{0,1},{1,0},{2,3},{3,2},{4,5},{5,4},{6,7},{7,6},{8,9},{9,8},{10,11... | collective-permute-start | bytes 4128776 | tf_op jit(solution)/shard_map/ppermute | solution.py:272
  182.4 43.7 %collective-permute-start.23 = (bf16[16,160,384]{2,1,0:T(8,128)(2,1)}, bf16[16,160,384]{2,1,0:T(8,128)(2,1)}, u32[]{:S(2)}, u32[]{:S(2)}) collective-permute-start(bf16[16,160,384]{2,1,0:T(8,128)(2,1)} %get-tuple-element.98), channel_id=1, source_target_pairs={{0,1},{1,0},{2,3},{3,2},{4,5},{5,4},{6,7},{7,6},{8,9},{9,8},{10,11... | collective-permute-start | bytes 5898248 | tf_op jit(solution)/shard_map/ppermute | solution.py:272
  184.1 38.5 %collective-permute-start.16 = (bf16[8,160,640]{2,1,0:T(8,128)(2,1)}, bf16[8,160,640]{2,1,0:T(8,128)(2,1)}, u32[]{:S(2)}, u32[]{:S(2)}) collective-permute-start(bf16[8,160,640]{2,1,0:T(8,128)(2,1)} %get-tuple-element.102), channel_id=1, source_target_pairs={{0,2},{1,3},{2,0},{3,1},{4,6},{5,7},{6,4},{7,5},{8,10},{9,11},{10,... | collective-permute-start | bytes 4915208 | tf_op jit(solution)/shard_map/ppermute | solution.py:272
  186.2 52.6 %collective-permute-start.5 = (bf16[16,112,640]{2,1,0:T(8,128)(2,1)}, bf16[16,112,640]{2,1,0:T(8,128)(2,1)}, u32[]{:S(2)}, u32[]{:S(2)}) collective-permute-start(bf16[16,112,640]{2,1,0:T(8,128)(2,1)} %get-tuple-element.88), channel_id=1, source_target_pairs={{0,1},{1,0},{2,3},{3,2},{4,5},{5,4},{6,7},{7,6},{8,9},{9,8},{10,11... | collective-permute-start | bytes 6881288 | tf_op jit(solution)/shard_map/ppermute | solution.py:272
  188.8 149.7 %collective-permute-start.29 = (bf16[16,128,640]{2,1,0:T(8,128)(2,1)}, bf16[16,128,640]{2,1,0:T(8,128)(2,1)}, u32[]{:S(2)}, u32[]{:S(2)}) collective-permute-start(bf16[16,128,640]{2,1,0:T(8,128)(2,1)} %get-tuple-element.86), channel_id=1, source_target_pairs={{0,1},{1,0},{2,3},{3,2},{4,5},{5,4},{6,7},{7,6},{8,9},{9,8},{10,11... | collective-permute-start | bytes 7864328 | tf_op jit(solution)/shard_map/ppermute | solution.py:272
  226.1 134.5 %collective-permute-start.17 = (bf16[16,160,640]{2,1,0:T(8,128)(2,1)}, bf16[16,160,640]{2,1,0:T(8,128)(2,1)}, u32[]{:S(2)}, u32[]{:S(2)}) collective-permute-start(bf16[16,160,640]{2,1,0:T(8,128)(2,1)} %get-tuple-element.84), channel_id=1, source_target_pairs={{0,1},{1,0},{2,3},{3,2},{4,5},{5,4},{6,7},{7,6},{8,9},{9,8},{10,11... | collective-permute-start | bytes 9830408 | tf_op jit(solution)/shard_map/ppermute | solution.py:272
  744.1 55.4 %collective-permute-start.42 = (bf16[16,112,384]{2,1,0:T(8,128)(2,1)}, bf16[16,112,384]{2,1,0:T(8,128)(2,1)}, u32[]{:S(2)}, u32[]{:S(2)}) collective-permute-start(bf16[16,112,384]{2,1,0:T(8,128)(2,1)} %slice.503), channel_id=1, source_target_pairs={{0,1},{1,0},{2,3},{3,2},{4,5},{5,4},{6,7},{7,6},{8,9},{9,8},{10,11... | collective-permute-start | bytes 4128776 | tf_op jit(solution)/shard_map/ppermute | solution.py:294
  759.7 79.5 %collective-permute-start.36 = (bf16[16,112,640]{2,1,0:T(8,128)(2,1)}, bf16[16,112,640]{2,1,0:T(8,128)(2,1)}, u32[]{:S(2)}, u32[]{:S(2)}) collective-permute-start(bf16[16,112,640]{2,1,0:T(8,128)(2,1)} %slice.493), channel_id=1, source_target_pairs={{0,1},{1,0},{2,3},{3,2},{4,5},{5,4},{6,7},{7,6},{8,9},{9,8},{10,11... | collective-permute-start | bytes 6881288 | tf_op jit(solution)/shard_map/ppermute | solution.py:294
  773.0 90.6 %collective-permute-start.60 = (bf16[16,128,640]{2,1,0:T(8,128)(2,1)}, bf16[16,128,640]{2,1,0:T(8,128)(2,1)}, u32[]{:S(2)}, u32[]{:S(2)}) collective-permute-start(bf16[16,128,640]{2,1,0:T(8,128)(2,1)} %slice.542), channel_id=1, source_target_pairs={{0,1},{1,0},{2,3},{3,2},{4,5},{5,4},{6,7},{7,6},{8,9},{9,8},{10,11... | collective-permute-start | bytes 7864328 | tf_op jit(solution)/shard_map/ppermute | solution.py:294
  780.5 44.3 %collective-permute-start.66 = (bf16[16,128,384]{2,1,0:T(8,128)(2,1)}, bf16[16,128,384]{2,1,0:T(8,128)(2,1)}, u32[]{:S(2)}, u32[]{:S(2)}) collective-permute-start(bf16[16,128,384]{2,1,0:T(8,128)(2,1)} %slice.553), channel_id=1, source_target_pairs={{0,1},{1,0},{2,3},{3,2},{4,5},{5,4},{6,7},{7,6},{8,9},{9,8},{10,11... | collective-permute-start | bytes 4718600 | tf_op jit(solution)/shard_map/ppermute | solution.py:294
  824.9 69.0 %collective-permute-start.48 = (bf16[16,160,640]{2,1,0:T(8,128)(2,1)}, bf16[16,160,640]{2,1,0:T(8,128)(2,1)S(1)}, u32[]{:S(2)}, u32[]{:S(2)}) collective-permute-start(bf16[16,160,640]{2,1,0:T(8,128)(2,1)} %slice.521), channel_id=1, source_target_pairs={{0,1},{1,0},{2,3},{3,2},{4,5},{5,4},{6,7},{7,6},{8,9},{9,8},{10,11... | collective-permute-start | bytes 9830408 | tf_op jit(solution)/shard_map/ppermute | solution.py:294
  847.5 38.2 %collective-permute-start.37 = (bf16[8,112,640]{2,1,0:T(8,128)(2,1)S(1)}, bf16[8,112,640]{2,1,0:T(8,128)(2,1)S(1)}, u32[]{:S(2)}, u32[]{:S(2)}) collective-permute-start(bf16[8,112,640]{2,1,0:T(8,128)(2,1)S(1)} %slice.495), channel_id=1, source_target_pairs={{0,2},{1,3},{2,0},{3,1},{4,6},{5,7},{6,4},{7,5},{8,10},{9,11},{10,... | collective-permute-start | bytes 3440648 | tf_op jit(solution)/shard_map/ppermute | solution.py:294
  871.1 73.4 %collective-permute-start.61 = (bf16[8,128,640]{2,1,0:T(8,128)(2,1)S(1)}, bf16[8,128,640]{2,1,0:T(8,128)(2,1)S(1)}, u32[]{:S(2)}, u32[]{:S(2)}) collective-permute-start(bf16[8,128,640]{2,1,0:T(8,128)(2,1)S(1)} %slice.544), channel_id=1, source_target_pairs={{0,2},{1,3},{2,0},{3,1},{4,6},{5,7},{6,4},{7,5},{8,10},{9,11},{10,... | collective-permute-start | bytes 3932168 | tf_op jit(solution)/shard_map/ppermute | solution.py:294
  895.0 56.4 %collective-permute-start.49 = (bf16[8,160,640]{2,1,0:T(8,128)(2,1)S(1)}, bf16[8,160,640]{2,1,0:T(8,128)(2,1)S(1)}, u32[]{:S(2)}, u32[]{:S(2)}) collective-permute-start(bf16[8,160,640]{2,1,0:T(8,128)(2,1)S(1)} %slice.523), channel_id=1, source_target_pairs={{0,2},{1,3},{2,0},{3,1},{4,6},{5,7},{6,4},{7,5},{8,10},{9,11},{10,... | collective-permute-start | bytes 4915208 | tf_op jit(solution)/shard_map/ppermute | solution.py:294
  907.9 36.3 %collective-permute-start.59 = (bf16[1,160,384]{2,1,0:T(8,128)(2,1)S(1)}, bf16[1,160,384]{2,1,0:T(8,128)(2,1)S(1)}, u32[]{:S(2)}, u32[]{:S(2)}) collective-permute-start(bf16[1,160,384]{2,1,0:T(8,128)(2,1)S(1)} %slice.539), channel_id=1, source_target_pairs={{0,2},{1,3},{2,0},{3,1},{4,6},{5,7},{6,4},{7,5},{8,10},{9,11},{10,... | collective-permute-start | bytes 368648 | tf_op jit(solution)/shard_map/ppermute | solution.py:294
  908.7 35.6 %collective-permute-start.39 = (bf16[1,112,640]{2,1,0:T(8,128)(2,1)S(1)}, bf16[1,112,640]{2,1,0:T(8,128)(2,1)S(1)}, u32[]{:S(2)}, u32[]{:S(2)}) collective-permute-start(bf16[1,112,640]{2,1,0:T(8,128)(2,1)S(1)} %slice.499), channel_id=1, source_target_pairs={{0,8},{1,9},{2,10},{3,11},{4,12},{5,13},{6,14},{7,15},{8,16},{9,17... | collective-permute-start | bytes 430088 | tf_op jit(solution)/shard_map/ppermute | solution.py:289
  (123 other events, 1754.3 us)

commit v2 on v0

v2 whole, which is shorter than its diff:
```python
import functools
import jax
import jax.numpy as jnp
from jax import lax
from jax.experimental import pallas as pl
from jax.experimental.pallas import tpu as pltpu
from jax.sharding import PartitionSpec as P

D = 1024
HEADS = 16
LEN = 512
EPS = 1e-12
LOW = jnp.bfloat16
FULL = jnp.float32
MIB = 1024 * 1024
WIDE = 512
STRIP = 256


def dot_nn(left_side, right_side):
    return lax.dot_general(left_side, right_side, (((1,), (0,)), ((), ())), preferred_element_type=FULL)


def dot_nt(left_side, right_side):
    return lax.dot_general(left_side, right_side, (((1,), (1,)), ((), ())), preferred_element_type=FULL)


def dot_tn(left_side, right_side):
    return lax.dot_general(left_side, right_side, (((0,), (0,)), ((), ())), preferred_element_type=FULL)


def head_mask(rows, head):
    lane = lax.broadcasted_iota(jnp.int32, (rows, 128), 1)
    return (lane // 64) == head


def attend_kernel(q_ref, k_ref, v_ref, probs_ref, rows_ref):
    scale = (D // HEADS) ** -0.5
    queries = (q_ref[...].astype(FULL) * scale).astype(LOW)
    keys, values = k_ref[...], v_ref[...]
    mixed = jnp.zeros((LEN, 128), FULL)
    for head in range(2):
        mask = head_mask(LEN, head)
        zero = jnp.zeros((), LOW)
        scores = dot_nt(queries, jnp.where(mask, keys, zero))
        maxima = jnp.max(scores, axis=-1, keepdims=True)
        exponent = jnp.exp(scores - maxima)
        total = jnp.sum(exponent, axis=-1, keepdims=True)
        probs = (exponent * (1.0 / total)).astype(LOW)
        probs_ref[0, head] = probs
        mixed = mixed + dot_nn(probs, jnp.where(mask, values, zero))
    rows_ref[...] = mixed.astype(LOW)


def placed(kernel, ins, count, *refs):
    kernel(*refs[:ins], *refs[ins + count :])


def continued(kernel, before, in_specs, out_specs, out_shape, **rest):
    aliases = {}
    if before:
        count = len(before)
        kernel = functools.partial(placed, kernel, len(in_specs), count)
        aliases = {len(in_specs) + index: index for index in range(count)}
        in_specs = list(in_specs) + [pl.BlockSpec(memory_space=pl.ANY)] * count
    call = pl.pallas_call(
        kernel, in_specs=in_specs, out_specs=out_specs, out_shape=out_shape, input_output_aliases=aliases, **rest
    )
    return lambda *operands: call(*operands, *before)


def attend(queries, keys, values, sequence, before=()):
    rows = queries.shape[0]
    column = pl.BlockSpec((LEN, 128), lambda p: (sequence, p))
    return continued(
        attend_kernel,
        before,
        grid=(HEADS // 2,),
        in_specs=[column] * 3,
        out_specs=[pl.BlockSpec((1, 2, LEN, LEN), lambda p: (sequence, p, 0, 0)), column],
        out_shape=[
            jax.ShapeDtypeStruct((rows // LEN, HEADS, LEN, LEN), LOW),
            jax.ShapeDtypeStruct((rows, D), LOW),
        ],
        compiler_params=pltpu.CompilerParams(vmem_limit_bytes=32 * MIB),
        cost_estimate=pl.CostEstimate(
            flops=12 * HEADS * LEN * LEN * 256, bytes_accessed=HEADS * LEN * LEN * 2 + LEN * D * 8,
            transcendentals=HEADS * LEN * LEN),
        name="attend",
    )(queries, keys, values)


def attend_back_kernel(q_ref, k_ref, v_ref, probs_ref, grad_ref, dq_ref, dk_ref, dv_ref):
    scale = (D // HEADS) ** -0.5
    queries, keys, values, grads = q_ref[...], k_ref[...], v_ref[...], grad_ref[...]
    zero = jnp.zeros((), LOW)
    d_queries = jnp.zeros((LEN, 128), FULL)
    d_keys = jnp.zeros((128, LEN), FULL)
    d_values = jnp.zeros((128, LEN), FULL)
    for head in range(2):
        mask = head_mask(LEN, head)
        probs = probs_ref[0, head]
        own_grads = jnp.where(mask, grads, zero)
        d_probs = dot_nt(own_grads, values).astype(LOW).astype(FULL)
        wide = probs.astype(FULL)
        product = d_probs * wide
        total = jnp.sum(product, axis=-1, keepdims=True)
        d_scores = (product - wide * total).astype(LOW)
        d_queries = d_queries + dot_nn(d_scores, jnp.where(mask, keys, zero))
        d_keys = d_keys + dot_tn(jnp.where(mask, queries, zero), d_scores)
        d_values = d_values + dot_tn(own_grads, probs)
    dq_ref[...] = (scale * d_queries).astype(LOW)
    dk_ref[...] = (scale * d_keys.T).astype(LOW)
    dv_ref[...] = d_values.T.astype(LOW)


def attend_back(queries, keys, values, probs, grads, sequence, before=()):
    rows = queries.shape[0]
    column = pl.BlockSpec((LEN, 128), lambda p: (sequence, p))
    return continued(
        attend_back_kernel,
        before,
        grid=(HEADS // 2,),
        in_specs=[column, column, column, pl.BlockSpec((1, 2, LEN, LEN), lambda p: (sequence, p, 0, 0)), column],
        out_specs=[column] * 3,
        out_shape=[jax.ShapeDtypeStruct((rows, D), LOW)] * 3,
        compiler_params=pltpu.CompilerParams(vmem_limit_bytes=32 * MIB),
        cost_estimate=pl.CostEstimate(
            flops=12 * HEADS * LEN * LEN * 256, bytes_accessed=HEADS * LEN * LEN * 2 + LEN * D * 14, transcendentals=0),
        name="attend_back",
    )(queries, keys, values, probs, grads)


def gelu_both(point):
    bell = jnp.exp(point * point * -0.5)
    ratio = 1.0 / (1.0 + (0.3275911 * 0.5**0.5) * jnp.abs(point))
    series = 0.5 * 1.061405429
    for factor in (-1.453152027, 1.421413741, -0.284496736, 0.254829592):
        series = series * ratio + 0.5 * factor
    below = series * ratio * bell
    normal = jnp.where(point < 0, below, 1.0 - below)
    return point * normal, normal + point * bell * 0.3989422804014327


def norm_rows(summed):
    centered = summed - jnp.mean(summed, axis=-1, keepdims=True)
    inverse = lax.rsqrt(jnp.mean(centered * centered, axis=-1, keepdims=True) + EPS)
    return centered * inverse, inverse


def norm_back_rows(scaled, normed, inverse):
    mean_grad = jnp.mean(scaled, axis=-1, keepdims=True)
    mean_cross = jnp.mean(scaled * normed, axis=-1, keepdims=True)
    return inverse * (scaled - mean_grad - normed * mean_cross)


def strips(rows, body):
    def step(index, carry):
        body(pl.ds(pl.multiple_of(index * STRIP, STRIP), STRIP))
        return carry

    lax.fori_loop(0, rows // STRIP, step, 0)


def fixed(array):
    return pl.BlockSpec(array.shape, lambda *place: (0,) * array.ndim, pipeline_mode=pl.Buffered(1))


def held(rows, cols):
    return pl.BlockSpec((rows, cols), lambda *place: (0, 0), pipeline_mode=pl.Buffered(1))


def branch_kernel(attn_ref, tokens_ref, wout_ref, bout_ref, gain_ref, shift_ref, normed_ref, inverse_ref, low_ref):
    summed = tokens_ref[...].astype(FULL) + dot_nn(attn_ref[...], wout_ref[...]) + bout_ref[...]
    normed, inverse = norm_rows(summed)
    normed_ref[...] = normed
    inverse_ref[...] = inverse
    low_ref[...] = (normed * gain_ref[...] + shift_ref[...]).astype(LOW)


def branch(attn_rows, tokens, w_out, b_out, gain, shift):
    rows = tokens.shape[0]
    strip = lambda cols: pl.BlockSpec((STRIP, cols), lambda i: (i, 0))
    return pl.pallas_call(
        branch_kernel,
        grid=(rows // STRIP,),
        in_specs=[strip(D), strip(D), fixed(w_out), fixed(b_out), fixed(gain), fixed(shift)],
        out_specs=[strip(D), strip(1), strip(D)],
        out_shape=[
            jax.ShapeDtypeStruct((rows, D), FULL), jax.ShapeDtypeStruct((rows, 1), FULL),
            jax.ShapeDtypeStruct((rows, D), LOW),
        ],
        compiler_params=pltpu.CompilerParams(vmem_limit_bytes=32 * MIB),
        cost_estimate=pl.CostEstimate(flops=4 * rows * D * D, bytes_accessed=rows * D * 10 + D * D * 2, transcendentals=0),
        name="branch",
    )(attn_rows, tokens, w_out, b_out, gain, shift)


def widen_kernel(low_ref, wup_ref, bup_ref, hidden_ref, slope_ref):
    def strip(rows):
        point = dot_nn(low_ref[rows, :], wup_ref[...]) + bup_ref[...]
        hidden, slope = gelu_both(point)
        hidden_ref[rows, :] = hidden.astype(LOW)
        slope_ref[rows, :] = slope.astype(LOW)

    strips(low_ref.shape[0], strip)


def widen(first_low, w_up, b_up, first, last, before=()):
    rows, width = first_low.shape[0], w_up.shape[1]
    chunk = lambda height: pl.BlockSpec((height, WIDE), lambda i: (0, i + first))
    return continued(
        widen_kernel,
        before,
        grid=(last - first,),
        in_specs=[fixed(first_low), chunk(D), chunk(1)],
        out_specs=[chunk(rows), chunk(rows)],
        out_shape=[jax.ShapeDtypeStruct((rows, width), LOW)] * 2,
        compiler_params=pltpu.CompilerParams(vmem_limit_bytes=32 * MIB),
        cost_estimate=pl.CostEstimate(
            flops=6 * rows * D * WIDE * (last - first), bytes_accessed=WIDE * (last - first) * (D * 2 + rows * 4),
            transcendentals=rows * WIDE * (last - first)),
        name="widen",
    )(first_low, w_up, b_up)


def fall_kernel(hidden_ref, wdown_ref, normed_ref, cot_ref, bdown_ref, gain1_ref, shift1_ref, gain2_ref, shift2_ref,
                out_ref, second_ref, ffn_ref, sums_ref, total):
    step = pl.program_id(0)

    @pl.when(step == 0)
    def _():
        total[...] = dot_nn(hidden_ref[...], wdown_ref[...])

    @pl.when(step > 0)
    def _():
        total[...] += dot_nn(hidden_ref[...], wdown_ref[...])

    @pl.when(step == pl.num_programs(0) - 1)
    def _():
        sums_ref[...] = jnp.zeros_like(sums_ref)

        def finish(rows):
            first_out = normed_ref[rows, :] * gain1_ref[...] + shift1_ref[...]
            normed, inverse = norm_rows(first_out + total[rows, :] + bdown_ref[...])
            out_ref[rows, :] = (normed * gain2_ref[...] + shift2_ref[...]).astype(LOW)
            upstream = cot_ref[rows, :].astype(FULL)
            second = norm_back_rows(upstream * gain2_ref[...], normed, inverse)
            low = second.astype(LOW)
            second_ref[rows, :] = second
            ffn_ref[rows, :] = low
            sums_ref[...] += jnp.concatenate([
                jnp.sum(part, axis=0, keepdims=True) for part in (upstream * normed, upstream, low.astype(FULL))
            ], axis=0)

        strips(out_ref.shape[0], finish)


def fall(hidden, w_down, normed, cotangent, b_down, gain1, shift1, gain2, shift2, chunk=1024):
    rows, width = hidden.shape
    return pl.pallas_call(
        fall_kernel,
        grid=(width // chunk,),
        in_specs=[
            pl.BlockSpec((rows, chunk), lambda i: (0, i)), pl.BlockSpec((chunk, D), lambda i: (i, 0)),
        ] + [fixed(a) for a in (normed, cotangent, b_down, gain1, shift1, gain2, shift2)],
        out_specs=[held(rows, D), held(rows, D), held(rows, D), held(3, D)],
        out_shape=[
            jax.ShapeDtypeStruct((rows, D), LOW), jax.ShapeDtypeStruct((rows, D), FULL),
            jax.ShapeDtypeStruct((rows, D), LOW), jax.ShapeDtypeStruct((3, D), FULL),
        ],
        scratch_shapes=[pltpu.VMEM((rows, D), FULL)],
        compiler_params=pltpu.CompilerParams(vmem_limit_bytes=40 * MIB),
        cost_estimate=pl.CostEstimate(
            flops=2 * rows * D * width, bytes_accessed=rows * (D * 14 + width * 2) + D * width * 2, transcendentals=0),
        name="fall",
    )(hidden, w_down, normed, cotangent, b_down, gain1, shift1, gain2, shift2)


def narrow_kernel(ffn_ref, slope_ref, wdown_ref, wup_ref, so_far_ref, pre_ref, wide_ref, total_ref):
    @pl.when(pl.program_id(0) == 0)
    def _():
        total_ref[...] = so_far_ref[...]

    wide_ref[...] = jnp.zeros_like(wide_ref)

    def strip(rows):
        d_hidden = dot_nt(ffn_ref[rows, :], wdown_ref[...])
        d_pre = (slope_ref[rows, :].astype(FULL) * d_hidden).astype(LOW)
        pre_ref[rows, :] = d_pre
        wide_ref[...] += jnp.sum(d_pre.astype(FULL), axis=0, keepdims=True)
        total_ref[rows, :] += dot_nt(d_pre, wup_ref[...])

    strips(ffn_ref.shape[0], strip)


def narrow(d_ffn, slope, w_down, w_up, so_far, first, last, before=()):
    rows, width = slope.shape
    chunk = lambda height: pl.BlockSpec((height, WIDE), lambda i: (0, i + first))
    return continued(
        narrow_kernel,
        before,
        grid=(last - first,),
        in_specs=[
            fixed(d_ffn), chunk(rows), pl.BlockSpec((WIDE, D), lambda i: (i + first, 0)), chunk(D), fixed(so_far),
        ],
        out_specs=[chunk(rows), chunk(1), held(rows, D)],
        out_shape=[
            jax.ShapeDtypeStruct((rows, width), LOW), jax.ShapeDtypeStruct((1, width), FULL),
            jax.ShapeDtypeStruct((rows, D), FULL),
        ],
        compiler_params=pltpu.CompilerParams(vmem_limit_bytes=40 * MIB),
        cost_estimate=pl.CostEstimate(
            flops=6 * rows * D * WIDE * (last - first), bytes_accessed=WIDE * (last - first) * (D * 4 + rows * 4) + rows * D * 10,
            transcendentals=0),
        name="narrow",
    )(d_ffn, slope, w_down, w_up, so_far)


def resid_kernel(first_ref, normed_ref, inverse_ref, gain_ref, wout_ref, resid_ref, branch_ref, attn_ref, sums_ref):
    d_first, normed = first_ref[...], normed_ref[...]
    resid = norm_back_rows(d_first * gain_ref[...], normed, inverse_ref[...])
    low = resid.astype(LOW)
    resid_ref[...] = resid
    branch_ref[...] = low
    attn_ref[...] = dot_nt(low, wout_ref[...]).astype(LOW)
    sums = jnp.concatenate([
        jnp.sum(part, axis=0, keepdims=True) for part in (d_first * normed, d_first, low.astype(FULL))
    ], axis=0)

    @pl.when(pl.program_id(0) == 0)
    def _():
        sums_ref[...] = sums

    @pl.when(pl.program_id(0) > 0)
    def _():
        sums_ref[...] += sums


def resid_back(d_first, normed, inverse, gain, w_out):
    rows = d_first.shape[0]
    strip = lambda cols: pl.BlockSpec((STRIP, cols), lambda i: (i, 0))
    return pl.pallas_call(
        resid_kernel,
        grid=(rows // STRIP,),
        in_specs=[strip(D), strip(D), strip(1), fixed(gain), fixed(w_out)],
        out_specs=[strip(D), strip(D), strip(D), held(3, D)],
        out_shape=[
            jax.ShapeDtypeStruct((rows, D), FULL), jax.ShapeDtypeStruct((rows, D), LOW),
            jax.ShapeDtypeStruct((rows, D), LOW), jax.ShapeDtypeStruct((3, D), FULL),
        ],
        compiler_params=pltpu.CompilerParams(vmem_limit_bytes=32 * MIB),
        cost_estimate=pl.CostEstimate(flops=4 * rows * D * D, bytes_accessed=rows * D * 16 + D * D * 2, transcendentals=0),
        name="resid_back",
    )(d_first, normed, inverse, gain, w_out)


def tall_kernel(cut, left_ref, right_ref, keep1_ref, send1_ref, keep2_ref, send2_ref, product):
    core = lax.axis_index("dp") % 2
    product[...] = dot_tn(left_ref[...], right_ref[...]).astype(LOW).reshape(product.shape)
    for keep, send, low, high in ((keep1_ref, send1_ref, 0, cut), (keep2_ref, send2_ref, cut, product.shape[-1])):
        for pair in range(2):
            keep[pair] = product[pair, core, :, low:high]
            send[pair] = product[pair, 1 - core, :, low:high]


def outer_tall(left, right, cut, count):
    rows, width = left.shape
    cols, part = right.shape[1], width // count
    out = lambda size: pl.BlockSpec((2, part, size), lambda i: (i, 0, 0))
    shape = lambda size: jax.ShapeDtypeStruct((count // 2, part, size), LOW)
    sizes = (cut, cut, cols - cut, cols - cut)
    return pl.pallas_call(
        functools.partial(tall_kernel, cut),
        grid=(count // 4,),
        in_specs=[pl.BlockSpec((rows, 4 * part), lambda i: (0, i)), fixed(right)],
        out_specs=[out(size) for size in sizes],
        out_shape=[shape(size) for size in sizes],
        scratch_shapes=[pltpu.VMEM((2, 2, part, cols), LOW)],
        compiler_params=pltpu.CompilerParams(vmem_limit_bytes=32 * MIB),
        cost_estimate=pl.CostEstimate(
            flops=2 * rows * width * cols, bytes_accessed=2 * (rows * (width + cols) + width * cols), transcendentals=0),
        name="outer_tall",
    )(left, right)


def wide_kernel(starts, first, *refs):
    pairs = len(starts) - 1
    lefts, rights, outs, product = refs[:pairs], refs[pairs : 2 * pairs], refs[2 * pairs : -1], refs[-1]
    step = pl.program_id(0)
    core = lax.axis_index("dp") % 2
    for left, right, low, high in zip(lefts, rights, starts, starts[1:]):
        @pl.when((step >= low) & (step < high))
        def _():
            product[...] = dot_tn(left[...], right[...]).astype(LOW).reshape(product.shape)

    for keep, send, wanted in ((outs[0], outs[1], step < first), (outs[2], outs[3], step >= first)):
        @pl.when(wanted)
        def _():
            keep[...] = product[:, core]
            send[...] = product[:, 1 - core]


def outer_wide(lefts, rights, first, count):
    rows, height = lefts[0].shape
    part = height // count
    starts = [0]
    for right in rights:
        starts.append(starts[-1] + right.shape[1] // WIDE)
    total = starts[-1]

    def strip(low, high):
        return pl.BlockSpec((rows, WIDE), lambda i: (0, jnp.clip(i - low, 0, high - low - 1)))

    def out(low, high):
        return pl.BlockSpec((count // 2, part, WIDE), lambda i: (0, 0, jnp.clip(i - low, 0, high - low - 1)))

    ranges = ((0, first), (0, first), (first, total), (first, total))
    return pl.pallas_call(
        functools.partial(wide_kernel, starts, first),
        grid=(total,),
        in_specs=[fixed(left) for left in lefts] + [strip(low, high) for low, high in zip(starts, starts[1:])],
        out_specs=[out(low, high) for low, high in ranges],
        out_shape=[jax.ShapeDtypeStruct((count // 2, part, WIDE * (high - low)), LOW) for low, high in ranges],
        scratch_shapes=[pltpu.VMEM((count // 2, 2, part, WIDE), LOW)],
        compiler_params=pltpu.CompilerParams(vmem_limit_bytes=32 * MIB),
        cost_estimate=pl.CostEstimate(
            flops=2 * rows * height * WIDE * total,
            bytes_accessed=2 * (rows * (height * len(lefts) + WIDE * total) + height * WIDE * total), transcendentals=0),
        name="outer_wide",
    )(*lefts, *rights)


FLIPS = {"c": 1, "x": 2, "y": 4}
ORDERS = ("zyx", "xzy")


def ring_pairs(count):
    return [(place, (place + 8) % count) for place in range(count)]


def hop(array, dim, count):
    if dim == "z":
        return lax.ppermute(array, "dp", ring_pairs(count))
    return lax.ppermute(array, "dp", [(place, place ^ FLIPS[dim]) for place in range(count)])


def after(value, *earlier):
    return lax.optimization_barrier((value, earlier))[0]


def mine_of(count):
    me = lax.axis_index("dp")
    return {"z": lax.shift_right_logical(me, 3), "y": lax.shift_right_logical(me, 2) & 1,
            "x": lax.shift_right_logical(me, 1) & 1, "c": me & 1}


def gather_part(shard, order, count, marks):
    stack = after(shard, marks[-1])[None] if marks else shard[None]
    for dim in order[:2]:
        pieces = [stack]
        for _ in range(count // 8 - 1 if dim == "z" else 1):
            pieces.append(hop(pieces[-1], dim, count))
        stack = jnp.concatenate(pieces, axis=0)
        if dim == "z":
            marks.append(pieces[-1])
    across = hop(stack, order[2], count)
    return (stack, across, hop(stack, "c", count), hop(across, "c", count))


def place_kernel(count, cuts, bases, rows, *refs):
    pieces, outs, sem = refs[:8], refs[8:-1], refs[-1]
    ring = count // 8
    mine = mine_of(count)

    def owner(digits):
        z = lax.rem(mine["z"] + ring - digits["z"], ring)
        low = [1 - mine[dim] if digits[dim] else mine[dim] for dim in "yxc"]
        return z * 8 + low[0] * 4 + low[1] * 2 + low[2]

    for part, order in enumerate(ORDERS):
        left, right = cuts[part], cuts[part + 1]
        for which in range(4):
            for slot in range(count // 4):
                digits = {"c": which // 2, order[2]: which % 2}
                rest = slot
                for dim in order[:2]:
                    size = ring if dim == "z" else 2
                    digits[dim] = rest % size
                    rest = rest // size
                row = pl.ds(pl.multiple_of(owner(digits) * rows, rows), rows)
                for out, base, stop in zip(outs, bases, bases[1:]):
                    low, high = max(left, base), min(right, stop)
                    if low < high:
                        pltpu.make_async_copy(
                            pieces[4 * part + which].at[slot, :, pl.ds(low - left, high - low)],
                            out.at[row, pl.ds(low - base, high - low)],
                            sem,
                        ).start()
    for out in outs:
        pltpu.make_async_copy(out, out, sem).wait()


def gather(shard, widths, cut, count, marks):
    rows, total = shard.shape
    bases = [sum(widths[:index]) for index in range(len(widths) + 1)]
    if count != 32:
        full = lax.all_gather(shard, "dp", axis=0, tiled=True)
        return [full[:, low:high] for low, high in zip(bases, bases[1:])]
    cuts = (0, cut, total)
    pieces = []
    for order, low, high, own_marks in zip(ORDERS, cuts, cuts[1:], marks):
        pieces.extend(gather_part(shard[:, low:high], order, count, own_marks))
    return pl.pallas_call(
        functools.partial(place_kernel, count, cuts, bases, rows),
        in_specs=[pl.BlockSpec(memory_space=pl.ANY)] * 8,
        out_specs=[pl.BlockSpec(memory_space=pl.ANY)] * len(widths),
        out_shape=[jax.ShapeDtypeStruct((count * rows, width), LOW) for width in widths],
        scratch_shapes=[pltpu.SemaphoreType.DMA(())],
        cost_estimate=pl.CostEstimate(flops=0, bytes_accessed=4 * count * rows * total, transcendentals=0),
        name="place",
    )(*pieces)


def add_low(left_side, right_side, kind=LOW):
    return (left_side.astype(FULL) + right_side.astype(FULL)).astype(kind)


def take(blocks, axis, index):
    return lax.dynamic_index_in_dim(blocks, index, axis, keepdims=False, allow_negative_indices=False)


def scatter_steps(keep, send, order, count):
    ring = count // 8
    mine = mine_of(count)
    dims = ["z", "y", "x"]
    shape = (ring, 2, 2) + keep.shape[1:]
    yield send
    held = [keep.reshape(shape), hop(send, "c", count).reshape(shape)]

    def pick(dim, index):
        axis = dims.index(dim)
        return add_low(take(held[0], axis, index), take(held[1], axis, index))

    for dim in order[::-1]:
        own = mine[dim]
        if dim == "z":
            moving = pick("z", (own + ring - 1) & (ring - 1))
            for step in range(2, ring + 1):
                yield moving
                moving = hop(moving, "z", count)
                if step < ring:
                    moving = add_low(moving, pick("z", (own + ring - step) & (ring - 1)))
        else:
            moving = pick(dim, 1 - own)
            yield moving
            moving = hop(moving, dim, count)
        held = [pick(dim, own), moving]
        dims.remove(dim)
    yield add_low(held[0], held[1], FULL)


class Sums:
    def __init__(self, parts, count):
        self.chains = [scatter_steps(keep, send, order, count) for (keep, send), order in zip(parts, ORDERS)]
        self.last = [None] * len(parts)

    def move(self, which):
        self.last[which] = next(self.chains[which])
        return self.last[which]

    def result(self):
        for which, chain in enumerate(self.chains):
            for value in chain:
                self.last[which] = value
        return jnp.concatenate(self.last, axis=-1)


def local(
    tokens,
    w_query,
    w_key,
    w_value,
    w_out,
    w_up,
    w_down,
    b_query,
    b_value,
    b_out,
    b_up,
    b_down,
    gain_attn,
    shift_attn,
    gain_ffn,
    shift_ffn,
    cotangent,
):
    count = D // w_query.shape[0]
    part = D // count
    wide = w_up.shape[1]
    vectors = (b_query, b_value, b_out, b_down, gain_attn, shift_attn, gain_ffn, shift_ffn, b_up)
    packed = jnp.concatenate(vectors)
    packed = jnp.pad(packed, (0, part * 128 - packed.shape[0])).reshape(part, 128)
    marks = ([], [])
    w_query, w_key, w_value, packed = gather(
        jnp.concatenate([w_query, w_key, w_value, packed], axis=1), (D, D, D, 128), 2 * D, count, marks
    )
    w_up, w_out = gather(jnp.concatenate([w_up, w_out], axis=1), (wide, D), 3328, count, marks)
    (w_down,) = gather(w_down, (D,), 640, count, marks)
    flat = packed.reshape(count, part * 128)
    vector = lambda col: flat[:, part * col : part * col + part].reshape(1, D).astype(FULL)
    b_query, b_value, b_out, b_down, gain_attn, shift_attn, gain_ffn, shift_ffn = map(vector, range(8))
    b_up = flat[:, 8 * part : 8 * part + wide // count].reshape(1, wide).astype(FULL)
    chunks = wide // WIDE
    sequences = tokens.shape[0] // LEN

    queries = (dot_nn(tokens, w_query) + b_query).astype(LOW)
    keys = dot_nn(tokens, w_key).astype(LOW)
    values = (dot_nn(tokens, w_value) + b_value).astype(LOW)
    seen = ()
    for sequence in range(sequences):
        seen = attend(queries, keys, values, sequence, seen)
    probs, attn_rows = seen
    normed, inverse, first_low = branch(attn_rows, tokens, w_out, b_out, gain_attn, shift_attn)
    half = widen(first_low, w_up, b_up, 0, chunks // 2)
    hidden, slope = widen(first_low, w_up, b_up, chunks // 2, chunks, half)
    result, second, d_ffn, sums_ffn = fall(
        hidden, w_down, normed, cotangent, b_down, gain_attn, shift_attn, gain_ffn, shift_ffn
    )

    custom = count == 32
    down, up, first = None, None, None

    def then(value, *moves):
        if not custom:
            return value
        return after(value, *[sums.move(which) for sums, which in moves])

    if custom:
        parts = outer_tall(hidden, d_ffn, 640, count)
        down = Sums((parts[:2], parts[2:]), count)
    d_ffn = then(d_ffn, (down, 0), (down, 1))
    d_pre, d_b_up, d_first = narrow(d_ffn, slope, w_down, w_up, second, 0, 2)
    d_first = then(d_first, (down, 0), (down, 1))
    d_pre, d_b_up, d_first = narrow(d_ffn, slope, w_down, w_up, d_first, 2, 5, (d_pre, d_b_up, d_first)[:2])
    d_first = then(d_first, (down, 1))
    d_pre, d_b_up, d_first = narrow(d_ffn, slope, w_down, w_up, d_first, 5, chunks, (d_pre, d_b_up, d_first)[:2])
    d_resid, d_branch, d_attn, sums_attn = resid_back(d_first, normed, inverse, gain_attn, w_out)
    d_branch = then(d_branch, (down, 0), (down, 1))
    if custom:
        parts = outer_wide([first_low, attn_rows], [d_pre, d_branch], 6, count)
        up = Sums((parts[:2], parts[2:]), count)
    d_attn = then(d_attn, (down, 0), (down, 1), (up, 0), (up, 1))
    seen = attend_back(queries, keys, values, probs, d_attn, 0)
    d_attn = then(d_attn, (up, 0), (up, 1), (down, 0), (down, 1))
    for sequence in range(1, sequences):
        seen = attend_back(queries, keys, values, probs, d_attn, sequence, seen)
    d_queries, d_keys, d_values = seen
    d_queries = then(d_queries, (down, 0), (down, 1))
    column_sum = lambda rows: jnp.sum(rows.astype(FULL), axis=0)
    sums = (
        column_sum(d_queries), column_sum(d_values), sums_attn[2], sums_ffn[2],
        sums_attn[0], sums_attn[1], sums_ffn[0], sums_ffn[1], d_b_up[0],
    )
    packed = jnp.concatenate([total.astype(LOW).reshape(count, -1) for total in sums], axis=1)
    packed = jnp.pad(packed, ((0, 0), (0, part * 128 - packed.shape[1]))).reshape(count // 2, 2, part, 128)
    if custom:
        parts = outer_wide([tokens, tokens, tokens], [d_queries, d_keys, d_values], 4, count)
        send = jnp.concatenate([parts[3], take(packed, 1, 1 - mine_of(count)["c"])], axis=-1)
        keep = jnp.concatenate([parts[2], take(packed, 1, mine_of(count)["c"])], axis=-1)
        first = Sums((parts[:2], (keep, send)), count)
    d_queries = then(d_queries, (first, 0), (first, 1), (up, 1), (down, 0))
    grad_rows = d_resid + dot_nt(d_queries, w_query)
    d_keys = then(d_keys, (first, 0), (first, 1))
    grad_rows = grad_rows + dot_nt(d_keys, w_key)
    d_values = then(d_values, (up, 0), (up, 1))
    grad_rows = (grad_rows + dot_nt(d_values, w_value)).astype(LOW)

    if custom:
        d_w_down = down.result()
        second = up.result()
        first = first.result()
    else:
        total = lambda grad: lax.psum_scatter(grad.astype(LOW), "dp", scatter_dimension=0, tiled=True).astype(FULL)
        d_w_down = total(dot_tn(hidden, d_ffn))
        second = total(jnp.concatenate([dot_tn(first_low, d_pre), dot_tn(attn_rows, d_branch)], axis=1))
        first = [dot_tn(tokens, grad) for grad in (d_queries, d_keys, d_values)]
        first = total(jnp.concatenate(first + [packed.reshape(D, 128)], axis=1))
    flat = first[:, 3 * D :].reshape(-1)
    vector = lambda col: flat[part * col : part * col + part]
    return (
        result,
        grad_rows,
        first[:, :D],
        first[:, D : 2 * D],
        first[:, 2 * D : 3 * D],
        second[:, wide:],
        second[:, :wide],
        d_w_down,
        vector(0),
        vector(1),
        vector(2),
        flat[8 * part : 8 * part + wide // count],
        vector(3),
        vector(4),
        vector(5),
        vector(6),
        vector(7),
    )


def solution(mesh):
    placed = (
        P("dp", None),
        P("dp", None),
        P("dp", None),
        P("dp", None),
        P("dp", None),
        P("dp", None),
        P("dp", None),
        P("dp"),
        P("dp"),
        P("dp"),
        P("dp"),
        P("dp"),
        P("dp"),
        P("dp"),
        P("dp"),
        P("dp"),
        P("dp", None),
    )
    return jax.shard_map(
        local,
        mesh=mesh,
        in_specs=placed,
        out_specs=(
            P("dp", None),
            P("dp", None),
            P("dp", None),
            P("dp", None),
            P("dp", None),
            P("dp", None),
            P("dp", None),
            P("dp", None),
            P("dp"),
            P("dp"),
            P("dp"),
            P("dp"),
            P("dp"),
            P("dp"),
            P("dp"),
            P("dp"),
            P("dp"),
        ),
        check_vma=False,
    )
```

time: 1430 us -> 1350 us (0.944)
  Pallas kernels: 0 us -> 965 us
  waiting for transfers between devices: 843 us -> 177 us
  matrix products: 318 us -> 17.3 us
  blocking collectives: 123 us -> 0 us
  starting transfers between devices: 1.09 us -> 48.2 us
  local copies, waits for them, and re-layouts: 63 us -> 82 us
    pallas_call x0 -> x18, Pallas kernels: none -> 965 us  [the longest x3 774 us: gather(): pl.pallas_call(functools.partial(place_kernel, count, cuts, bases, rows),...]
    reduce_scatter x3 -> x0, waiting for transfers between devices: 369 us -> none  [the longest x1 187 us: local(): lax.psum_scatter(running[5], 'dp', scatter_dimension=0, tiled=True)]
    unnamed x15 -> x0, waiting for transfers between devices: 322 us -> none
    dot_general x48 -> x6, matrix products: 318 us -> 17.3 us  [the longest x3 8.76 us: dot_nn(): lax.dot_general(left_side, right_side, (((1,), (0,)), ((), ())), preferre...]
    ppermute x0 -> x78, waiting for transfers between devices: none -> 177 us  [the longest x36 127 us: hop(): return lax.ppermute(array, 'dp', ring_pairs(count))]
    all_gather x6 -> x0, waiting for transfers between devices: 152 us -> none  [the longest x1 49.8 us: local(): lax.all_gather(w_key, 'dp', axis=0, tiled=True)]
    unnamed x2 -> x0, blocking collectives: 82.9 us -> none
    ppermute x0 -> x78, starting transfers between devices: none -> 48.2 us  [the longest x42 32.5 us: hop(): lax.ppermute(array, 'dp', [(place, place ^ FLIPS[dim]) for place in range...]
  transfers between devices with their start and end apart: 12 -> 78, of which waited for: 10 -> 38; matrix products, arithmetic and copies ran while one was open for 23% -> 6% of each run, Pallas kernels for 0% -> 42%
where the time goes in v2:
time: 1350 us; the launch traced here: 1340 us
  Pallas kernels  965 us (71%)
  waiting for transfers between devices  177 us (13%)
  local copies, waits for them, and re-layouts  82 us (6%)
  other arithmetic  50.7 us (4%)
  starting transfers between devices  48.2 us (4%)
  matrix products  17.3 us (1%)
    pallas_call x3, Pallas kernels, gather(): pl.pallas_call(functools.partial(place_kernel, count, cuts, bases, rows),...  774 us
    ppermute x36, waiting for transfers between devices, hop(): return lax.ppermute(array, 'dp', ring_pairs(count))  127 us
    pallas_call x9, Pallas kernels, continued(): return lambda *operands: call(*operands, *before)  126 us
    unnamed x170, local copies, waits for them, and re-layouts  60.6 us
    ppermute x42, waiting for transfers between devices, hop(): lax.ppermute(array, 'dp', [(place, place ^ FLIPS[dim]) for place in range...  50 us
    convert_element_type x33, other arithmetic, add_low(): return (left_side.astype(FULL) + right_side.astype(FULL)).astype(kind)  35.7 us
    ppermute x42, starting transfers between devices, hop(): lax.ppermute(array, 'dp', [(place, place ^ FLIPS[dim]) for place in range...  32.5 us
  transfers between devices with their start and end apart: 78, of which 38 were waited for; matrix products, arithmetic and copies ran while one was open for 6% of the time, Pallas kernels for 42%

profile of v2, /device:TPU:0, one launch (start us, length us, event | category | flops | bytes accessed | tf_op | source)
XLA Modules:
  0.0 1342.8 jit_solution(2778083989116145569)
XLA Ops:
  81.8 6.3 collective-permute-done.30
  90.5 7.2 collective-permute-done.37
  119.5 199.6 %place.3 = (bf16[1024,1024]{1,0:T(8,128)(2,1)}, bf16[1024,1024]{1,0:T(8,128)(2,1)}, bf16[1024,1024]{1,0:T(8,128)(2,1)}, bf16[1024,128]{1,0:T(8,128)(2,1)}) custom-call(bf16[8,32,2048]{2,1,0:T(8,128)(2,1)} %copy-done.50, bf16[8,32,2048]{2,1,0:T(8,128)(2,1)} %copy-done.51, bf16[8,32,2048]{2,1,0:T(8,128)(2,1)} %copy-done.52, bf16[8,32,2048]{2,1,0:T(8,128)(2,1)} %copy-done.53, ...), custom_call_target="tpu_custom_call" | custom-call | bytes 13107200 | tf_op jit(solution)/shard_map/place/pallas_call | solution.py:514
  332.0 14.4 %attend.2 = (bf16[2,16,512,512]{3,2,1,0:T(8,128)(2,1)}, bf16[1024,1024]{1,0:T(8,128)(2,1)S(1)}) custom-call(bf16[1024,1024]{1,0:T(8,128)(2,1)S(1)} %fusion.q_ref.refs_0_, bf16[1024,1024]{1,0:T(8,128)(2,1)S(1)} %convert_bitcast_fusion.k_ref.refs_1_, bf16[1024,1024]{1,0:T(8,128)(2,1)S(1)} %fusion.1.v_ref.refs_2_), custom_call_target="tpu_custom_call" | custom-call | flops 12884901888 | bytes 12582912 | tf_op jit(solution)/shard_map/attend/pallas_call | solution.py:69
  355.9 14.0 %attend.3 = (bf16[2,16,512,512]{3,2,1,0:T(8,128)(2,1)}, bf16[1024,1024]{1,0:T(8,128)(2,1)S(1)}) custom-call(bf16[1024,1024]{1,0:T(8,128)(2,1)S(1)} %copy-done.43, bf16[1024,1024]{1,0:T(8,128)(2,1)S(1)} %copy-done.30, bf16[1024,1024]{1,0:T(8,128)(2,1)S(1)} %copy-done.40, ...), custom_call_target="tpu_custom_call", output_to_operand_aliasing={{0}: (3, {}), {1}: (4, {})} | custom-call | flops 12884901888 | bytes 12582912 | tf_op jit(solution)/shard_map/attend/pallas_call | solution.py:69
  371.2 255.2 %place.5.wdown_ref.refs_2_ = bf16[4096,1024]{1,0:T(8,128)(2,1)} custom-call(bf16[8,128,640]{2,1,0:T(8,128)(2,1)} %copy-done.49, bf16[8,128,640]{2,1,0:T(8,128)(2,1)} %collective-permute-done.32.refs_1_, bf16[8,128,640]{2,1,0:T(8,128)(2,1)} %collective-permute-done.33.refs_2_, bf16[8,128,640]{2,1,0:T(8,128)(2,1)} %collective-permute-done.34.refs_3_, ...), custom_call_target="tpu_custom_call" | custom-call | bytes 16777216 | tf_op jit(solution)/shard_map/place/pallas_call | solution.py:514
  627.9 318.7 %place.4 = (bf16[1024,4096]{1,0:T(8,128)(2,1)}, bf16[1024,1024]{1,0:T(8,128)(2,1)}) custom-call(bf16[8,32,3328]{2,1,0:T(8,128)(2,1)} %constant_dynamic-update-slice_fusion.10.refs_0_, bf16[8,32,3328]{2,1,0:T(8,128)(2,1)} %collective-permute-done.18.refs_1_, bf16[8,32,3328]{2,1,0:T(8,128)(2,1)} %copy-done.48, ...), custom_call_target="tpu_custom_call" | custom-call | bytes 20971520 | tf_op jit(solution)/shard_map/place/pallas_call | solution.py:514
  955.6 16.1 %widen.2 = (bf16[1024,4096]{1,0:T(8,128)(2,1)S(1)}, bf16[1024,4096]{1,0:T(8,128)(2,1)S(1)}) custom-call(bf16[1024,1024]{1,0:T(8,128)(2,1)S(1)} %get-tuple-element.93.low_ref.refs_0_, bf16[1024,4096]{1,0:T(8,128)(2,1)} %get-tuple-element.94.wup_ref.refs_1_.refs_3_, f32[1,4096]{1,0:T(1,128)S(1)} %bitcast.325), custom_call_target="tpu_custom_call" | custom-call | flops 12884901888 | bytes 12582912 | tf_op jit(solution)/shard_map/widen/pallas_call | solution.py:69
  971.8 15.5 %widen.3 = (bf16[1024,4096]{1,0:T(8,128)(2,1)S(1)}, bf16[1024,4096]{1,0:T(8,128)(2,1)S(1)}) custom-call(bf16[1024,1024]{1,0:T(8,128)(2,1)S(1)} %get-tuple-element.93.low_ref.refs_0_, bf16[1024,4096]{1,0:T(8,128)(2,1)} %get-tuple-element.94.wup_ref.refs_1_.refs_3_, f32[1,4096]{1,0:T(1,128)S(1)} %bitcast.326, ...), custom_call_target="tpu_custom_call", output_to_operand_aliasing={{0}: (3, {}), {1}: (4, {})} | custom-call | flops 12884901888 | bytes 12582912 | tf_op jit(solution)/shard_map/widen/pallas_call | solution.py:69
  993.9 17.2 %fall.1 = (bf16[1024,1024]{1,0:T(8,128)(2,1)}, f32[1024,1024]{1,0:T(8,128)S(1)}, bf16[1024,1024]{1,0:T(8,128)(2,1)S(1)}, f32[3,1024]{1,0:T(4,128)S(1)}) custom-call(bf16[1024,4096]{1,0:T(8,128)(2,1)} %copy-done.23, bf16[4096,1024]{1,0:T(8,128)(2,1)} %place.5.wdown_ref.refs_2_, f32[1024,1024]{1,0:T(8,128)S(1)} %get-tuple-element.100.normed_ref, ...), custom_call_target="tpu_custom_call" | custom-call | flops 8589934592 | bytes 31457280 | tf_op jit(solution)/shard_map/fall/pallas_call | solution.py:261
  1016.6 12.9 outer_tall.1
  1041.1 18.6 %collective-permute-done.44 = bf16[4,2,128,384]{3,2,1,0:T(8,128)(2,1)} collective-permute-done((bf16[4,2,128,384]{3,2,1,0:T(8,128)(2,1)}, bf16[4,2,128,384]{3,2,1,0:T(8,128)(2,1)}, u32[]{:S(2)}, u32[]{:S(2)}) %collective-permute-start.44) | collective-permute-done | bytes 786464 | tf_op jit(solution)/shard_map/ppermute | solution.py:445
  1063.3 10.1 narrow.3
  1079.2 13.4 narrow.4
  1095.4 13.5 %narrow.5 = (bf16[1024,4096]{1,0:T(8,128)(2,1)}, f32[1,4096]{1,0:T(1,128)S(1)}, f32[1024,1024]{1,0:T(8,128)S(1)}) custom-call(bf16[1024,1024]{1,0:T(8,128)(2,1)S(1)} %get-tuple-element.105.right_ref.ffn_ref.refs_0_, bf16[1024,4096]{1,0:T(8,128)(2,1)} %copy-done, ...), custom_call_target="tpu_custom_call", output_to_operand_aliasing={{0}: (5, {}), {1}: (6, {})} | custom-call | flops 9663676416 | bytes 23068672 | tf_op jit(solution)/shard_map/narrow/pallas_call | solution.py:69
  1119.3 17.0 %outer_wide.2 = (bf16[16,32,3072]{2,1,0:T(8,128)(2,1)S(1)}, bf16[16,32,3072]{2,1,0:T(8,128)(2,1)S(1)}, bf16[16,32,2048]{2,1,0:T(8,128)(2,1)S(1)}, bf16[16,32,2048]{2,1,0:T(8,128)(2,1)}) custom-call(bf16[1024,1024]{1,0:T(8,128)(2,1)S(1)} %copy-done.33, bf16[1024,1024]{1,0:T(8,128)(2,1)S(1)} %copy-done.38, bf16[1024,4096]{1,0:T(8,128)(2,1)} %get-tuple-element.123.refs_2_, ...), custom_call_target="tpu_custom_call" | custom-call | flops 10737418240 | bytes 25165824 | tf_op jit(solution)/shard_map/outer_wide/pallas_call | solution.py:419
  1142.8 6.7 collective-permute-done.48
  1180.7 14.5 %attend_back.2 = (bf16[1024,1024]{1,0:T(8,128)(2,1)S(1)}, bf16[1024,1024]{1,0:T(8,128)(2,1)S(1)}, bf16[1024,1024]{1,0:T(8,128)(2,1)S(1)}) custom-call(bf16[1024,1024]{1,0:T(8,128)(2,1)S(1)} %copy-done.44, bf16[1024,1024]{1,0:T(8,128)(2,1)S(1)} %copy-done.31, bf16[1024,1024]{1,0:T(8,128)(2,1)S(1)} %copy-done.41, ...), custom_call_target="tpu_custom_call" | custom-call | flops 12884901888 | bytes 15728640 | tf_op jit(solution)/shard_map/attend_back/pallas_call | solution.py:69
  1203.3 14.2 %attend_back.3 = (bf16[1024,1024]{1,0:T(8,128)(2,1)S(1)}, bf16[1024,1024]{1,0:T(8,128)(2,1)S(1)}, bf16[1024,1024]{1,0:T(8,128)(2,1)S(1)}) custom-call(bf16[1024,1024]{1,0:T(8,128)(2,1)S(1)} %copy-done.44, bf16[1024,1024]{1,0:T(8,128)(2,1)S(1)} %copy-done.31, ...), custom_call_target="tpu_custom_call", output_to_operand_aliasing={{0}: (5, {}), {1}: (6, {}), {2}: (7, {})} | custom-call | flops 12884901888 | bytes 15728640 | tf_op jit(solution)/shard_map/attend_back/pallas_call | solution.py:69
  1232.4 9.6 outer_wide.3
  1247.4 6.6 collective-permute-done.71
  1294.7 10.4 collective-permute-done.70
  1308.4 8.1 collective-permute-done.75
  1318.4 7.2 collective-permute-done.76
  (424 shorter events, 313.2 us)
Async XLA Ops:
  42.8 55.7 %collective-permute-start.11 = (bf16[8,32,1152]{2,1,0:T(8,128)(2,1)S(1)}, bf16[8,32,1152]{2,1,0:T(8,128)(2,1)S(1)}, u32[]{:S(2)}, u32[]{:S(2)}) collective-permute-start(bf16[8,32,1152]{2,1,0:T(8,128)(2,1)S(1)} %constant_dynamic-update-slice_fusion.5.refs_4_), channel_id=1, source_target_pairs={{0,4},{1,5},{2,6},{3,7},{4,0},{5,1},{6,2},{7,3},{8,12},{9,13},{10,... | collective-permute-start | bytes 1769480 | tf_op jit(solution)/shard_map/ppermute | solution.py:445
  59.2 31.2 %collective-permute-start.4 = (bf16[8,32,2048]{2,1,0:T(8,128)(2,1)S(1)}, bf16[8,32,2048]{2,1,0:T(8,128)(2,1)S(1)}, u32[]{:S(2)}, u32[]{:S(2)}) collective-permute-start(bf16[8,32,2048]{2,1,0:T(8,128)(2,1)S(1)} %constant_dynamic-update-slice_fusion.refs_0_), channel_id=1, source_target_pairs={{0,2},{1,3},{2,0},{3,1},{4,6},{5,7},{6,4},{7,5},{8,10},{9,11},{10,... | collective-permute-start | bytes 3145736 | tf_op jit(solution)/shard_map/ppermute | solution.py:445
  63.4 37.3 %collective-permute-start.17 = (bf16[4,32,3328]{2,1,0:T(8,128)(2,1)S(1)}, bf16[4,32,3328]{2,1,0:T(8,128)(2,1)S(1)}, u32[]{:S(2)}, u32[]{:S(2)}) collective-permute-start(bf16[4,32,3328]{2,1,0:T(8,128)(2,1)S(1)} %pad_maximum_fusion.1), channel_id=1, source_target_pairs={{0,4},{1,5},{2,6},{3,7},{4,0},{5,1},{6,2},{7,3},{8,12},{9,13},{10,... | collective-permute-start | bytes 2555912 | tf_op jit(solution)/shard_map/ppermute | solution.py:445
  88.2 28.6 %collective-permute-start.5 = (bf16[8,32,2048]{2,1,0:T(8,128)(2,1)S(1)}, bf16[8,32,2048]{2,1,0:T(8,128)(2,1)S(1)}, u32[]{:S(2)}, u32[]{:S(2)}) collective-permute-start(bf16[8,32,2048]{2,1,0:T(8,128)(2,1)S(1)} %constant_dynamic-update-slice_fusion.refs_0_), channel_id=1, source_target_pairs={{0,1},{1,0},{2,3},{3,2},{4,5},{5,4},{6,7},{7,6},{8,9},{9,8},{10,11... | collective-permute-start | bytes 3145736 | tf_op jit(solution)/shard_map/ppermute | solution.py:445
  90.4 26.4 %collective-permute-start.6 = (bf16[8,32,2048]{2,1,0:T(8,128)(2,1)S(1)}, bf16[8,32,2048]{2,1,0:T(8,128)(2,1)S(1)}, u32[]{:S(2)}, u32[]{:S(2)}) collective-permute-start(bf16[8,32,2048]{2,1,0:T(8,128)(2,1)S(1)} %collective-permute-done.4.refs_1_), channel_id=1, source_target_pairs={{0,1},{1,0},{2,3},{3,2},{4,5},{5,4},{6,7},{7,6},{8,9},{9,8},{10,11... | collective-permute-start | bytes 3145736 | tf_op jit(solution)/shard_map/ppermute | solution.py:445
  113.2 217.7 %collective-permute-start.25 = (bf16[8,32,1792]{2,1,0:T(8,128)(2,1)}, bf16[8,32,1792]{2,1,0:T(8,128)(2,1)}, u32[]{:S(2)}, u32[]{:S(2)}) collective-permute-start(bf16[8,32,1792]{2,1,0:T(8,128)(2,1)} %constant_dynamic-update-slice_fusion.15.refs_4_), channel_id=1, source_target_pairs={{0,4},{1,5},{2,6},{3,7},{4,0},{5,1},{6,2},{7,3},{8,12},{9,13},{10,... | collective-permute-start | bytes 2752520 | tf_op jit(solution)/shard_map/ppermute | solution.py:445
  114.8 216.7 %collective-permute-start.18 = (bf16[8,32,3328]{2,1,0:T(8,128)(2,1)}, bf16[8,32,3328]{2,1,0:T(8,128)(2,1)}, u32[]{:S(2)}, u32[]{:S(2)}) collective-permute-start(bf16[8,32,3328]{2,1,0:T(8,128)(2,1)} %constant_dynamic-update-slice_fusion.10.refs_0_), channel_id=1, source_target_pairs={{0,2},{1,3},{2,0},{3,1},{4,6},{5,7},{6,4},{7,5},{8,10},{9,11},{10,... | collective-permute-start | bytes 5111816 | tf_op jit(solution)/shard_map/ppermute | solution.py:445
  115.4 215.5 %collective-permute-start.39 = (bf16[8,128,384]{2,1,0:T(8,128)(2,1)}, bf16[8,128,384]{2,1,0:T(8,128)(2,1)}, u32[]{:S(2)}, u32[]{:S(2)}) collective-permute-start(bf16[8,128,384]{2,1,0:T(8,128)(2,1)} %constant_dynamic-update-slice_fusion.25.refs_4_), channel_id=1, source_target_pairs={{0,4},{1,5},{2,6},{3,7},{4,0},{5,1},{6,2},{7,3},{8,12},{9,13},{10,... | collective-permute-start | bytes 2359304 | tf_op jit(solution)/shard_map/ppermute | solution.py:445
  116.8 214.7 %collective-permute-start.40 = (bf16[8,128,384]{2,1,0:T(8,128)(2,1)}, bf16[8,128,384]{2,1,0:T(8,128)(2,1)}, u32[]{:S(2)}, u32[]{:S(2)}) collective-permute-start(bf16[8,128,384]{2,1,0:T(8,128)(2,1)} %constant_dynamic-update-slice_fusion.25.refs_4_), channel_id=1, source_target_pairs={{0,1},{1,0},{2,3},{3,2},{4,5},{5,4},{6,7},{7,6},{8,9},{9,8},{10,11... | collective-permute-start | bytes 2359304 | tf_op jit(solution)/shard_map/ppermute | solution.py:445
  118.8 228.9 %collective-permute-start.32 = (bf16[8,128,640]{2,1,0:T(8,128)(2,1)S(1)}, bf16[8,128,640]{2,1,0:T(8,128)(2,1)}, u32[]{:S(2)}, u32[]{:S(2)}) collective-permute-start(bf16[8,128,640]{2,1,0:T(8,128)(2,1)S(1)} %constant_dynamic-update-slice_fusion.20.refs_0_), channel_id=1, source_target_pairs={{0,2},{1,3},{2,0},{3,1},{4,6},{5,7},{6,4},{7,5},{8,10},{9,11},{10,... | collective-permute-start | bytes 3932168 | tf_op jit(solution)/shard_map/ppermute | solution.py:445
  330.9 295.6 %collective-permute-start.19 = (bf16[8,32,3328]{2,1,0:T(8,128)(2,1)}, bf16[8,32,3328]{2,1,0:T(8,128)(2,1)S(1)}, u32[]{:S(2)}, u32[]{:S(2)}) collective-permute-start(bf16[8,32,3328]{2,1,0:T(8,128)(2,1)} %constant_dynamic-update-slice_fusion.10.refs_0_), channel_id=1, source_target_pairs={{0,1},{1,0},{2,3},{3,2},{4,5},{5,4},{6,7},{7,6},{8,9},{9,8},{10,11... | collective-permute-start | bytes 5111816 | tf_op jit(solution)/shard_map/ppermute | solution.py:445
  331.6 294.9 %collective-permute-start.20 = (bf16[8,32,3328]{2,1,0:T(8,128)(2,1)}, bf16[8,32,3328]{2,1,0:T(8,128)(2,1)}, u32[]{:S(2)}, u32[]{:S(2)}) collective-permute-start(bf16[8,32,3328]{2,1,0:T(8,128)(2,1)} %collective-permute-done.18.refs_1_), channel_id=1, source_target_pairs={{0,1},{1,0},{2,3},{3,2},{4,5},{5,4},{6,7},{7,6},{8,9},{9,8},{10,11... | collective-permute-start | bytes 5111816 | tf_op jit(solution)/shard_map/ppermute | solution.py:445
  347.7 23.5 %collective-permute-start.34 = (bf16[8,128,640]{2,1,0:T(8,128)(2,1)}, bf16[8,128,640]{2,1,0:T(8,128)(2,1)}, u32[]{:S(2)}, u32[]{:S(2)}) collective-permute-start(bf16[8,128,640]{2,1,0:T(8,128)(2,1)} %collective-permute-done.32.refs_1_), channel_id=1, source_target_pairs={{0,1},{1,0},{2,3},{3,2},{4,5},{5,4},{6,7},{7,6},{8,9},{9,8},{10,11... | collective-permute-start | bytes 3932168 | tf_op jit(solution)/shard_map/ppermute | solution.py:445
  349.0 277.4 %collective-permute-start.26 = (bf16[8,32,1792]{2,1,0:T(8,128)(2,1)}, bf16[8,32,1792]{2,1,0:T(8,128)(2,1)S(1)}, u32[]{:S(2)}, u32[]{:S(2)}) collective-permute-start(bf16[8,32,1792]{2,1,0:T(8,128)(2,1)} %constant_dynamic-update-slice_fusion.15.refs_4_), channel_id=1, source_target_pairs={{0,1},{1,0},{2,3},{3,2},{4,5},{5,4},{6,7},{7,6},{8,9},{9,8},{10,11... | collective-permute-start | bytes 2752520 | tf_op jit(solution)/shard_map/ppermute | solution.py:445
  349.5 277.0 %collective-permute-start.27 = (bf16[8,32,1792]{2,1,0:T(8,128)(2,1)}, bf16[8,32,1792]{2,1,0:T(8,128)(2,1)}, u32[]{:S(2)}, u32[]{:S(2)}) collective-permute-start(bf16[8,32,1792]{2,1,0:T(8,128)(2,1)} %collective-permute-done.25.refs_5_), channel_id=1, source_target_pairs={{0,1},{1,0},{2,3},{3,2},{4,5},{5,4},{6,7},{7,6},{8,9},{9,8},{10,11... | collective-permute-start | bytes 2752520 | tf_op jit(solution)/shard_map/ppermute | solution.py:445
  1032.6 42.5 %collective-permute-start.42 = (bf16[16,128,640]{2,1,0:T(8,128)(2,1)}, bf16[16,128,640]{2,1,0:T(8,128)(2,1)}, u32[]{:S(2)}, u32[]{:S(2)}) collective-permute-start(bf16[16,128,640]{2,1,0:T(8,128)(2,1)} %get-tuple-element.103), channel_id=1, source_target_pairs={{0,1},{1,0},{2,3},{3,2},{4,5},{5,4},{6,7},{7,6},{8,9},{9,8},{10,11... | collective-permute-start | bytes 7864328 | tf_op jit(solution)/shard_map/ppermute | solution.py:445
  1077.9 37.9 %collective-permute-start.45 = (bf16[4,2,128,640]{3,2,1,0:T(8,128)(2,1)}, bf16[4,2,128,640]{3,2,1,0:T(8,128)(2,1)}, u32[]{:S(2)}, u32[]{:S(2)}) collective-permute-start(bf16[4,2,128,640]{3,2,1,0:T(8,128)(2,1)} %fusion.5), channel_id=1, source_target_pairs={{0,2},{1,3},{2,0},{3,1},{4,6},{5,7},{6,4},{7,5},{8,10},{9,11},{10,... | collective-permute-start | bytes 3932168 | tf_op jit(solution)/shard_map/ppermute | solution.py:445
  1139.3 36.0 %collective-permute-start.50 = (bf16[16,32,2048]{2,1,0:T(8,128)(2,1)}, bf16[16,32,2048]{2,1,0:T(8,128)(2,1)}, u32[]{:S(2)}, u32[]{:S(2)}) collective-permute-start(bf16[16,32,2048]{2,1,0:T(8,128)(2,1)} %get-tuple-element.127), channel_id=1, source_target_pairs={{0,1},{1,0},{2,3},{3,2},{4,5},{5,4},{6,7},{7,6},{8,9},{9,8},{10,11... | collective-permute-start | bytes 6291464 | tf_op jit(solution)/shard_map/ppermute | solution.py:445
  1142.8 54.3 %collective-permute-start.49 = (bf16[16,32,3072]{2,1,0:T(8,128)(2,1)}, bf16[16,32,3072]{2,1,0:T(8,128)(2,1)}, u32[]{:S(2)}, u32[]{:S(2)}) collective-permute-start(bf16[16,32,3072]{2,1,0:T(8,128)(2,1)} %copy-done.12), channel_id=1, source_target_pairs={{0,1},{1,0},{2,3},{3,2},{4,5},{5,4},{6,7},{7,6},{8,9},{9,8},{10,11... | collective-permute-start | bytes 9437192 | tf_op jit(solution)/shard_map/ppermute | solution.py:445
  1200.2 76.2 %collective-permute-start.59 = (bf16[4,2,32,3072]{3,2,1,0:T(8,128)(2,1)}, bf16[4,2,32,3072]{3,2,1,0:T(8,128)(2,1)}, u32[]{:S(2)}, u32[]{:S(2)}) collective-permute-start(bf16[4,2,32,3072]{3,2,1,0:T(8,128)(2,1)} %fusion.2), channel_id=1, source_target_pairs={{0,2},{1,3},{2,0},{3,1},{4,6},{5,7},{6,4},{7,5},{8,10},{9,11},{10,... | collective-permute-start | bytes 4718600 | tf_op jit(solution)/shard_map/ppermute | solution.py:445
  1202.3 40.5 %collective-permute-start.60 = (bf16[2,32,2048]{2,1,0:T(8,128)(2,1)}, bf16[2,32,2048]{2,1,0:T(8,128)(2,1)}, u32[]{:S(2)}, u32[]{:S(2)}) collective-permute-start(bf16[2,32,2048]{2,1,0:T(8,128)(2,1)} %get-tuple-element.166), channel_id=1, source_target_pairs={{0,8},{1,9},{2,10},{3,11},{4,12},{5,13},{6,14},{7,15},{8,16},{9,17... | collective-permute-start | bytes 786440 | tf_op jit(solution)/shard_map/ppermute | solution.py:444
  1242.3 40.8 %collective-permute-start.57 = (bf16[16,32,2048]{2,1,0:T(8,128)(2,1)S(1)}, bf16[16,32,2048]{2,1,0:T(8,128)(2,1)S(1)}, u32[]{:S(2)}, u32[]{:S(2)}) collective-permute-start(bf16[16,32,2048]{2,1,0:T(8,128)(2,1)S(1)} %get-tuple-element.139), channel_id=1, source_target_pairs={{0,1},{1,0},{2,3},{3,2},{4,5},{5,4},{6,7},{7,6},{8,9},{9,8},{10,11... | collective-permute-start | bytes 6291464 | tf_op jit(solution)/shard_map/ppermute | solution.py:445
  1278.4 28.5 %collective-permute-start.74 = (bf16[4,32,3072]{2,1,0:T(8,128)(2,1)S(1)}, bf16[4,32,3072]{2,1,0:T(8,128)(2,1)S(1)}, u32[]{:S(2)}, u32[]{:S(2)}) collective-permute-start(bf16[4,32,3072]{2,1,0:T(8,128)(2,1)S(1)} %get-tuple-element.158), channel_id=1, source_target_pairs={{0,4},{1,5},{2,6},{3,7},{4,0},{5,1},{6,2},{7,3},{8,12},{9,13},{10,... | collective-permute-start | bytes 2359304 | tf_op jit(solution)/shard_map/ppermute | solution.py:445
  1283.5 23.5 %collective-permute-start.61 = (bf16[4,2,32,2048]{3,2,1,0:T(8,128)(2,1)S(1)}, bf16[4,2,32,2048]{3,2,1,0:T(8,128)(2,1)S(1)}, u32[]{:S(2)}, u32[]{:S(2)}) collective-permute-start(bf16[4,2,32,2048]{3,2,1,0:T(8,128)(2,1)S(1)} %fusion.9), channel_id=1, source_target_pairs={{0,2},{1,3},{2,0},{3,1},{4,6},{5,7},{6,4},{7,5},{8,10},{9,11},{10,... | collective-permute-start | bytes 3145736 | tf_op jit(solution)/shard_map/ppermute | solution.py:445
  (127 other events, 1461.6 us)

commit v3 on v2

--- a/solution.py
+++ b/solution.py
@@ -294,17 +294,17 @@
     strips(ffn_ref.shape[0], strip)
 
 
-def narrow(d_ffn, slope, w_down, w_up, so_far, first, last, before=()):
-    rows, width = slope.shape
+def narrow(d_ffn, slope, w_down, w_up, so_far, first, last):
+    rows, width = slope.shape[0], WIDE * (last - first)
+    own = lambda height: pl.BlockSpec((height, WIDE), lambda i: (0, i))
     chunk = lambda height: pl.BlockSpec((height, WIDE), lambda i: (0, i + first))
-    return continued(
+    return pl.pallas_call(
         narrow_kernel,
-        before,
         grid=(last - first,),
         in_specs=[
             fixed(d_ffn), chunk(rows), pl.BlockSpec((WIDE, D), lambda i: (i + first, 0)), chunk(D), fixed(so_far),
         ],
-        out_specs=[chunk(rows), chunk(1), held(rows, D)],
+        out_specs=[own(rows), own(1), held(rows, D)],
         out_shape=[
             jax.ShapeDtypeStruct((rows, width), LOW), jax.ShapeDtypeStruct((1, width), FULL),
             jax.ShapeDtypeStruct((rows, D), FULL),
@@ -384,7 +384,7 @@
     )(left, right)
 
 
-def wide_kernel(starts, first, *refs):
+def wide_kernel(starts, cuts, *refs):
     pairs = len(starts) - 1
     lefts, rights, outs, product = refs[:pairs], refs[pairs : 2 * pairs], refs[2 * pairs : -1], refs[-1]
     step = pl.program_id(0)
@@ -394,14 +394,14 @@
         def _():
             product[...] = dot_tn(left[...], right[...]).astype(LOW).reshape(product.shape)
 
-    for keep, send, wanted in ((outs[0], outs[1], step < first), (outs[2], outs[3], step >= first)):
-        @pl.when(wanted)
+    for keep, send, low, high in zip(outs[::2], outs[1::2], cuts, cuts[1:]):
+        @pl.when((step >= low) & (step < high))
         def _():
             keep[...] = product[:, core]
             send[...] = product[:, 1 - core]
 
 
-def outer_wide(lefts, rights, first, count):
+def outer_wide(lefts, rights, cuts, count):
     rows, height = lefts[0].shape
     part = height // count
     starts = [0]
@@ -415,9 +415,9 @@
     def out(low, high):
         return pl.BlockSpec((count // 2, part, WIDE), lambda i: (0, 0, jnp.clip(i - low, 0, high - low - 1)))
 
-    ranges = ((0, first), (0, first), (first, total), (first, total))
+    ranges = [part_range for part_range in zip(cuts, cuts[1:]) for _ in range(2)]
     return pl.pallas_call(
-        functools.partial(wide_kernel, starts, first),
+        functools.partial(wide_kernel, starts, cuts),
         grid=(total,),
         in_specs=[fixed(left) for left in lefts] + [strip(low, high) for low, high in zip(starts, starts[1:])],
         out_specs=[out(low, high) for low, high in ranges],
@@ -432,7 +432,9 @@
 
 
 FLIPS = {"c": 1, "x": 2, "y": 4}
-ORDERS = ("zyx", "xzy")
+TWO_WAYS = ("zyx", "xzy")
+EARLY_WAYS = ("zyx", "xzy", "yzx")
+THREE_WAYS = ("zyx", "xzy", "yxz")
 
 
 def ring_pairs(count):
@@ -446,82 +448,106 @@
 
 
 def after(value, *earlier):
-    return lax.optimization_barrier((value, earlier))[0]
-
-
-def mine_of(count):
+    return lax.optimization_barrier((value, earlier))[0] if earlier else value
+
+
+def mine_of():
     me = lax.axis_index("dp")
-    return {"z": lax.shift_right_logical(me, 3), "y": lax.shift_right_logical(me, 2) & 1,
-            "x": lax.shift_right_logical(me, 1) & 1, "c": me & 1}
-
-
-def gather_part(shard, order, count, marks):
-    stack = after(shard, marks[-1])[None] if marks else shard[None]
-    for dim in order[:2]:
+    return {
+        "z": lax.shift_right_logical(me, 3),
+        "y": lax.shift_right_logical(me, 2) & 1,
+        "x": lax.shift_right_logical(me, 1) & 1,
+        "c": me & 1,
+    }
+
+
+def gather_part(shard, order, count, first=(), second=(), third=()):
+    stack = shard[None]
+    mark = None
+    for dim, earlier in zip(order[:2], (first, second)):
+        stack = after(stack, *earlier)
         pieces = [stack]
         for _ in range(count // 8 - 1 if dim == "z" else 1):
             pieces.append(hop(pieces[-1], dim, count))
         stack = jnp.concatenate(pieces, axis=0)
         if dim == "z":
-            marks.append(pieces[-1])
-    across = hop(stack, order[2], count)
-    return (stack, across, hop(stack, "c", count), hop(across, "c", count))
-
-
-def place_kernel(count, cuts, bases, rows, *refs):
-    pieces, outs, sem = refs[:8], refs[8:-1], refs[-1]
+            mark = pieces[-1]
+    across = hop(after(stack, *third), order[2], count)
+    return (stack, across, hop(stack, "c", count), hop(across, "c", count)), mark
+
+
+def place_kernel(count, orders, cuts, bases, rows, *refs):
+    pieces, outs = refs[: 4 * len(orders)], refs[4 * len(orders) :]
     ring = count // 8
-    mine = mine_of(count)
-
-    def owner(digits):
-        z = lax.rem(mine["z"] + ring - digits["z"], ring)
-        low = [1 - mine[dim] if digits[dim] else mine[dim] for dim in "yxc"]
-        return z * 8 + low[0] * 4 + low[1] * 2 + low[2]
-
-    for part, order in enumerate(ORDERS):
+    mine = mine_of()
+    slot = pl.program_id(0)
+    for part, order in enumerate(orders):
         left, right = cuts[part], cuts[part + 1]
         for which in range(4):
-            for slot in range(count // 4):
-                digits = {"c": which // 2, order[2]: which % 2}
-                rest = slot
-                for dim in order[:2]:
-                    size = ring if dim == "z" else 2
-                    digits[dim] = rest % size
-                    rest = rest // size
-                row = pl.ds(pl.multiple_of(owner(digits) * rows, rows), rows)
-                for out, base, stop in zip(outs, bases, bases[1:]):
-                    low, high = max(left, base), min(right, stop)
-                    if low < high:
-                        pltpu.make_async_copy(
-                            pieces[4 * part + which].at[slot, :, pl.ds(low - left, high - low)],
-                            out.at[row, pl.ds(low - base, high - low)],
-                            sem,
-                        ).start()
-    for out in outs:
-        pltpu.make_async_copy(out, out, sem).wait()
-
-
-def gather(shard, widths, cut, count, marks):
-    rows, total = shard.shape
+            digits = {"c": which // 2, order[2]: which % 2}
+            rest = slot
+            for dim in order[:2]:
+                size = ring if dim == "z" else 2
+                digits[dim] = lax.rem(rest, size)
+                rest = lax.div(rest, size)
+            owner = lax.rem(mine["z"] + ring - digits["z"], ring) * 8
+            for dim, weight in (("y", 4), ("x", 2), ("c", 1)):
+                owner = owner + weight * (mine[dim] ^ digits[dim])
+            row = pl.ds(pl.multiple_of(owner * rows, rows), rows)
+            for out, base, stop in zip(outs, bases, bases[1:]):
+                low, high = max(left, base), min(right, stop)
+                if low < high:
+                    out[row, low - base : high - base] = pieces[4 * part + which][0, :, low - left : high - left]
+
+
+def place(pieces, orders, cuts, widths, rows, count):
     bases = [sum(widths[:index]) for index in range(len(widths) + 1)]
-    if count != 32:
-        full = lax.all_gather(shard, "dp", axis=0, tiled=True)
-        return [full[:, low:high] for low, high in zip(bases, bases[1:])]
-    cuts = (0, cut, total)
-    pieces = []
-    for order, low, high, own_marks in zip(ORDERS, cuts, cuts[1:], marks):
-        pieces.extend(gather_part(shard[:, low:high], order, count, own_marks))
+    size = count * rows
     return pl.pallas_call(
-        functools.partial(place_kernel, count, cuts, bases, rows),
-        in_specs=[pl.BlockSpec(memory_space=pl.ANY)] * 8,
-        out_specs=[pl.BlockSpec(memory_space=pl.ANY)] * len(widths),
-        out_shape=[jax.ShapeDtypeStruct((count * rows, width), LOW) for width in widths],
-        scratch_shapes=[pltpu.SemaphoreType.DMA(())],
-        cost_estimate=pl.CostEstimate(flops=0, bytes_accessed=4 * count * rows * total, transcendentals=0),
+        functools.partial(place_kernel, count, orders, cuts, bases, rows),
+        grid=(count // 4,),
+        in_specs=[pl.BlockSpec((1, rows, piece.shape[2]), lambda i: (i, 0, 0)) for piece in pieces],
+        out_specs=[held(size, width) for width in widths],
+        out_shape=[jax.ShapeDtypeStruct((size, width), LOW) for width in widths],
+        compiler_params=pltpu.CompilerParams(vmem_limit_bytes=32 * MIB),
+        cost_estimate=pl.CostEstimate(flops=0, bytes_accessed=4 * size * bases[-1], transcendentals=0),
         name="place",
     )(*pieces)
 
 
+def whole_arrays(shard, widths):
+    full = lax.all_gather(shard, "dp", axis=0, tiled=True)
+    bases = [sum(widths[:index]) for index in range(len(widths) + 1)]
+    return [full[:, low:high] for low, high in zip(bases, bases[1:])]
+
+
+def gather_all(first, second, third, wide, count):
+    first_widths, second_widths, third_widths = (D, D, D, 128), (wide, D), (D,)
+    if count != 32:
+        return whole_arrays(first, first_widths) + whole_arrays(second, second_widths) + whole_arrays(third, third_widths)
+
+    def pieces_of(shard, cuts, orders, ties):
+        pieces, marks = [], []
+        for order, low, high, tie in zip(orders, cuts, cuts[1:], ties):
+            four, mark = gather_part(shard[:, low:high], order, count, *tie)
+            pieces.append(four)
+            marks.append(mark)
+        return pieces, marks
+
+    cuts = (0, D, 2 * D, 3 * D + 128)
+    early, marks = pieces_of(first, cuts, EARLY_WAYS, [()] * 3)
+    placed_first = place(sum(early, ()), EARLY_WAYS, cuts, first_widths, first.shape[0], count)
+    cuts = (0, 3328, wide + D)
+    ties = [((marks[0],), (early[0][1],)), ((marks[1],), (), (early[1][1],))]
+    pieces, _ = pieces_of(second, cuts, TWO_WAYS, ties)
+    placed_second = place(sum(pieces, ()), TWO_WAYS, cuts, second_widths, second.shape[0], count)
+    cuts = (0, 640, D)
+    ties = [((placed_first[0],),), ((placed_first[0],),)]
+    pieces, _ = pieces_of(third, cuts, TWO_WAYS, ties)
+    placed_third = place(sum(pieces, ()), TWO_WAYS, cuts, third_widths, third.shape[0], count)
+    return list(placed_first) + list(placed_second) + list(placed_third)
+
+
 def add_low(left_side, right_side, kind=LOW):
     return (left_side.astype(FULL) + right_side.astype(FULL)).astype(kind)
 
@@ -532,48 +558,53 @@
 
 def scatter_steps(keep, send, order, count):
     ring = count // 8
-    mine = mine_of(count)
+    mine = mine_of()
     dims = ["z", "y", "x"]
     shape = (ring, 2, 2) + keep.shape[1:]
-    yield send
-    held = [keep.reshape(shape), hop(send, "c", count).reshape(shape)]
+
+    def hopped(array, dim, gate):
+        return after(hop(array, dim, count), *gate)
+
+    gate = yield send
+    held_sums = [keep.reshape(shape), hopped(send, "c", gate).reshape(shape)]
 
     def pick(dim, index):
         axis = dims.index(dim)
-        return add_low(take(held[0], axis, index), take(held[1], axis, index))
+        return add_low(take(held_sums[0], axis, index), take(held_sums[1], axis, index))
 
     for dim in order[::-1]:
         own = mine[dim]
         if dim == "z":
             moving = pick("z", (own + ring - 1) & (ring - 1))
             for step in range(2, ring + 1):
-                yield moving
-                moving = hop(moving, "z", count)
+                gate = yield moving
+                moving = hopped(moving, "z", gate)
                 if step < ring:
                     moving = add_low(moving, pick("z", (own + ring - step) & (ring - 1)))
         else:
             moving = pick(dim, 1 - own)
-            yield moving
-            moving = hop(moving, dim, count)
-        held = [pick(dim, own), moving]
+            gate = yield moving
+            moving = hopped(moving, dim, gate)
+        held_sums = [pick(dim, own), moving]
         dims.remove(dim)
-    yield add_low(held[0], held[1], FULL)
+    yield add_low(held_sums[0], held_sums[1], FULL)
 
 
 class Sums:
-    def __init__(self, parts, count):
-        self.chains = [scatter_steps(keep, send, order, count) for (keep, send), order in zip(parts, ORDERS)]
-        self.last = [None] * len(parts)
-
-    def move(self, which):
-        self.last[which] = next(self.chains[which])
+    def __init__(self, parts, orders, count):
+        pairs = zip(parts[::2], parts[1::2])
+        self.chains = [scatter_steps(keep, send, order, count) for (keep, send), order in zip(pairs, orders)]
+        self.last = [next(chain) for chain in self.chains]
+
+    def move(self, which, *gate):
+        self.last[which] = self.chains[which].send(gate)
         return self.last[which]
 
-    def result(self):
+    def results(self):
         for which, chain in enumerate(self.chains):
-            for value in chain:
-                self.last[which] = value
-        return jnp.concatenate(self.last, axis=-1)
+            while self.last[which].dtype != FULL:
+                self.move(which)
+        return self.last
 
 
 def local(
@@ -601,12 +632,13 @@
     vectors = (b_query, b_value, b_out, b_down, gain_attn, shift_attn, gain_ffn, shift_ffn, b_up)
     packed = jnp.concatenate(vectors)
     packed = jnp.pad(packed, (0, part * 128 - packed.shape[0])).reshape(part, 128)
-    marks = ([], [])
-    w_query, w_key, w_value, packed = gather(
-        jnp.concatenate([w_query, w_key, w_value, packed], axis=1), (D, D, D, 128), 2 * D, count, marks
+    w_query, w_key, w_value, packed, w_up, w_out, w_down = gather_all(
+        jnp.concatenate([w_query, w_key, w_value, packed], axis=1),
+        jnp.concatenate([w_up, w_out], axis=1),
+        w_down,
+        wide,
+        count,
     )
-    w_up, w_out = gather(jnp.concatenate([w_up, w_out], axis=1), (wide, D), 3328, count, marks)
-    (w_down,) = gather(w_down, (D,), 640, count, marks)
     flat = packed.reshape(count, part * 128)
     vector = lambda col: flat[:, part * col : part * col + part].reshape(1, D).astype(FULL)
     b_query, b_value, b_out, b_down, gain_attn, shift_attn, gain_ffn, shift_ffn = map(vector, range(8))
@@ -629,73 +661,86 @@
     )
 
     custom = count == 32
-    down, up, first = None, None, None
-
-    def then(value, *moves):
+
+    def then(value, gate, *moves):
         if not custom:
             return value
-        return after(value, *[sums.move(which) for sums, which in moves])
+        return after(value, *[sums.move(which, gate) for sums, which in moves])
 
     if custom:
-        parts = outer_tall(hidden, d_ffn, 640, count)
-        down = Sums((parts[:2], parts[2:]), count)
-    d_ffn = then(d_ffn, (down, 0), (down, 1))
-    d_pre, d_b_up, d_first = narrow(d_ffn, slope, w_down, w_up, second, 0, 2)
-    d_first = then(d_first, (down, 0), (down, 1))
-    d_pre, d_b_up, d_first = narrow(d_ffn, slope, w_down, w_up, d_first, 2, 5, (d_pre, d_b_up, d_first)[:2])
-    d_first = then(d_first, (down, 1))
-    d_pre, d_b_up, d_first = narrow(d_ffn, slope, w_down, w_up, d_first, 5, chunks, (d_pre, d_b_up, d_first)[:2])
+        down = Sums(outer_tall(hidden, d_ffn, 640, count), TWO_WAYS, count)
+        second = after(second, *down.last)
+    pre_1, wide_1, d_first = narrow(d_ffn, slope, w_down, w_up, second, 0, 2)
+    d_first = then(d_first, wide_1, (down, 0), (down, 1)) if custom else d_first
+    pre_2, wide_2, d_first = narrow(d_ffn, slope, w_down, w_up, d_first, 2, 5)
+    if custom:
+        parts = outer_wide([first_low, first_low], [pre_1, pre_2], (0, 3, 5), count)
+        up_1 = Sums(parts, TWO_WAYS, count)
+        d_first = after(then(d_first, parts[2], (down, 1)), *up_1.last)
+    pre_3, wide_3, d_first = narrow(d_ffn, slope, w_down, w_up, d_first, 5, chunks)
+    if custom:
+        d_first = then(d_first, wide_3, (down, 0), (down, 1), (up_1, 0), (up_1, 1))
     d_resid, d_branch, d_attn, sums_attn = resid_back(d_first, normed, inverse, gain_attn, w_out)
-    d_branch = then(d_branch, (down, 0), (down, 1))
     if custom:
-        parts = outer_wide([first_low, attn_rows], [d_pre, d_branch], 6, count)
-        up = Sums((parts[:2], parts[2:]), count)
-    d_attn = then(d_attn, (down, 0), (down, 1), (up, 0), (up, 1))
+        d_branch = then(d_branch, sums_attn, (down, 1))
+        parts = outer_wide([first_low, attn_rows], [pre_3, d_branch], (0, 3, 5), count)
+        up_2 = Sums(parts, TWO_WAYS, count)
+        d_attn = after(then(d_attn, parts[2], (down, 0), (down, 1)), *up_2.last)
     seen = attend_back(queries, keys, values, probs, d_attn, 0)
-    d_attn = then(d_attn, (up, 0), (up, 1), (down, 0), (down, 1))
+    if custom:
+        d_attn = then(
+            d_attn, seen[0], (down, 0), (down, 1), (up_1, 0), (up_1, 1), (up_2, 0), (up_2, 1)
+        )
     for sequence in range(1, sequences):
         seen = attend_back(queries, keys, values, probs, d_attn, sequence, seen)
     d_queries, d_keys, d_values = seen
-    d_queries = then(d_queries, (down, 0), (down, 1))
+    if custom:
+        d_queries = then(d_queries, d_values, (down, 0), (up_1, 0), (up_1, 1), (up_2, 1))
     column_sum = lambda rows: jnp.sum(rows.astype(FULL), axis=0)
     sums = (
         column_sum(d_queries), column_sum(d_values), sums_attn[2], sums_ffn[2],
-        sums_attn[0], sums_attn[1], sums_ffn[0], sums_ffn[1], d_b_up[0],
+        sums_attn[0], sums_attn[1], sums_ffn[0], sums_ffn[1],
+        jnp.concatenate([wide_1[0], wide_2[0], wide_3[0]]),
     )
     packed = jnp.concatenate([total.astype(LOW).reshape(count, -1) for total in sums], axis=1)
     packed = jnp.pad(packed, ((0, 0), (0, part * 128 - packed.shape[1]))).reshape(count // 2, 2, part, 128)
     if custom:
-        parts = outer_wide([tokens, tokens, tokens], [d_queries, d_keys, d_values], 4, count)
-        send = jnp.concatenate([parts[3], take(packed, 1, 1 - mine_of(count)["c"])], axis=-1)
-        keep = jnp.concatenate([parts[2], take(packed, 1, mine_of(count)["c"])], axis=-1)
-        first = Sums((parts[:2], (keep, send)), count)
-    d_queries = then(d_queries, (first, 0), (first, 1), (up, 1), (down, 0))
+        parts = outer_wide([tokens, tokens, tokens], [d_queries, d_keys, d_values], (0, 2, 4, 6), count)
+        core = mine_of()["c"]
+        keep = jnp.concatenate([parts[4], take(packed, 1, core)], axis=-1)
+        send = jnp.concatenate([parts[5], take(packed, 1, 1 - core)], axis=-1)
+        first = Sums(list(parts[:4]) + [keep, send], THREE_WAYS, count)
+        d_queries = after(d_queries, *first.last)
+        d_queries = then(d_queries, parts[0], (down, 0), (up_1, 0), (up_1, 1), (up_2, 0), (up_2, 1))
     grad_rows = d_resid + dot_nt(d_queries, w_query)
-    d_keys = then(d_keys, (first, 0), (first, 1))
-    grad_rows = grad_rows + dot_nt(d_keys, w_key)
-    d_values = then(d_values, (up, 0), (up, 1))
-    grad_rows = (grad_rows + dot_nt(d_values, w_value)).astype(LOW)
-
     if custom:
-        d_w_down = down.result()
-        second = up.result()
-        first = first.result()
+        grad_rows = then(grad_rows, grad_rows, (first, 0), (first, 1), (first, 2))
+    grad_rows = grad_rows + dot_nt(d_keys, w_key) + dot_nt(d_values, w_value)
+
+    if custom:
+        grad_rows = grad_rows.astype(LOW)
+        d_w_down = jnp.concatenate(down.results(), axis=-1)
+        d_w_up = jnp.concatenate(up_1.results() + up_2.results()[:1], axis=-1)
+        d_w_out = up_2.results()[1]
+        d_w_query, d_w_key, last = first.results()
+        d_w_value, flat = last[:, :D], last[:, D:].reshape(-1)
     else:
         total = lambda grad: lax.psum_scatter(grad.astype(LOW), "dp", scatter_dimension=0, tiled=True).astype(FULL)
+        grad_rows = grad_rows.astype(LOW)
         d_w_down = total(dot_tn(hidden, d_ffn))
-        second = total(jnp.concatenate([dot_tn(first_low, d_pre), dot_tn(attn_rows, d_branch)], axis=1))
-        first = [dot_tn(tokens, grad) for grad in (d_queries, d_keys, d_values)]
-        first = total(jnp.concatenate(first + [packed.reshape(D, 128)], axis=1))
-    flat = first[:, 3 * D :].reshape(-1)
+        d_w_up = total(jnp.concatenate([dot_tn(first_low, pre) for pre in (pre_1, pre_2, pre_3)], axis=1))
+        d_w_out = total(dot_tn(attn_rows, d_branch))
+        d_w_query, d_w_key, d_w_value = [total(dot_tn(tokens, grad)) for grad in (d_queries, d_keys, d_values)]
+        flat = total(packed.reshape(D, 128)).reshape(-1)
     vector = lambda col: flat[part * col : part * col + part]
     return (
         result,
         grad_rows,
-        first[:, :D],
-        first[:, D : 2 * D],
-        first[:, 2 * D : 3 * D],
-        second[:, wide:],
-        second[:, :wide],
+        d_w_query,
+        d_w_key,
+        d_w_value,
+        d_w_out,
+        d_w_up,
         d_w_down,
         vector(0),
         vector(1),

time: 1350 us -> 636 us (0.47)
  Pallas kernels: 965 us -> 194 us
  local copies, waits for them, and re-layouts: 82 us -> 114 us
    pallas_call x5 -> x9, Pallas kernels: 800 us -> 66.9 us  [the longest x3 34.8 us: narrow(): pl.pallas_call(narrow_kernel, grid=(last - first,), in_specs=[fixed(d_ffn...]
    pallas_call x9 -> x6, Pallas kernels: 126 us -> 88.1 us  [continued(): return lambda *operands: call(*operands, *before)]
    ppermute x42 -> x55, waiting for transfers between devices: 50 us -> 28.9 us  [hop(): lax.ppermute(array, 'dp', [(place, place ^ FLIPS[dim]) for place in range...]
    unnamed x170 -> x222, local copies, waits for them, and re-layouts: 60.6 us -> 81.2 us
    ppermute x36 -> x48, waiting for transfers between devices: 127 us -> 141 us  [hop(): return lax.ppermute(array, 'dp', ring_pairs(count))]
    ppermute x42 -> x55, starting transfers between devices: 32.5 us -> 36.3 us  [hop(): lax.ppermute(array, 'dp', [(place, place ^ FLIPS[dim]) for place in range...]
    convert_element_type x33 -> x50, other arithmetic: 35.7 us -> 37.9 us  [add_low(): return (left_side.astype(FULL) + right_side.astype(FULL)).astype(kind)]
  transfers between devices with their start and end apart: 78 -> 103, of which waited for: 38 -> 36; matrix products, arithmetic and copies ran while one was open for 6% -> 21% of each run, Pallas kernels for 42% -> 26%
where the time goes in v3:
time: 636 us; the launch traced here: 625 us
  Pallas kernels  194 us (31%)
  waiting for transfers between devices  169 us (27%)
  local copies, waits for them, and re-layouts  114 us (18%)
  starting transfers between devices  60.1 us (9%)
  other arithmetic  58.1 us (9%)
  matrix products  27.2 us (4%)
    ppermute x48, waiting for transfers between devices, hop(): return lax.ppermute(array, 'dp', ring_pairs(count))  141 us
    pallas_call x6, Pallas kernels, continued(): return lambda *operands: call(*operands, *before)  88.1 us
    unnamed x222, local copies, waits for them, and re-layouts  81.2 us
    convert_element_type x50, other arithmetic, add_low(): return (left_side.astype(FULL) + right_side.astype(FULL)).astype(kind)  37.9 us
    ppermute x55, starting transfers between devices, hop(): lax.ppermute(array, 'dp', [(place, place ^ FLIPS[dim]) for place in range...  36.3 us
    pallas_call x3, Pallas kernels, narrow(): pl.pallas_call(narrow_kernel, grid=(last - first,), in_specs=[fixed(d_ffn...  34.8 us
    ppermute x55, waiting for transfers between devices, hop(): lax.ppermute(array, 'dp', [(place, place ^ FLIPS[dim]) for place in range...  28.9 us
    pallas_call x3, Pallas kernels, outer_wide(): pl.pallas_call(functools.partial(wide_kernel, starts, cuts), grid=(total,...  25.6 us
  transfers between devices with their start and end apart: 103, of which 36 were waited for; matrix products, arithmetic and copies ran while one was open for 21% of the time, Pallas kernels for 26%

profile of v3, /device:TPU:0, one launch (start us, length us, event | category | flops | bytes accessed | tf_op | source)
XLA Modules:
  0.0 624.7 jit_solution(11821253025415672419)
XLA Ops:
  38.2 9.1 %collective-permute-done.9 = bf16[2,32,1024]{2,1,0:T(8,128)(2,1)S(1)} collective-permute-done((bf16[2,32,1024]{2,1,0:T(8,128)(2,1)S(1)}, bf16[2,32,1024]{2,1,0:T(8,128)(2,1)S(1)}, u32[]{:S(2)}, u32[]{:S(2)}) %collective-permute-start.9) | collective-permute-done | bytes 131104 | tf_op jit(solution)/shard_map/ppermute | solution.py:446
  61.7 7.9 %collective-permute-done.29 = bf16[2,32,1792]{2,1,0:T(8,128)(2,1)S(1)} collective-permute-done((bf16[2,32,1792]{2,1,0:T(8,128)(2,1)S(1)}, bf16[2,32,1792]{2,1,0:T(8,128)(2,1)S(1)}, u32[]{:S(2)}, u32[]{:S(2)}) %collective-permute-start.29) | collective-permute-done | bytes 229408 | tf_op jit(solution)/shard_map/ppermute | solution.py:446
  72.6 7.1 %collective-permute-done.30 = bf16[2,32,1792]{2,1,0:T(8,128)(2,1)S(1)} collective-permute-done((bf16[2,32,1792]{2,1,0:T(8,128)(2,1)S(1)}, bf16[2,32,1792]{2,1,0:T(8,128)(2,1)S(1)}, u32[]{:S(2)}, u32[]{:S(2)}) %collective-permute-start.30) | collective-permute-done | bytes 229408 | tf_op jit(solution)/shard_map/ppermute | solution.py:446
  115.7 14.0 %attend.2 = (bf16[2,16,512,512]{3,2,1,0:T(8,128)(2,1)}, bf16[1024,1024]{1,0:T(8,128)(2,1)S(1)}) custom-call(bf16[1024,1024]{1,0:T(8,128)(2,1)S(1)} %copy-done.71, bf16[1024,1024]{1,0:T(8,128)(2,1)S(1)} %copy-done.60, bf16[1024,1024]{1,0:T(8,128)(2,1)S(1)} %fusion.1.v_ref.refs_2_), custom_call_target="tpu_custom_call" | custom-call | flops 12884901888 | bytes 12582912 | tf_op jit(solution)/shard_map/attend/pallas_call | solution.py:69
  176.4 14.2 %attend.3 = (bf16[2,16,512,512]{3,2,1,0:T(8,128)(2,1)}, bf16[1024,1024]{1,0:T(8,128)(2,1)S(1)}) custom-call(bf16[1024,1024]{1,0:T(8,128)(2,1)S(1)} %copy-done.72, bf16[1024,1024]{1,0:T(8,128)(2,1)S(1)} %copy-done.61, bf16[1024,1024]{1,0:T(8,128)(2,1)S(1)} %copy-done.75, ...), custom_call_target="tpu_custom_call", output_to_operand_aliasing={{0}: (3, {}), {1}: (4, {})} | custom-call | flops 12884901888 | bytes 12582912 | tf_op jit(solution)/shard_map/attend/pallas_call | solution.py:69
  192.5 8.2 %collective-permute-done.39.refs_1_ = bf16[8,128,640]{2,1,0:T(8,128)(2,1)S(1)} collective-permute-done((bf16[8,128,640]{2,1,0:T(8,128)(2,1)}, bf16[8,128,640]{2,1,0:T(8,128)(2,1)S(1)}, u32[]{:S(2)}, u32[]{:S(2)}) %collective-permute-start.39) | collective-permute-done | bytes 1310752 | tf_op jit(solution)/shard_map/ppermute | solution.py:447
  220.9 16.1 %widen.2 = (bf16[1024,4096]{1,0:T(8,128)(2,1)S(1)}, bf16[1024,4096]{1,0:T(8,128)(2,1)S(1)}) custom-call(bf16[1024,1024]{1,0:T(8,128)(2,1)S(1)} %get-tuple-element.134.low_ref.refs_0_.refs_1_, bf16[1024,4096]{1,0:T(8,128)(2,1)} %copy-done.1, f32[1,4096]{1,0:T(1,128)S(1)} %bitcast.457), custom_call_target="tpu_custom_call" | custom-call | flops 12884901888 | bytes 12582912 | tf_op jit(solution)/shard_map/widen/pallas_call | solution.py:69
  237.0 15.3 %widen.3 = (bf16[1024,4096]{1,0:T(8,128)(2,1)S(1)}, bf16[1024,4096]{1,0:T(8,128)(2,1)S(1)}) custom-call(bf16[1024,1024]{1,0:T(8,128)(2,1)S(1)} %get-tuple-element.134.low_ref.refs_0_.refs_1_, bf16[1024,4096]{1,0:T(8,128)(2,1)} %copy-done.1, f32[1,4096]{1,0:T(1,128)S(1)} %bitcast.458, ...), custom_call_target="tpu_custom_call", output_to_operand_aliasing={{0}: (3, {}), {1}: (4, {})} | custom-call | flops 12884901888 | bytes 12582912 | tf_op jit(solution)/shard_map/widen/pallas_call | solution.py:69
  263.7 17.3 %fall.1 = (bf16[1024,1024]{1,0:T(8,128)(2,1)}, f32[1024,1024]{1,0:T(8,128)S(1)}, bf16[1024,1024]{1,0:T(8,128)(2,1)S(1)}, f32[3,1024]{1,0:T(4,128)S(1)}) custom-call(bf16[1024,4096]{1,0:T(8,128)(2,1)} %copy-done.52, bf16[4096,1024]{1,0:T(8,128)(2,1)} %copy-done, f32[1024,1024]{1,0:T(8,128)S(1)} %copy-done.48, bf16[1024,1024]{1,0:T(8,128)(2,1)S(1)} %copy-done.24, ...), custom_call_target="tpu_custom_call" | custom-call | flops 8589934592 | bytes 31457280 | tf_op jit(solution)/shard_map/fall/pallas_call | solution.py:261
  287.1 12.5 %outer_tall.1 = (bf16[16,128,640]{2,1,0:T(8,128)(2,1)S(1)}, bf16[16,128,640]{2,1,0:T(8,128)(2,1)}, bf16[16,128,384]{2,1,0:T(8,128)(2,1)S(1)}, bf16[16,128,384]{2,1,0:T(8,128)(2,1)}) custom-call(bf16[1024,4096]{1,0:T(8,128)(2,1)S(1)} %copy-done.53, bf16[1024,1024]{1,0:T(8,128)(2,1)S(1)} %get-tuple-element.143.right_ref.ffn_ref), custom_call_target="tpu_custom_call" | custom-call | flops 8589934592 | bytes 18874368 | tf_op jit(solution)/shard_map/outer_tall/pallas_call | solution.py:373
  306.0 9.2 %narrow.3 = (bf16[1024,1024]{1,0:T(8,128)(2,1)S(1)}, f32[1,1024]{1,0:T(1,128)S(1)}, f32[1024,1024]{1,0:T(8,128)S(1)}) custom-call(bf16[1024,1024]{1,0:T(8,128)(2,1)S(1)} %copy-done.11, bf16[1024,4096]{1,0:T(8,128)(2,1)} %copy-done.2, bf16[4096,1024]{1,0:T(8,128)(2,1)} %copy-done, bf16[1024,4096]{1,0:T(8,128)(2,1)} %copy-done.1, f32[1024,1024]{1,0:T(8,128)S(1)} %copy-done.6), custom_call_target="tpu_custom_call" | custom-call | flops 6442450944 | bytes 18874368 | tf_op jit(solution)/shard_map/narrow/pallas_call | solution.py:301
  322.7 13.1 %narrow.4 = (bf16[1024,1536]{1,0:T(8,128)(2,1)S(1)}, f32[1,1536]{1,0:T(1,128)S(1)}, f32[1024,1024]{1,0:T(8,128)S(1)}) custom-call(bf16[1024,1024]{1,0:T(8,128)(2,1)S(1)} %copy-done.12, bf16[1024,4096]{1,0:T(8,128)(2,1)} %copy-done.2, bf16[4096,1024]{1,0:T(8,128)(2,1)} %copy-done, bf16[1024,4096]{1,0:T(8,128)(2,1)} %copy-done.1, ...), custom_call_target="tpu_custom_call" | custom-call | flops 9663676416 | bytes 23068672 | tf_op jit(solution)/shard_map/narrow/pallas_call | solution.py:301
  338.9 7.8 %outer_wide.3 = (bf16[16,32,1536]{2,1,0:T(8,128)(2,1)S(1)}, bf16[16,32,1536]{2,1,0:T(8,128)(2,1)S(1)}, bf16[16,32,1024]{2,1,0:T(8,128)(2,1)S(1)}, bf16[16,32,1024]{2,1,0:T(8,128)(2,1)S(1)}) custom-call(bf16[1024,1024]{1,0:T(8,128)(2,1)S(1)} %copy-done.64, bf16[1024,1024]{1,0:T(8,128)(2,1)S(1)} %copy-done.64, bf16[1024,1024]{1,0:T(8,128)(2,1)S(1)} %copy-done.38, ...), custom_call_target="tpu_custom_call" | custom-call | flops 5368709120 | bytes 14680064 | tf_op jit(solution)/shard_map/outer_wide/pallas_call | solution.py:419
  350.6 12.5 %narrow.5 = (bf16[1024,1536]{1,0:T(8,128)(2,1)S(1)}, f32[1,1536]{1,0:T(1,128)S(1)}, f32[1024,1024]{1,0:T(8,128)S(1)}) custom-call(bf16[1024,1024]{1,0:T(8,128)(2,1)S(1)} %copy-done.12, bf16[1024,4096]{1,0:T(8,128)(2,1)} %copy-done.2, bf16[4096,1024]{1,0:T(8,128)(2,1)} %copy-done, bf16[1024,4096]{1,0:T(8,128)(2,1)} %copy-done.1, f32[1024,1024]{1,0:T(8,128)S(1)} %copy-done.46), custom_call_target="tpu_custom_call" | custom-call | flops 9663676416 | bytes 23068672 | tf_op jit(solution)/shard_map/narrow/pallas_call | solution.py:301
  401.6 8.0 %outer_wide.4 = (bf16[16,32,1536]{2,1,0:T(8,128)(2,1)S(1)}, bf16[16,32,1536]{2,1,0:T(8,128)(2,1)S(1)}, bf16[16,32,1024]{2,1,0:T(8,128)(2,1)S(1)}, bf16[16,32,1024]{2,1,0:T(8,128)(2,1)S(1)}) custom-call(bf16[1024,1024]{1,0:T(8,128)(2,1)S(1)} %copy-done.65, bf16[1024,1024]{1,0:T(8,128)(2,1)S(1)} %copy-done.70, bf16[1024,1536]{1,0:T(8,128)(2,1)S(1)} %copy-done.51, ...), custom_call_target="tpu_custom_call" | custom-call | flops 5368709120 | bytes 14680064 | tf_op jit(solution)/shard_map/outer_wide/pallas_call | solution.py:419
  413.5 14.3 %attend_back.2 = (bf16[1024,1024]{1,0:T(8,128)(2,1)S(1)}, bf16[1024,1024]{1,0:T(8,128)(2,1)S(1)}, bf16[1024,1024]{1,0:T(8,128)(2,1)S(1)}) custom-call(bf16[1024,1024]{1,0:T(8,128)(2,1)S(1)} %copy-done.73, bf16[1024,1024]{1,0:T(8,128)(2,1)S(1)} %copy-done.62, bf16[1024,1024]{1,0:T(8,128)(2,1)S(1)} %copy-done.76, ...), custom_call_target="tpu_custom_call" | custom-call | flops 12884901888 | bytes 15728640 | tf_op jit(solution)/shard_map/attend_back/pallas_call | solution.py:69
  446.6 14.3 %attend_back.3 = (bf16[1024,1024]{1,0:T(8,128)(2,1)S(1)}, bf16[1024,1024]{1,0:T(8,128)(2,1)S(1)}, bf16[1024,1024]{1,0:T(8,128)(2,1)S(1)}) custom-call(bf16[1024,1024]{1,0:T(8,128)(2,1)S(1)} %copy-done.73, bf16[1024,1024]{1,0:T(8,128)(2,1)S(1)} %copy-done.62, ...), custom_call_target="tpu_custom_call", output_to_operand_aliasing={{0}: (5, {}), {1}: (6, {}), {2}: (7, {})} | custom-call | flops 12884901888 | bytes 15728640 | tf_op jit(solution)/shard_map/attend_back/pallas_call | solution.py:69
  477.9 6.7 %fusion.133 = f32[1024,1024]{1,0:T(8,128)} fusion(bf16[1024,1024]{1,0:T(8,128)(2,1)} %copy-done.58, bf16[1024,1024]{1,0:T(8,128)(2,1)} %copy-done.32), kind=kOutput, calls=%fused_computation.328 | convolution fusion | flops 2147483648 | bytes 8388608 | tf_op jit(solution)/shard_map/dot_general | solution.py:25
  484.6 9.8 %outer_wide.5 = (bf16[16,32,1024]{2,1,0:T(8,128)(2,1)S(1)}, bf16[16,32,1024]{2,1,0:T(8,128)(2,1)S(1)}, bf16[16,32,1024]{2,1,0:T(8,128)(2,1)S(1)}, bf16[16,32,102...) custom-call(bf16[1024,1024]{1,0:T(8,128)(2,1)S(1)} %copy-done.27, ...), custom_call_target="tpu_custom_call" | custom-call | flops 6442450944 | bytes 18874368 | tf_op jit(solution)/shard_map/outer_wide/pallas_call | solution.py:419
  517.0 6.8 %collective-permute-done.92 = bf16[2,32,1024]{2,1,0:T(8,128)(2,1)S(1)} collective-permute-done((bf16[2,32,1024]{2,1,0:T(8,128)(2,1)S(1)}, bf16[2,32,1024]{2,1,0:T(8,128)(2,1)S(1)}, u32[]{:S(2)}, u32[]{:S(2)}) %collective-permute-start.92) | collective-permute-done | bytes 131104 | tf_op jit(solution)/shard_map/ppermute | solution.py:446
  523.9 6.7 %collective-permute-done.97 = bf16[2,32,1024]{2,1,0:T(8,128)(2,1)S(1)} collective-permute-done((bf16[2,32,1024]{2,1,0:T(8,128)(2,1)S(1)}, bf16[2,32,1024]{2,1,0:T(8,128)(2,1)S(1)}, u32[]{:S(2)}, u32[]{:S(2)}) %collective-permute-start.97) | collective-permute-done | bytes 131104 | tf_op jit(solution)/shard_map/ppermute | solution.py:446
  537.1 6.7 %collective-permute-done.93 = bf16[2,32,1024]{2,1,0:T(8,128)(2,1)S(1)} collective-permute-done((bf16[2,32,1024]{2,1,0:T(8,128)(2,1)S(1)}, bf16[2,32,1024]{2,1,0:T(8,128)(2,1)S(1)}, u32[]{:S(2)}, u32[]{:S(2)}) %collective-permute-start.93) | collective-permute-done | bytes 131104 | tf_op jit(solution)/shard_map/ppermute | solution.py:446
  588.7 7.4 %collective-permute-done.83 = bf16[2,32,1024]{2,1,0:T(8,128)(2,1)S(1)} collective-permute-done((bf16[2,32,1024]{2,1,0:T(8,128)(2,1)S(1)}, bf16[2,32,1024]{2,1,0:T(8,128)(2,1)S(1)}, u32[]{:S(2)}, u32[]{:S(2)}) %collective-permute-start.83) | collective-permute-done | bytes 131104 | tf_op jit(solution)/shard_map/ppermute | solution.py:446
  597.1 6.7 %collective-permute-done.79 = bf16[32,1024]{1,0:T(8,128)(2,1)S(1)} collective-permute-done((bf16[32,1024]{1,0:T(8,128)(2,1)S(1)}, bf16[32,1024]{1,0:T(8,128)(2,1)S(1)}, u32[]{:S(2)}, u32[]{:S(2)}) %collective-permute-start.79) | collective-permute-done | bytes 65568 | tf_op jit(solution)/shard_map/ppermute | solution.py:446
  (553 shorter events, 370.4 us)
Async XLA Ops:
  90.5 82.0 %collective-permute-start.33 = (bf16[8,32,1792]{2,1,0:T(8,128)(2,1)}, bf16[8,32,1792]{2,1,0:T(8,128)(2,1)}, u32[]{:S(2)}, u32[]{:S(2)}) collective-permute-start(bf16[8,32,1792]{2,1,0:T(8,128)(2,1)} %constant_dynamic-update-slice_fusion.17.refs_4_), channel_id=1, source_target_pairs={{0,1},{1,0},{2,3},{3,2},{4,5},{5,4},{6,7},{7,6},{8,9},{9,8},{10,11... | collective-permute-start | bytes 2752520 | tf_op jit(solution)/shard_map/ppermute | solution.py:447
  90.7 71.2 %collective-permute-start.32 = (bf16[8,32,1792]{2,1,0:T(8,128)(2,1)}, bf16[8,32,1792]{2,1,0:T(8,128)(2,1)}, u32[]{:S(2)}, u32[]{:S(2)}) collective-permute-start(bf16[8,32,1792]{2,1,0:T(8,128)(2,1)} %constant_dynamic-update-slice_fusion.17.refs_4_), channel_id=1, source_target_pairs={{0,4},{1,5},{2,6},{3,7},{4,0},{5,1},{6,2},{7,3},{8,12},{9,13},{10,... | collective-permute-start | bytes 2752520 | tf_op jit(solution)/shard_map/ppermute | solution.py:447
  96.9 46.3 %collective-permute-start.42 = (bf16[1,128,384]{2,1,0:T(8,128)(2,1)S(1)}, bf16[1,128,384]{2,1,0:T(8,128)(2,1)}, u32[]{:S(2)}, u32[]{:S(2)}) collective-permute-start(bf16[1,128,384]{2,1,0:T(8,128)(2,1)S(1)} %slice_bitcast_fusion.2), channel_id=1, source_target_pairs={{0,2},{1,3},{2,0},{3,1},{4,6},{5,7},{6,4},{7,5},{8,10},{9,11},{10,... | collective-permute-start | bytes 294920 | tf_op jit(solution)/shard_map/ppermute | solution.py:447
  98.1 32.9 %collective-permute-start.35 = (bf16[1,128,640]{2,1,0:T(8,128)(2,1)}, bf16[1,128,640]{2,1,0:T(8,128)(2,1)}, u32[]{:S(2)}, u32[]{:S(2)}) collective-permute-start(bf16[1,128,640]{2,1,0:T(8,128)(2,1)} %slice_bitcast_fusion.1), channel_id=1, source_target_pairs={{0,8},{1,9},{2,10},{3,11},{4,12},{5,13},{6,14},{7,15},{8,16},{9,17... | collective-permute-start | bytes 491528 | tf_op jit(solution)/shard_map/ppermute | solution.py:446
  114.4 44.7 %collective-permute-start.25 = (bf16[8,32,3328]{2,1,0:T(8,128)(2,1)S(1)}, bf16[8,32,3328]{2,1,0:T(8,128)(2,1)S(1)}, u32[]{:S(2)}, u32[]{:S(2)}) collective-permute-start(bf16[8,32,3328]{2,1,0:T(8,128)(2,1)S(1)} %constant_dynamic-update-slice_fusion.15.refs_0_), channel_id=1, source_target_pairs={{0,2},{1,3},{2,0},{3,1},{4,6},{5,7},{6,4},{7,5},{8,10},{9,11},{10,... | collective-permute-start | bytes 5111816 | tf_op jit(solution)/shard_map/ppermute | solution.py:447
  159.2 33.2 %collective-permute-start.26 = (bf16[8,32,3328]{2,1,0:T(8,128)(2,1)S(1)}, bf16[8,32,3328]{2,1,0:T(8,128)(2,1)S(1)}, u32[]{:S(2)}, u32[]{:S(2)}) collective-permute-start(bf16[8,32,3328]{2,1,0:T(8,128)(2,1)S(1)} %constant_dynamic-update-slice_fusion.15.refs_0_), channel_id=1, source_target_pairs={{0,1},{1,0},{2,3},{3,2},{4,5},{5,4},{6,7},{7,6},{8,9},{9,8},{10,11... | collective-permute-start | bytes 5111816 | tf_op jit(solution)/shard_map/ppermute | solution.py:447
  159.2 41.5 %collective-permute-start.27 = (bf16[8,32,3328]{2,1,0:T(8,128)(2,1)S(1)}, bf16[8,32,3328]{2,1,0:T(8,128)(2,1)S(1)}, u32[]{:S(2)}, u32[]{:S(2)}) collective-permute-start(bf16[8,32,3328]{2,1,0:T(8,128)(2,1)S(1)} %collective-permute-done.25.refs_1_), channel_id=1, source_target_pairs={{0,1},{1,0},{2,3},{3,2},{4,5},{5,4},{6,7},{7,6},{8,9},{9,8},{10,11... | collective-permute-start | bytes 5111816 | tf_op jit(solution)/shard_map/ppermute | solution.py:447
  191.8 67.1 %collective-permute-start.47 = (bf16[8,128,384]{2,1,0:T(8,128)(2,1)S(1)}, bf16[8,128,384]{2,1,0:T(8,128)(2,1)S(1)}, u32[]{:S(2)}, u32[]{:S(2)}) collective-permute-start(bf16[8,128,384]{2,1,0:T(8,128)(2,1)S(1)} %copy-done.23), channel_id=1, source_target_pairs={{0,1},{1,0},{2,3},{3,2},{4,5},{5,4},{6,7},{7,6},{8,9},{9,8},{10,11... | collective-permute-start | bytes 2359304 | tf_op jit(solution)/shard_map/ppermute | solution.py:447
  191.9 67.1 %collective-permute-start.40 = (bf16[8,128,640]{2,1,0:T(8,128)(2,1)S(1)}, bf16[8,128,640]{2,1,0:T(8,128)(2,1)S(1)}, u32[]{:S(2)}, u32[]{:S(2)}) collective-permute-start(bf16[8,128,640]{2,1,0:T(8,128)(2,1)S(1)} %copy-done.13), channel_id=1, source_target_pairs={{0,1},{1,0},{2,3},{3,2},{4,5},{5,4},{6,7},{7,6},{8,9},{9,8},{10,11... | collective-permute-start | bytes 3932168 | tf_op jit(solution)/shard_map/ppermute | solution.py:447
  192.4 66.6 %collective-permute-start.48 = (bf16[8,128,384]{2,1,0:T(8,128)(2,1)S(1)}, bf16[8,128,384]{2,1,0:T(8,128)(2,1)S(1)}, u32[]{:S(2)}, u32[]{:S(2)}) collective-permute-start(bf16[8,128,384]{2,1,0:T(8,128)(2,1)S(1)} %collective-permute-done.46.refs_5_), channel_id=1, source_target_pairs={{0,1},{1,0},{2,3},{3,2},{4,5},{5,4},{6,7},{7,6},{8,9},{9,8},{10,11... | collective-permute-start | bytes 2359304 | tf_op jit(solution)/shard_map/ppermute | solution.py:447
  200.6 58.4 %collective-permute-start.41 = (bf16[8,128,640]{2,1,0:T(8,128)(2,1)S(1)}, bf16[8,128,640]{2,1,0:T(8,128)(2,1)S(1)}, u32[]{:S(2)}, u32[]{:S(2)}) collective-permute-start(bf16[8,128,640]{2,1,0:T(8,128)(2,1)S(1)} %collective-permute-done.39.refs_1_), channel_id=1, source_target_pairs={{0,1},{1,0},{2,3},{3,2},{4,5},{5,4},{6,7},{7,6},{8,9},{9,8},{10,11... | collective-permute-start | bytes 3932168 | tf_op jit(solution)/shard_map/ppermute | solution.py:447
  321.9 52.0 %collective-permute-start.52 = (bf16[4,2,128,640]{3,2,1,0:T(8,128)(2,1)}, bf16[4,2,128,640]{3,2,1,0:T(8,128)(2,1)}, u32[]{:S(2)}, u32[]{:S(2)}) collective-permute-start(bf16[4,2,128,640]{3,2,1,0:T(8,128)(2,1)} %fusion.2), channel_id=1, source_target_pairs={{0,2},{1,3},{2,0},{3,1},{4,6},{5,7},{6,4},{7,5},{8,10},{9,11},{10,... | collective-permute-start | bytes 3932168 | tf_op jit(solution)/shard_map/ppermute | solution.py:447
  372.7 55.2 %collective-permute-start.62 = (bf16[4,2,32,1024]{3,2,1,0:T(8,128)(2,1)}, bf16[4,2,32,1024]{3,2,1,0:T(8,128)(2,1)}, u32[]{:S(2)}, u32[]{:S(2)}) collective-permute-start(bf16[4,2,32,1024]{3,2,1,0:T(8,128)(2,1)} %get-tuple-element.242), channel_id=1, source_target_pairs={{0,4},{1,5},{2,6},{3,7},{4,0},{5,1},{6,2},{7,3},{8,12},{9,13},{10,... | collective-permute-start | bytes 1572872 | tf_op jit(solution)/shard_map/ppermute | solution.py:447
  376.7 35.0 %collective-permute-start.56 = (bf16[4,128,640]{2,1,0:T(8,128)(2,1)}, bf16[4,128,640]{2,1,0:T(8,128)(2,1)}, u32[]{:S(2)}, u32[]{:S(2)}) collective-permute-start(bf16[4,128,640]{2,1,0:T(8,128)(2,1)} %get-tuple-element.236), channel_id=1, source_target_pairs={{0,4},{1,5},{2,6},{3,7},{4,0},{5,1},{6,2},{7,3},{8,12},{9,13},{10,... | collective-permute-start | bytes 1966088 | tf_op jit(solution)/shard_map/ppermute | solution.py:447
  379.7 60.6 %collective-permute-start.61 = (bf16[4,2,32,1536]{3,2,1,0:T(8,128)(2,1)}, bf16[4,2,32,1536]{3,2,1,0:T(8,128)(2,1)}, u32[]{:S(2)}, u32[]{:S(2)}) collective-permute-start(bf16[4,2,32,1536]{3,2,1,0:T(8,128)(2,1)} %fusion.6), channel_id=1, source_target_pairs={{0,2},{1,3},{2,0},{3,1},{4,6},{5,7},{6,4},{7,5},{8,10},{9,11},{10,... | collective-permute-start | bytes 2359304 | tf_op jit(solution)/shard_map/ppermute | solution.py:447
  409.6 33.2 %collective-permute-start.64 = (bf16[16,32,1024]{2,1,0:T(8,128)(2,1)S(1)}, bf16[16,32,1024]{2,1,0:T(8,128)(2,1)S(1)}, u32[]{:S(2)}, u32[]{:S(2)}) collective-permute-start(bf16[16,32,1024]{2,1,0:T(8,128)(2,1)S(1)} %get-tuple-element.187), channel_id=1, source_target_pairs={{0,1},{1,0},{2,3},{3,2},{4,5},{5,4},{6,7},{7,6},{8,9},{9,8},{10,11... | collective-permute-start | bytes 3145736 | tf_op jit(solution)/shard_map/ppermute | solution.py:447
  411.2 33.0 %collective-permute-start.63 = (bf16[16,32,1536]{2,1,0:T(8,128)(2,1)S(1)}, bf16[16,32,1536]{2,1,0:T(8,128)(2,1)S(1)}, u32[]{:S(2)}, u32[]{:S(2)}) collective-permute-start(bf16[16,32,1536]{2,1,0:T(8,128)(2,1)S(1)} %get-tuple-element.186), channel_id=1, source_target_pairs={{0,1},{1,0},{2,3},{3,2},{4,5},{5,4},{6,7},{7,6},{8,9},{9,8},{10,11... | collective-permute-start | bytes 4718600 | tf_op jit(solution)/shard_map/ppermute | solution.py:447
  445.4 107.7 %collective-permute-start.72 = (bf16[4,2,32,1536]{3,2,1,0:T(8,128)(2,1)}, bf16[4,2,32,1536]{3,2,1,0:T(8,128)(2,1)}, u32[]{:S(2)}, u32[]{:S(2)}) collective-permute-start(bf16[4,2,32,1536]{3,2,1,0:T(8,128)(2,1)} %fusion.7), channel_id=1, source_target_pairs={{0,2},{1,3},{2,0},{3,1},{4,6},{5,7},{6,4},{7,5},{8,10},{9,11},{10,... | collective-permute-start | bytes 2359304 | tf_op jit(solution)/shard_map/ppermute | solution.py:447
  471.2 34.9 %collective-permute-start.70 = (bf16[32,1536]{1,0:T(8,128)(2,1)}, bf16[32,1536]{1,0:T(8,128)(2,1)}, u32[]{:S(2)}, u32[]{:S(2)}) collective-permute-start(bf16[32,1536]{1,0:T(8,128)(2,1)} %fusion.111), channel_id=1, source_target_pairs={{0,8},{1,9},{2,10},{3,11},{4,12},{5,13},{6,14},{7,15},{8,16},{9,17... | collective-permute-start | bytes 294920 | tf_op jit(solution)/shard_map/ppermute | solution.py:446
  471.2 37.5 %collective-permute-start.71 = (bf16[2,32,1024]{2,1,0:T(8,128)(2,1)}, bf16[2,32,1024]{2,1,0:T(8,128)(2,1)}, u32[]{:S(2)}, u32[]{:S(2)}) collective-permute-start(bf16[2,32,1024]{2,1,0:T(8,128)(2,1)} %fusion.60), channel_id=1, source_target_pairs={{0,8},{1,9},{2,10},{3,11},{4,12},{5,13},{6,14},{7,15},{8,16},{9,17... | collective-permute-start | bytes 393224 | tf_op jit(solution)/shard_map/ppermute | solution.py:446
  471.8 38.1 %collective-permute-start.69 = (bf16[128,640]{1,0:T(8,128)(2,1)}, bf16[128,640]{1,0:T(8,128)(2,1)}, u32[]{:S(2)}, u32[]{:S(2)}) collective-permute-start(bf16[128,640]{1,0:T(8,128)(2,1)} %fusion.30), channel_id=1, source_target_pairs={{0,8},{1,9},{2,10},{3,11},{4,12},{5,13},{6,14},{7,15},{8,16},{9,17... | collective-permute-start | bytes 491528 | tf_op jit(solution)/shard_map/ppermute | solution.py:446
  506.1 52.9 %collective-permute-start.74 = (bf16[16,32,1024]{2,1,0:T(8,128)(2,1)S(1)}, bf16[16,32,1024]{2,1,0:T(8,128)(2,1)S(1)}, u32[]{:S(2)}, u32[]{:S(2)}) collective-permute-start(bf16[16,32,1024]{2,1,0:T(8,128)(2,1)S(1)} %copy-done.42), channel_id=1, source_target_pairs={{0,1},{1,0},{2,3},{3,2},{4,5},{5,4},{6,7},{7,6},{8,9},{9,8},{10,11... | collective-permute-start | bytes 3145736 | tf_op jit(solution)/shard_map/ppermute | solution.py:447
  507.2 53.3 %collective-permute-start.75 = (bf16[16,32,1024]{2,1,0:T(8,128)(2,1)S(1)}, bf16[16,32,1024]{2,1,0:T(8,128)(2,1)S(1)}, u32[]{:S(2)}, u32[]{:S(2)}) collective-permute-start(bf16[16,32,1024]{2,1,0:T(8,128)(2,1)S(1)} %copy-done.40), channel_id=1, source_target_pairs={{0,1},{1,0},{2,3},{3,2},{4,5},{5,4},{6,7},{7,6},{8,9},{9,8},{10,11... | collective-permute-start | bytes 3145736 | tf_op jit(solution)/shard_map/ppermute | solution.py:447
  508.7 53.3 %collective-permute-start.76 = (bf16[16,32,1152]{2,1,0:T(8,128)(2,1)S(1)}, bf16[16,32,1152]{2,1,0:T(8,128)(2,1)S(1)}, u32[]{:S(2)}, u32[]{:S(2)}) collective-permute-start(bf16[16,32,1152]{2,1,0:T(8,128)(2,1)S(1)} %pad_maximum_fusion), channel_id=1, source_target_pairs={{0,1},{1,0},{2,3},{3,2},{4,5},{5,4},{6,7},{7,6},{8,9},{9,8},{10,11... | collective-permute-start | bytes 3538952 | tf_op jit(solution)/shard_map/ppermute | solution.py:447
  (177 other events, 1885.4 us)

commit v4 on v3

--- a/solution.py
+++ b/solution.py
@@ -82,7 +82,7 @@
             jax.ShapeDtypeStruct((rows // LEN, HEADS, LEN, LEN), LOW),
             jax.ShapeDtypeStruct((rows, D), LOW),
         ],
-        compiler_params=pltpu.CompilerParams(vmem_limit_bytes=32 * MIB),
+        compiler_params=pltpu.CompilerParams(vmem_limit_bytes=GRANT),
         cost_estimate=pl.CostEstimate(
             flops=12 * HEADS * LEN * LEN * 256, bytes_accessed=HEADS * LEN * LEN * 2 + LEN * D * 8,
             transcendentals=HEADS * LEN * LEN),
@@ -124,7 +124,7 @@
         in_specs=[column, column, column, pl.BlockSpec((1, 2, LEN, LEN), lambda p: (sequence, p, 0, 0)), column],
         out_specs=[column] * 3,
         out_shape=[jax.ShapeDtypeStruct((rows, D), LOW)] * 3,
-        compiler_params=pltpu.CompilerParams(vmem_limit_bytes=32 * MIB),
+        compiler_params=pltpu.CompilerParams(vmem_limit_bytes=GRANT),
         cost_estimate=pl.CostEstimate(
             flops=12 * HEADS * LEN * LEN * 256, bytes_accessed=HEADS * LEN * LEN * 2 + LEN * D * 14, transcendentals=0),
         name="attend_back",
@@ -190,7 +190,7 @@
             jax.ShapeDtypeStruct((rows, D), FULL), jax.ShapeDtypeStruct((rows, 1), FULL),
             jax.ShapeDtypeStruct((rows, D), LOW),
         ],
-        compiler_params=pltpu.CompilerParams(vmem_limit_bytes=32 * MIB),
+        compiler_params=pltpu.CompilerParams(vmem_limit_bytes=GRANT),
         cost_estimate=pl.CostEstimate(flops=4 * rows * D * D, bytes_accessed=rows * D * 10 + D * D * 2, transcendentals=0),
         name="branch",
     )(attn_rows, tokens, w_out, b_out, gain, shift)
@@ -216,7 +216,7 @@
         in_specs=[fixed(first_low), chunk(D), chunk(1)],
         out_specs=[chunk(rows), chunk(rows)],
         out_shape=[jax.ShapeDtypeStruct((rows, width), LOW)] * 2,
-        compiler_params=pltpu.CompilerParams(vmem_limit_bytes=32 * MIB),
+        compiler_params=pltpu.CompilerParams(vmem_limit_bytes=GRANT),
         cost_estimate=pl.CostEstimate(
             flops=6 * rows * D * WIDE * (last - first), bytes_accessed=WIDE * (last - first) * (D * 2 + rows * 4),
             transcendentals=rows * WIDE * (last - first)),
@@ -270,7 +270,7 @@
             jax.ShapeDtypeStruct((rows, D), LOW), jax.ShapeDtypeStruct((3, D), FULL),
         ],
         scratch_shapes=[pltpu.VMEM((rows, D), FULL)],
-        compiler_params=pltpu.CompilerParams(vmem_limit_bytes=40 * MIB),
+        compiler_params=pltpu.CompilerParams(vmem_limit_bytes=GRANT),
         cost_estimate=pl.CostEstimate(
             flops=2 * rows * D * width, bytes_accessed=rows * (D * 14 + width * 2) + D * width * 2, transcendentals=0),
         name="fall",
@@ -309,7 +309,7 @@
             jax.ShapeDtypeStruct((rows, width), LOW), jax.ShapeDtypeStruct((1, width), FULL),
             jax.ShapeDtypeStruct((rows, D), FULL),
         ],
-        compiler_params=pltpu.CompilerParams(vmem_limit_bytes=40 * MIB),
+        compiler_params=pltpu.CompilerParams(vmem_limit_bytes=GRANT),
         cost_estimate=pl.CostEstimate(
             flops=6 * rows * D * WIDE * (last - first), bytes_accessed=WIDE * (last - first) * (D * 4 + rows * 4) + rows * D * 10,
             transcendentals=0),
@@ -349,59 +349,53 @@
             jax.ShapeDtypeStruct((rows, D), FULL), jax.ShapeDtypeStruct((rows, D), LOW),
             jax.ShapeDtypeStruct((rows, D), LOW), jax.ShapeDtypeStruct((3, D), FULL),
         ],
-        compiler_params=pltpu.CompilerParams(vmem_limit_bytes=32 * MIB),
+        compiler_params=pltpu.CompilerParams(vmem_limit_bytes=GRANT),
         cost_estimate=pl.CostEstimate(flops=4 * rows * D * D, bytes_accessed=rows * D * 16 + D * D * 2, transcendentals=0),
         name="resid_back",
     )(d_first, normed, inverse, gain, w_out)
 
 
-def tall_kernel(cut, left_ref, right_ref, keep1_ref, send1_ref, keep2_ref, send2_ref, product):
-    core = lax.axis_index("dp") % 2
+def tall_kernel(left_ref, right_ref, keep_ref, send_ref, product):
+    core = lax.axis_index("dp") & 1
     product[...] = dot_tn(left_ref[...], right_ref[...]).astype(LOW).reshape(product.shape)
-    for keep, send, low, high in ((keep1_ref, send1_ref, 0, cut), (keep2_ref, send2_ref, cut, product.shape[-1])):
-        for pair in range(2):
-            keep[pair] = product[pair, core, :, low:high]
-            send[pair] = product[pair, 1 - core, :, low:high]
-
-
-def outer_tall(left, right, cut, count):
+    for pair in range(2):
+        keep_ref[pair] = product[pair, core]
+        send_ref[pair] = product[pair, 1 - core]
+
+
+def outer_tall(left, right, count):
     rows, width = left.shape
     cols, part = right.shape[1], width // count
-    out = lambda size: pl.BlockSpec((2, part, size), lambda i: (i, 0, 0))
-    shape = lambda size: jax.ShapeDtypeStruct((count // 2, part, size), LOW)
-    sizes = (cut, cut, cols - cut, cols - cut)
+    out = pl.BlockSpec((2, part, cols), lambda i: (i, 0, 0))
     return pl.pallas_call(
-        functools.partial(tall_kernel, cut),
+        tall_kernel,
         grid=(count // 4,),
         in_specs=[pl.BlockSpec((rows, 4 * part), lambda i: (0, i)), fixed(right)],
-        out_specs=[out(size) for size in sizes],
-        out_shape=[shape(size) for size in sizes],
+        out_specs=[out, out],
+        out_shape=[jax.ShapeDtypeStruct((count // 2, part, cols), LOW)] * 2,
         scratch_shapes=[pltpu.VMEM((2, 2, part, cols), LOW)],
-        compiler_params=pltpu.CompilerParams(vmem_limit_bytes=32 * MIB),
+        compiler_params=pltpu.CompilerParams(vmem_limit_bytes=GRANT),
         cost_estimate=pl.CostEstimate(
             flops=2 * rows * width * cols, bytes_accessed=2 * (rows * (width + cols) + width * cols), transcendentals=0),
         name="outer_tall",
     )(left, right)
 
 
-def wide_kernel(starts, cuts, *refs):
+def wide_kernel(starts, *refs):
     pairs = len(starts) - 1
-    lefts, rights, outs, product = refs[:pairs], refs[pairs : 2 * pairs], refs[2 * pairs : -1], refs[-1]
+    lefts, rights, (keep, send, product) = refs[:pairs], refs[pairs : 2 * pairs], refs[2 * pairs :]
     step = pl.program_id(0)
-    core = lax.axis_index("dp") % 2
+    core = lax.axis_index("dp") & 1
     for left, right, low, high in zip(lefts, rights, starts, starts[1:]):
         @pl.when((step >= low) & (step < high))
         def _():
             product[...] = dot_tn(left[...], right[...]).astype(LOW).reshape(product.shape)
 
-    for keep, send, low, high in zip(outs[::2], outs[1::2], cuts, cuts[1:]):
-        @pl.when((step >= low) & (step < high))
-        def _():
-            keep[...] = product[:, core]
-            send[...] = product[:, 1 - core]
-
-
-def outer_wide(lefts, rights, cuts, count):
+    keep[...] = product[:, core]
+    send[...] = product[:, 1 - core]
+
+
+def outer_wide(lefts, rights, count):
     rows, height = lefts[0].shape
     part = height // count
     starts = [0]
@@ -412,18 +406,15 @@
     def strip(low, high):
         return pl.BlockSpec((rows, WIDE), lambda i: (0, jnp.clip(i - low, 0, high - low - 1)))
 
-    def out(low, high):
-        return pl.BlockSpec((count // 2, part, WIDE), lambda i: (0, 0, jnp.clip(i - low, 0, high - low - 1)))
-
-    ranges = [part_range for part_range in zip(cuts, cuts[1:]) for _ in range(2)]
+    out = pl.BlockSpec((count // 2, part, WIDE), lambda i: (0, 0, i))
     return pl.pallas_call(
-        functools.partial(wide_kernel, starts, cuts),
+        functools.partial(wide_kernel, starts),
         grid=(total,),
         in_specs=[fixed(left) for left in lefts] + [strip(low, high) for low, high in zip(starts, starts[1:])],
-        out_specs=[out(low, high) for low, high in ranges],
-        out_shape=[jax.ShapeDtypeStruct((count // 2, part, WIDE * (high - low)), LOW) for low, high in ranges],
+        out_specs=[out, out],
+        out_shape=[jax.ShapeDtypeStruct((count // 2, part, WIDE * total), LOW)] * 2,
         scratch_shapes=[pltpu.VMEM((count // 2, 2, part, WIDE), LOW)],
-        compiler_params=pltpu.CompilerParams(vmem_limit_bytes=32 * MIB),
+        compiler_params=pltpu.CompilerParams(vmem_limit_bytes=GRANT),
         cost_estimate=pl.CostEstimate(
             flops=2 * rows * height * WIDE * total,
             bytes_accessed=2 * (rows * (height * len(lefts) + WIDE * total) + height * WIDE * total), transcendentals=0),
@@ -434,17 +425,14 @@
 FLIPS = {"c": 1, "x": 2, "y": 4}
 TWO_WAYS = ("zyx", "xzy")
 EARLY_WAYS = ("zyx", "xzy", "yzx")
-THREE_WAYS = ("zyx", "xzy", "yxz")
-
-
-def ring_pairs(count):
-    return [(place, (place + 8) % count) for place in range(count)]
+GRANT = 58 * 1024 * 1024
 
 
 def hop(array, dim, count):
-    if dim == "z":
-        return lax.ppermute(array, "dp", ring_pairs(count))
-    return lax.ppermute(array, "dp", [(place, place ^ FLIPS[dim]) for place in range(count)])
+    if dim in FLIPS:
+        return lax.ppermute(array, "dp", [(place, place ^ FLIPS[dim]) for place in range(count)])
+    step = 8 * (1 if dim == "z" else dim)
+    return lax.ppermute(array, "dp", [(place, (place + step) % count) for place in range(count)])
 
 
 def after(value, *earlier):
@@ -461,19 +449,26 @@
     }
 
 
-def gather_part(shard, order, count, first=(), second=(), third=()):
+def gather_steps(shard, order, count):
     stack = shard[None]
-    mark = None
-    for dim, earlier in zip(order[:2], (first, second)):
-        stack = after(stack, *earlier)
+    gate = yield
+    for dim in order[:2]:
         pieces = [stack]
         for _ in range(count // 8 - 1 if dim == "z" else 1):
-            pieces.append(hop(pieces[-1], dim, count))
+            pieces.append(hop(after(pieces[-1], *gate), dim, count))
+            gate = yield pieces[-1]
         stack = jnp.concatenate(pieces, axis=0)
-        if dim == "z":
-            mark = pieces[-1]
-    across = hop(after(stack, *third), order[2], count)
-    return (stack, across, hop(stack, "c", count), hop(across, "c", count)), mark
+    across = hop(after(stack, *gate), order[2], count)
+    gate = yield across
+    yield (stack, across, hop(after(stack, *gate), "c", count), hop(after(across, *gate), "c", count))
+
+
+def gather_part(shard, order, count):
+    steps = gather_steps(shard, order, count)
+    next(steps)
+    for _ in range(6):
+        last = steps.send(())
+    return last
 
 
 def place_kernel(count, orders, cuts, bases, rows, *refs):
@@ -509,7 +504,7 @@
         in_specs=[pl.BlockSpec((1, rows, piece.shape[2]), lambda i: (i, 0, 0)) for piece in pieces],
         out_specs=[held(size, width) for width in widths],
         out_shape=[jax.ShapeDtypeStruct((size, width), LOW) for width in widths],
-        compiler_params=pltpu.CompilerParams(vmem_limit_bytes=32 * MIB),
+        compiler_params=pltpu.CompilerParams(vmem_limit_bytes=GRANT),
         cost_estimate=pl.CostEstimate(flops=0, bytes_accessed=4 * size * bases[-1], transcendentals=0),
         name="place",
     )(*pieces)
@@ -521,31 +516,32 @@
     return [full[:, low:high] for low, high in zip(bases, bases[1:])]
 
 
-def gather_all(first, second, third, wide, count):
-    first_widths, second_widths, third_widths = (D, D, D, 128), (wide, D), (D,)
+def gather_early(shard, widths, count):
     if count != 32:
-        return whole_arrays(first, first_widths) + whole_arrays(second, second_widths) + whole_arrays(third, third_widths)
-
-    def pieces_of(shard, cuts, orders, ties):
-        pieces, marks = [], []
-        for order, low, high, tie in zip(orders, cuts, cuts[1:], ties):
-            four, mark = gather_part(shard[:, low:high], order, count, *tie)
-            pieces.append(four)
-            marks.append(mark)
-        return pieces, marks
-
-    cuts = (0, D, 2 * D, 3 * D + 128)
-    early, marks = pieces_of(first, cuts, EARLY_WAYS, [()] * 3)
-    placed_first = place(sum(early, ()), EARLY_WAYS, cuts, first_widths, first.shape[0], count)
-    cuts = (0, 3328, wide + D)
-    ties = [((marks[0],), (early[0][1],)), ((marks[1],), (), (early[1][1],))]
-    pieces, _ = pieces_of(second, cuts, TWO_WAYS, ties)
-    placed_second = place(sum(pieces, ()), TWO_WAYS, cuts, second_widths, second.shape[0], count)
-    cuts = (0, 640, D)
-    ties = [((placed_first[0],),), ((placed_first[0],),)]
-    pieces, _ = pieces_of(third, cuts, TWO_WAYS, ties)
-    placed_third = place(sum(pieces, ()), TWO_WAYS, cuts, third_widths, third.shape[0], count)
-    return list(placed_first) + list(placed_second) + list(placed_third)
+        return whole_arrays(shard, widths)
+    cuts = (0, D, 2 * D, sum(widths))
+    pieces = ()
+    for order, low, high in zip(EARLY_WAYS, cuts, cuts[1:]):
+        pieces += tuple(gather_part(shard[:, low:high], order, count))
+    return place(pieces, EARLY_WAYS, cuts, widths, shard.shape[0], count)
+
+
+class Gathering:
+    def __init__(self, shard, cut, count):
+        self.count, self.cuts, self.rows = count, (0, cut, shard.shape[1]), shard.shape[0]
+        self.steps = [
+            gather_steps(shard[:, low:high], order, count)
+            for order, low, high in zip(TWO_WAYS, self.cuts, self.cuts[1:])
+        ]
+        self.last = None
+
+    def move(self, *gate):
+        if self.last is None:
+            [next(steps) for steps in self.steps]
+        self.last = [steps.send(gate) for steps in self.steps]
+
+    def result(self):
+        return place(self.last[0] + self.last[1], TWO_WAYS, self.cuts, (self.cuts[-1],), self.rows, self.count)[0]
 
 
 def add_low(left_side, right_side, kind=LOW):
@@ -556,55 +552,110 @@
     return lax.dynamic_index_in_dim(blocks, index, axis, keepdims=False, allow_negative_indices=False)
 
 
-def scatter_steps(keep, send, order, count):
-    ring = count // 8
+def split_kernel(cut, keep_ref, came_ref, keep1_ref, send1_ref, keep2_ref, send2_ref):
     mine = mine_of()
-    dims = ["z", "y", "x"]
-    shape = (ring, 2, 2) + keep.shape[1:]
-
-    def hopped(array, dim, gate):
-        return after(hop(array, dim, count), *gate)
-
-    gate = yield send
-    held_sums = [keep.reshape(shape), hopped(send, "c", gate).reshape(shape)]
-
-    def pick(dim, index):
-        axis = dims.index(dim)
-        return add_low(take(held_sums[0], axis, index), take(held_sums[1], axis, index))
-
-    for dim in order[::-1]:
-        own = mine[dim]
-        if dim == "z":
-            moving = pick("z", (own + ring - 1) & (ring - 1))
-            for step in range(2, ring + 1):
-                gate = yield moving
-                moving = hopped(moving, "z", gate)
-                if step < ring:
-                    moving = add_low(moving, pick("z", (own + ring - step) & (ring - 1)))
+    for side in range(2):
+        for keep, send, dim, cols in (
+            (keep1_ref, send1_ref, "x", slice(0, cut)),
+            (keep2_ref, send2_ref, "y", slice(cut, None)),
+        ):
+            for out, index in ((keep, mine[dim]), (send, 1 - mine[dim])):
+                where = (0, side, index, slice(None), cols) if dim == "x" else (0, index, side, slice(None), cols)
+                out[0, side] = add_low(keep_ref[where], came_ref[where])
+
+
+def turn_kernel(keep1_ref, came1_ref, keep2_ref, came2_ref, keep3_ref, send3_ref, keep4_ref, send4_ref):
+    mine = mine_of()
+    for kept, came, keep, send, dim in (
+        (keep1_ref, came1_ref, keep3_ref, send3_ref, "y"),
+        (keep2_ref, came2_ref, keep4_ref, send4_ref, "x"),
+    ):
+        for out, index in ((keep, mine[dim]), (send, 1 - mine[dim])):
+            out[...] = add_low(kept[:, index], came[:, index])
+
+
+def tower_kernel(cut, keep3_ref, came3_ref, keep4_ref, came4_ref, *outs):
+    own = mine_of()["z"]
+    ring = keep3_ref.shape[0]
+    for distance, out in enumerate(outs):
+        index = lax.rem(own + distance, ring)
+        out[:, :cut] = add_low(keep3_ref[index], came3_ref[index])
+        out[:, cut:] = add_low(keep4_ref[index], came4_ref[index])
+
+
+def local_kernel(kernel, name, outs, grid, in_specs, out_specs, operands):
+    size = sum(array.size * array.dtype.itemsize for array in operands)
+    return pl.pallas_call(
+        kernel,
+        grid=grid,
+        in_specs=in_specs,
+        out_specs=out_specs,
+        out_shape=outs,
+        compiler_params=pltpu.CompilerParams(vmem_limit_bytes=GRANT),
+        cost_estimate=pl.CostEstimate(flops=0, bytes_accessed=2 * size, transcendentals=0),
+        name=name,
+    )(*operands)
+
+
+class Sums:
+    def __init__(self, keep, send, count):
+        self.count, self.ring = count, count // 8
+        self.rows, self.cols = keep.shape[1:]
+        self.cut = self.cols // 2
+        self.stage = 0
+        self.keeps, self.sends, self.dims = [keep], [send], ["c"]
+
+    def start(self):
+        self.came = [hop(send, dim, self.count) for send, dim in zip(self.sends, self.dims)]
+        return self.sends
+
+    def move(self, *gate):
+        came = [after(array, *gate) for array in self.came]
+        ring, rows, cut, rest = self.ring, self.rows, self.cut, self.cols - self.cut
+        self.stage += 1
+        if self.stage == 1:
+            whole = lambda array: array.reshape(ring, 2, 2, rows, self.cols)
+            block = pl.BlockSpec((1, 2, 2, rows, self.cols), lambda i: (i, 0, 0, 0, 0))
+            widths = (cut, cut, rest, rest)
+            self.pairs(local_kernel(
+                functools.partial(split_kernel, cut), "split",
+                [jax.ShapeDtypeStruct((ring, 2, rows, width), LOW) for width in widths], (ring,), [block] * 2,
+                [pl.BlockSpec((1, 2, rows, width), lambda i: (i, 0, 0, 0)) for width in widths],
+                [whole(self.keeps[0]), whole(came[0])],
+            ), ["x", "y"])
+        elif self.stage == 2:
+            operands = [self.keeps[0], came[0], self.keeps[1], came[1]]
+            self.pairs(local_kernel(
+                turn_kernel, "turn",
+                [jax.ShapeDtypeStruct((ring, rows, width), LOW) for width in (cut, cut, rest, rest)], (ring,),
+                [pl.BlockSpec((1,) + array.shape[1:], lambda i: (i, 0, 0, 0)) for array in operands],
+                [pl.BlockSpec((1, rows, width), lambda i: (i, 0, 0)) for width in (cut, cut, rest, rest)],
+                operands,
+            ), ["y", "x"])
+        elif self.stage == 3:
+            operands = [self.keeps[0], came[0], self.keeps[1], came[1]]
+            outs = local_kernel(
+                functools.partial(tower_kernel, cut), "tower",
+                [jax.ShapeDtypeStruct((rows, self.cols), LOW)] * ring, (1,),
+                [fixed(array) for array in operands], [held(rows, self.cols)] * ring, operands,
+            )
+            self.keeps, self.sends, self.dims = list(outs[:1]), list(outs[1:]), list(range(1, ring))
         else:
-            moving = pick(dim, 1 - own)
-            gate = yield moving
-            moving = hopped(moving, dim, gate)
-        held_sums = [pick(dim, own), moving]
-        dims.remove(dim)
-    yield add_low(held_sums[0], held_sums[1], FULL)
-
-
-class Sums:
-    def __init__(self, parts, orders, count):
-        pairs = zip(parts[::2], parts[1::2])
-        self.chains = [scatter_steps(keep, send, order, count) for (keep, send), order in zip(pairs, orders)]
-        self.last = [next(chain) for chain in self.chains]
-
-    def move(self, which, *gate):
-        self.last[which] = self.chains[which].send(gate)
-        return self.last[which]
-
-    def results(self):
-        for which, chain in enumerate(self.chains):
-            while self.last[which].dtype != FULL:
-                self.move(which)
-        return self.last
+            self.total = self.keeps[0].astype(FULL)
+            for array in came:
+                self.total = self.total + array.astype(FULL)
+            return [self.total]
+        return self.start()
+
+    def pairs(self, arrays, dims):
+        self.keeps, self.sends, self.dims = [arrays[0], arrays[2]], [arrays[1], arrays[3]], dims
+
+
+def sum_everywhere(rows, count):
+    for dim in "cxy":
+        rows = rows + hop(rows, dim, count)
+    shifts = [hop(rows, distance, count) for distance in range(1, count // 8)]
+    return functools.reduce(jnp.add, shifts, rows)
 
 
 def local(
@@ -629,110 +680,117 @@
     count = D // w_query.shape[0]
     part = D // count
     wide = w_up.shape[1]
-    vectors = (b_query, b_value, b_out, b_down, gain_attn, shift_attn, gain_ffn, shift_ffn, b_up)
-    packed = jnp.concatenate(vectors)
-    packed = jnp.pad(packed, (0, part * 128 - packed.shape[0])).reshape(part, 128)
-    w_query, w_key, w_value, packed, w_up, w_out, w_down = gather_all(
-        jnp.concatenate([w_query, w_key, w_value, packed], axis=1),
-        jnp.concatenate([w_up, w_out], axis=1),
-        w_down,
-        wide,
-        count,
+    custom = count == 32
+    small = (b_query, b_value, b_out, b_down, gain_attn, shift_attn, gain_ffn, shift_ffn)
+    packed = sum(
+        jnp.pad(array[None], ((row, 15 - row), (0, 128 - array.shape[0]))) for row, array in enumerate(small + (b_up,))
     )
-    flat = packed.reshape(count, part * 128)
-    vector = lambda col: flat[:, part * col : part * col + part].reshape(1, D).astype(FULL)
+    height = max(part, 16)
+    tops = [jnp.pad(array, ((0, height - part), (0, 0))) for array in (w_query, w_key, w_value)]
+    early = jnp.concatenate(tops + [jnp.pad(packed, ((0, height - 16), (0, 0)))], axis=1)
+    w_query, w_key, w_value, packed = gather_early(early, (D, D, D, 128), count)
+    if height > part:
+        w_query, w_key, w_value = [
+            array.reshape(count, height, D)[:, :part].reshape(D, D) for array in (w_query, w_key, w_value)
+        ]
+    w_up = lax.all_gather(w_up, "dp", axis=0, tiled=True)
+    w_out = lax.all_gather(w_out, "dp", axis=0, tiled=True)
+    packed = packed.reshape(count, height, 128)
+    vector = lambda row: packed[:, row, :part].reshape(1, D).astype(FULL)
     b_query, b_value, b_out, b_down, gain_attn, shift_attn, gain_ffn, shift_ffn = map(vector, range(8))
-    b_up = flat[:, 8 * part : 8 * part + wide // count].reshape(1, wide).astype(FULL)
+    b_up = packed[:, 8, : wide // count].reshape(1, wide).astype(FULL)
     chunks = wide // WIDE
     sequences = tokens.shape[0] // LEN
 
-    queries = (dot_nn(tokens, w_query) + b_query).astype(LOW)
-    keys = dot_nn(tokens, w_key).astype(LOW)
-    values = (dot_nn(tokens, w_value) + b_value).astype(LOW)
+    def under(value, gather, gate):
+        if not custom:
+            return value
+        earlier = gather.last or ()
+        gather.move(gate)
+        return after(value, *earlier)
+
+    down_gather = Gathering(w_down, D // 2, count) if custom else None
+    tokens_in = under(tokens, down_gather, w_query)
+    queries = (dot_nn(tokens_in, w_query) + b_query).astype(LOW)
+    tokens_in = under(tokens, down_gather, queries)
+    keys = dot_nn(tokens_in, w_key).astype(LOW)
+    tokens_in = under(tokens, down_gather, keys)
+    values = (dot_nn(tokens_in, w_value) + b_value).astype(LOW)
+    values = under(values, down_gather, values)
     seen = ()
     for sequence in range(sequences):
         seen = attend(queries, keys, values, sequence, seen)
+        if sequence == 0:
+            values = under(values, down_gather, seen[1])
     probs, attn_rows = seen
     normed, inverse, first_low = branch(attn_rows, tokens, w_out, b_out, gain_attn, shift_attn)
     half = widen(first_low, w_up, b_up, 0, chunks // 2)
+    first_low = under(first_low, down_gather, half[0])
     hidden, slope = widen(first_low, w_up, b_up, chunks // 2, chunks, half)
+    w_down = down_gather.result() if custom else lax.all_gather(w_down, "dp", axis=0, tiled=True)
     result, second, d_ffn, sums_ffn = fall(
         hidden, w_down, normed, cotangent, b_down, gain_attn, shift_attn, gain_ffn, shift_ffn
     )
 
-    custom = count == 32
-
-    def then(value, gate, *moves):
-        if not custom:
-            return value
-        return after(value, *[sums.move(which, gate) for sums, which in moves])
-
     if custom:
-        down = Sums(outer_tall(hidden, d_ffn, 640, count), TWO_WAYS, count)
-        second = after(second, *down.last)
+        down = Sums(*outer_tall(hidden, d_ffn, count), count)
+        second = after(second, *down.start())
     pre_1, wide_1, d_first = narrow(d_ffn, slope, w_down, w_up, second, 0, 2)
-    d_first = then(d_first, wide_1, (down, 0), (down, 1)) if custom else d_first
+    if custom:
+        d_first = after(d_first, *down.move(wide_1))
     pre_2, wide_2, d_first = narrow(d_ffn, slope, w_down, w_up, d_first, 2, 5)
-    if custom:
-        parts = outer_wide([first_low, first_low], [pre_1, pre_2], (0, 3, 5), count)
-        up_1 = Sums(parts, TWO_WAYS, count)
-        d_first = after(then(d_first, parts[2], (down, 1)), *up_1.last)
     pre_3, wide_3, d_first = narrow(d_ffn, slope, w_down, w_up, d_first, 5, chunks)
     if custom:
-        d_first = then(d_first, wide_3, (down, 0), (down, 1), (up_1, 0), (up_1, 1))
+        d_first = after(d_first, *down.move(wide_3))
     d_resid, d_branch, d_attn, sums_attn = resid_back(d_first, normed, inverse, gain_attn, w_out)
     if custom:
-        d_branch = then(d_branch, sums_attn, (down, 1))
-        parts = outer_wide([first_low, attn_rows], [pre_3, d_branch], (0, 3, 5), count)
-        up_2 = Sums(parts, TWO_WAYS, count)
-        d_attn = after(then(d_attn, parts[2], (down, 0), (down, 1)), *up_2.last)
+        up = Sums(*outer_wide([first_low] * 3 + [attn_rows], [pre_1, pre_2, pre_3, d_branch], count), count)
+        d_attn = after(d_attn, *up.start())
+        d_attn = after(d_attn, *down.move(*up.keeps))
     seen = attend_back(queries, keys, values, probs, d_attn, 0)
     if custom:
-        d_attn = then(
-            d_attn, seen[0], (down, 0), (down, 1), (up_1, 0), (up_1, 1), (up_2, 0), (up_2, 1)
-        )
+        d_attn = after(d_attn, *up.move(seen[0]))
     for sequence in range(1, sequences):
         seen = attend_back(queries, keys, values, probs, d_attn, sequence, seen)
     d_queries, d_keys, d_values = seen
     if custom:
-        d_queries = then(d_queries, d_values, (down, 0), (up_1, 0), (up_1, 1), (up_2, 1))
-    column_sum = lambda rows: jnp.sum(rows.astype(FULL), axis=0)
-    sums = (
-        column_sum(d_queries), column_sum(d_values), sums_attn[2], sums_ffn[2],
-        sums_attn[0], sums_attn[1], sums_ffn[0], sums_ffn[1],
-        jnp.concatenate([wide_1[0], wide_2[0], wide_3[0]]),
-    )
-    packed = jnp.concatenate([total.astype(LOW).reshape(count, -1) for total in sums], axis=1)
-    packed = jnp.pad(packed, ((0, 0), (0, part * 128 - packed.shape[1]))).reshape(count // 2, 2, part, 128)
-    if custom:
-        parts = outer_wide([tokens, tokens, tokens], [d_queries, d_keys, d_values], (0, 2, 4, 6), count)
-        core = mine_of()["c"]
-        keep = jnp.concatenate([parts[4], take(packed, 1, core)], axis=-1)
-        send = jnp.concatenate([parts[5], take(packed, 1, 1 - core)], axis=-1)
-        first = Sums(list(parts[:4]) + [keep, send], THREE_WAYS, count)
-        d_queries = after(d_queries, *first.last)
-        d_queries = then(d_queries, parts[0], (down, 0), (up_1, 0), (up_1, 1), (up_2, 0), (up_2, 1))
+        first = Sums(*outer_wide([tokens] * 3, [d_queries, d_keys, d_values], count), count)
+        d_queries = after(d_queries, *first.start())
+        d_queries = after(d_queries, *down.move(*first.keeps))
+        d_queries = after(d_queries, *up.move(*first.keeps))
+    column_sum = lambda rows: jnp.sum(rows.astype(FULL), axis=0, keepdims=True)
+    sums = jnp.concatenate([
+        column_sum(d_queries), column_sum(d_values), sums_attn[2:], sums_ffn[2:], sums_attn[:2], sums_ffn[:2],
+        jnp.concatenate([wide_1, wide_2, wide_3], axis=1).reshape(-1, D),
+    ], axis=0)
     grad_rows = d_resid + dot_nt(d_queries, w_query)
     if custom:
-        grad_rows = then(grad_rows, grad_rows, (first, 0), (first, 1), (first, 2))
-    grad_rows = grad_rows + dot_nt(d_keys, w_key) + dot_nt(d_values, w_value)
+        grad_rows = after(grad_rows, *first.move(grad_rows))
+    grad_rows = (grad_rows + dot_nt(d_keys, w_key) + dot_nt(d_values, w_value)).astype(LOW)
 
     if custom:
-        grad_rows = grad_rows.astype(LOW)
-        d_w_down = jnp.concatenate(down.results(), axis=-1)
-        d_w_up = jnp.concatenate(up_1.results() + up_2.results()[:1], axis=-1)
-        d_w_out = up_2.results()[1]
-        d_w_query, d_w_key, last = first.results()
-        d_w_value, flat = last[:, :D], last[:, D:].reshape(-1)
+        up.move(grad_rows)
+        first.move(grad_rows)
+        up.move()
+        first.move()
+        first.move()
+        d_w_down, second, first = down.total, up.total, first.total
+        d_w_up, d_w_out = second[:, :wide], second[:, wide:]
+        d_w_query, d_w_key, d_w_value = first[:, :D], first[:, D : 2 * D], first[:, 2 * D :]
+        sums = sum_everywhere(sums, count)
     else:
         total = lambda grad: lax.psum_scatter(grad.astype(LOW), "dp", scatter_dimension=0, tiled=True).astype(FULL)
-        grad_rows = grad_rows.astype(LOW)
         d_w_down = total(dot_tn(hidden, d_ffn))
         d_w_up = total(jnp.concatenate([dot_tn(first_low, pre) for pre in (pre_1, pre_2, pre_3)], axis=1))
         d_w_out = total(dot_tn(attn_rows, d_branch))
         d_w_query, d_w_key, d_w_value = [total(dot_tn(tokens, grad)) for grad in (d_queries, d_keys, d_values)]
-        flat = total(packed.reshape(D, 128)).reshape(-1)
-    vector = lambda col: flat[part * col : part * col + part]
+        sums = lax.psum(sums, "dp")
+    me = lax.axis_index("dp")
+    own = lax.dynamic_slice_in_dim(sums[:8], me * part, part, axis=1, allow_negative_indices=False)
+    vector = lambda row: own[row]
+    d_b_up = lax.dynamic_slice_in_dim(
+        sums[8:].reshape(-1), me * (wide // count), wide // count, allow_negative_indices=False
+    )
     return (
         result,
         grad_rows,
@@ -745,7 +803,7 @@
         vector(0),
         vector(1),
         vector(2),
-        flat[8 * part : 8 * part + wide // count],
+        d_b_up,
         vector(3),
         vector(4),
         vector(5),

time: 636 us -> 599 us (0.942)
  local copies, waits for them, and re-layouts: 114 us -> 24.6 us
  Pallas kernels: 194 us -> 283 us
  other arithmetic: 58.1 us -> 11.7 us
  waiting for transfers between devices: 169 us -> 150 us
  between operations: 2.68 us -> 15 us
  starting transfers between devices: 60.1 us -> 70.4 us
  matrix products: 27.2 us -> 34.9 us
    unnamed x222 -> x106, local copies, waits for them, and re-layouts: 81.2 us -> 14.5 us
    pallas_call x4 -> x12, Pallas kernels: 38.1 us -> 88.5 us  [the longest x9 38.5 us: local_kernel(): pl.pallas_call(kernel, grid=grid, in_specs=in_specs, out_specs=out_specs,...]
    ppermute x48 -> x27, waiting for transfers between devices: 141 us -> 95.3 us  [hop(): lax.ppermute(array, 'dp', [(place, (place + step) % count) for place in r...]
    convert_element_type x53 -> x6, other arithmetic: 40 us -> 1.64 us  [the longest x5 1.03 us: local(): vector = lambda row: packed[:, row, :part].reshape(1, D).astype(FULL)]
    ppermute x55 -> x38, waiting for transfers between devices: 28.9 us -> 53.8 us  [hop(): lax.ppermute(array, 'dp', [(place, place ^ FLIPS[dim]) for place in range...]
    ppermute x48 -> x27, starting transfers between devices: 23.8 us -> 41.8 us  [hop(): lax.ppermute(array, 'dp', [(place, (place + step) % count) for place in r...]
    pallas_call x3, Pallas kernels: 34.8 us -> 47.5 us  [narrow(): pl.pallas_call(narrow_kernel, grid=(last - first,), in_specs=[fixed(d_ffn...]
    concatenate x9 -> x6, local copies, waits for them, and re-layouts: 11.8 us -> 0.17 us  [the longest x5 0.1 us: gather_steps(): stack = jnp.concatenate(pieces, axis=0)]
  transfers between devices with their start and end apart: 103 -> 67, of which waited for: 36 -> 24; matrix products, arithmetic and copies ran while one was open for 21% -> 10% of each run, Pallas kernels for 26% -> 29%
where the time goes in v4:
time: 599 us; the launch traced here: 590 us
  Pallas kernels  283 us (47%)
  waiting for transfers between devices  150 us (25%)
  starting transfers between devices  70.4 us (12%)
  matrix products  34.9 us (6%)
  local copies, waits for them, and re-layouts  24.6 us (4%)
  between operations  15 us (3%)
  other arithmetic  11.7 us (2%)
    ppermute x27, waiting for transfers between devices, hop(): lax.ppermute(array, 'dp', [(place, (place + step) % count) for place in r...  95.3 us
    pallas_call x6, Pallas kernels, continued(): return lambda *operands: call(*operands, *before)  89.7 us
    ppermute x38, waiting for transfers between devices, hop(): lax.ppermute(array, 'dp', [(place, place ^ FLIPS[dim]) for place in range...  53.8 us
    pallas_call x3, Pallas kernels, narrow(): pl.pallas_call(narrow_kernel, grid=(last - first,), in_specs=[fixed(d_ffn...  47.5 us
    ppermute x27, starting transfers between devices, hop(): lax.ppermute(array, 'dp', [(place, (place + step) % count) for place in r...  41.8 us
    pallas_call x9, Pallas kernels, local_kernel(): pl.pallas_call(kernel, grid=grid, in_specs=in_specs, out_specs=out_specs,...  38.5 us
    pallas_call x2, Pallas kernels, outer_wide(): pl.pallas_call(functools.partial(wide_kernel, starts), grid=(total,), in_...  35.2 us
    ppermute x38, starting transfers between devices, hop(): lax.ppermute(array, 'dp', [(place, place ^ FLIPS[dim]) for place in range...  28.6 us
  transfers between devices with their start and end apart: 67, of which 24 were waited for; matrix products, arithmetic and copies ran while one was open for 10% of the time, Pallas kernels for 29%

profile of v4, /device:TPU:0, one launch (start us, length us, event | category | flops | bytes accessed | tf_op | source)
XLA Modules:
  0.0 589.7 jit_solution(312240473871634200)
XLA Ops:
  60.7 14.4 %collective-permute-done.18.refs_9_ = bf16[8,32,1152]{2,1,0:T(8,128)(2,1)S(1)} collective-permute-done((bf16[8,32,1152]{2,1,0:T(8,128)(2,1)S(1)}, bf16[8,32,1152]{2,1,0:T(8,128)(2,1)S(1)}, u32[]{:S(2)}, u32[]{:S(2)}) %collective-permute-start.18) | collective-permute-done | bytes 589856 | tf_op jit(solution)/shard_map/ppermute | solution.py:433
  115.5 13.5 %collective-permute-done.23 = bf16[1,128,512]{2,1,0:T(8,128)(2,1)S(1)} collective-permute-done((bf16[1,128,512]{2,1,0:T(8,128)(2,1)S(1)}, bf16[1,128,512]{2,1,0:T(8,128)(2,1)S(1)}, u32[]{:S(2)}, u32[]{:S(2)}) %collective-permute-start.23) | collective-permute-done | bytes 131104 | tf_op jit(solution)/shard_map/ppermute | solution.py:435
  140.5 8.4 %collective-permute-done.26 = bf16[2,128,512]{2,1,0:T(8,128)(2,1)S(1)} collective-permute-done((bf16[2,128,512]{2,1,0:T(8,128)(2,1)S(1)}, bf16[2,128,512]{2,1,0:T(8,128)(2,1)S(1)}, u32[]{:S(2)}, u32[]{:S(2)}) %collective-permute-start.26) | collective-permute-done | bytes 262176 | tf_op jit(solution)/shard_map/ppermute | solution.py:435
  149.0 14.4 %attend.2 = (bf16[2,16,512,512]{3,2,1,0:T(8,128)(2,1)}, bf16[1024,1024]{1,0:T(8,128)(2,1)}) custom-call(bf16[1024,1024]{1,0:T(8,128)(2,1)} %fusion.q_ref.refs_0_, bf16[1024,1024]{1,0:T(8,128)(2,1)} %convolution_convert_fusion.k_ref.refs_1_, bf16[1024,1024]{1,0:T(8,128)(2,1)} %add_convert_fusion.1.v_ref.refs_2_), custom_call_target="tpu_custom_call" | custom-call | flops 12884901888 | bytes 12582912 | tf_op jit(solution)/shard_map/attend/pallas_call | solution.py:69
  166.5 14.3 %attend.3 = (bf16[2,16,512,512]{3,2,1,0:T(8,128)(2,1)}, bf16[1024,1024]{1,0:T(8,128)(2,1)}) custom-call(bf16[1024,1024]{1,0:T(8,128)(2,1)} %fusion.q_ref.refs_0_, bf16[1024,1024]{1,0:T(8,128)(2,1)} %convolution_convert_fusion.k_ref.refs_1_, bf16[1024,1024]{1,0:T(8,128)(2,1)} %add_convert_fusion.1.v_ref.refs_2_, ...), custom_call_target="tpu_custom_call", output_to_operand_aliasing={{0}: (3, {}), {1}: (4, {})} | custom-call | flops 12884901888 | bytes 12582912 | tf_op jit(solution)/shard_map/attend/pallas_call | solution.py:69
  180.8 8.2 %branch.1 = (f32[1024,1024]{1,0:T(8,128)}, f32[1024,1]{1,0:T(8,128)}, bf16[1024,1024]{1,0:T(8,128)(2,1)}) custom-call(bf16[1024,1024]{1,0:T(8,128)(2,1)} %get-tuple-element.160.attn_ref.refs_3_, bf16[1024,1024]{1,0:T(8,128)(2,1)} %refs_2_.1, bf16[1024,1024]{1,0:T(8,128)(2,1)} %all-gather.3.cloned.1.call-done.wout_ref, f32[1,1024]{1,0:T(1,128)} %reshape.188.bout_ref, ...), custom_call_target="tpu_custom_call" | custom-call | flops 4294967296 | bytes 12582912 | tf_op jit(solution)/shard_map/branch/pallas_call | solution.py:184
  189.0 17.1 %widen.2 = (bf16[1024,4096]{1,0:T(8,128)(2,1)}, bf16[1024,4096]{1,0:T(8,128)(2,1)}) custom-call(bf16[1024,1024]{1,0:T(8,128)(2,1)} %get-tuple-element.164.low_ref.refs_0_.refs_1_.refs_2_, bf16[1024,4096]{1,0:T(8,128)(2,1)} %all-gather.5.cloned.1.call-done.wup_ref.refs_1_, f32[1,4096]{1,0:T(1,128)} %bitcast.97), custom_call_target="tpu_custom_call" | custom-call | flops 12884901888 | bytes 12582912 | tf_op jit(solution)/shard_map/widen/pallas_call | solution.py:69
  207.2 16.8 %widen.3 = (bf16[1024,4096]{1,0:T(8,128)(2,1)}, bf16[1024,4096]{1,0:T(8,128)(2,1)}) custom-call(bf16[1024,1024]{1,0:T(8,128)(2,1)} %get-tuple-element.164.low_ref.refs_0_.refs_1_.refs_2_, bf16[1024,4096]{1,0:T(8,128)(2,1)} %all-gather.5.cloned.1.call-done.wup_ref.refs_1_, f32[1,4096]{1,0:T(1,128)} %bitcast.98, ...), custom_call_target="tpu_custom_call", output_to_operand_aliasing={{0}: (3, {}), {1}: (4, {})} | custom-call | flops 12884901888 | bytes 12582912 | tf_op jit(solution)/shard_map/widen/pallas_call | solution.py:69
  225.3 9.0 %place.3.wdown_ref = bf16[4096,1024]{1,0:T(8,128)(2,1)} custom-call(bf16[8,128,512]{2,1,0:T(8,128)(2,1)} %copy-done.6, bf16[8,128,512]{2,1,0:T(8,128)(2,1)} %collective-permute-done.29.refs_1_, bf16[8,128,512]{2,1,0:T(8,128)(2,1)} %copy-done.9, bf16[8,128,512]{2,1,0:T(8,128)(2,1)} %copy-done.10, bf16[8,128,512]{2,1,0:T(8,128)(2,1)} %copy-done.7, ...), custom_call_target="tpu_custom_call" | custom-call | bytes 16777216 | tf_op jit(solution)/shard_map/place/pallas_call | solution.py:501
  234.3 21.2 %fall.1 = (bf16[1024,1024]{1,0:T(8,128)(2,1)}, f32[1024,1024]{1,0:T(8,128)}, bf16[1024,1024]{1,0:T(8,128)(2,1)}, f32[3,1024]{1,0:T(4,128)}) custom-call(bf16[1024,4096]{1,0:T(8,128)(2,1)} %get-tuple-element.167.hidden_ref.left_ref, bf16[4096,1024]{1,0:T(8,128)(2,1)} %place.3.wdown_ref, f32[1024,1024]{1,0:T(8,128)} %get-tuple-element.172.normed_ref, ...), custom_call_target="tpu_custom_call" | custom-call | flops 8589934592 | bytes 31457280 | tf_op jit(solution)/shard_map/fall/pallas_call | solution.py:261
  255.5 14.8 %outer_tall.1 = (bf16[16,128,1024]{2,1,0:T(8,128)(2,1)}, bf16[16,128,1024]{2,1,0:T(8,128)(2,1)}) custom-call(bf16[1024,4096]{1,0:T(8,128)(2,1)} %get-tuple-element.167.hidden_ref.left_ref, bf16[1024,1024]{1,0:T(8,128)(2,1)} %get-tuple-element.174.right_ref.ffn_ref), custom_call_target="tpu_custom_call" | custom-call | flops 8589934592 | bytes 18874368 | tf_op jit(solution)/shard_map/outer_tall/pallas_call | solution.py:370
  270.3 13.5 %narrow.3 = (bf16[1024,1024]{1,0:T(8,128)(2,1)}, f32[1,1024]{1,0:T(1,128)}, f32[1024,1024]{1,0:T(8,128)}) custom-call(bf16[1024,1024]{1,0:T(8,128)(2,1)} %get-tuple-element.174.right_ref.ffn_ref, bf16[1024,4096]{1,0:T(8,128)(2,1)} %get-tuple-element.175.slope_ref, bf16[4096,1024]{1,0:T(8,128)(2,1)} %place.3.wdown_ref, ...), custom_call_target="tpu_custom_call" | custom-call | flops 6442450944 | bytes 18874368 | tf_op jit(solution)/shard_map/narrow/pallas_call | solution.py:301
  292.9 17.1 %narrow.4 = (bf16[1024,1536]{1,0:T(8,128)(2,1)}, f32[1,1536]{1,0:T(1,128)}, f32[1024,1024]{1,0:T(8,128)}) custom-call(bf16[1024,1024]{1,0:T(8,128)(2,1)} %get-tuple-element.174.right_ref.ffn_ref, bf16[1024,4096]{1,0:T(8,128)(2,1)} %get-tuple-element.175.slope_ref, bf16[4096,1024]{1,0:T(8,128)(2,1)} %place.3.wdown_ref, ...), custom_call_target="tpu_custom_call" | custom-call | flops 9663676416 | bytes 23068672 | tf_op jit(solution)/shard_map/narrow/pallas_call | solution.py:301
  310.0 16.9 %narrow.5 = (bf16[1024,1536]{1,0:T(8,128)(2,1)}, f32[1,1536]{1,0:T(1,128)}, f32[1024,1024]{1,0:T(8,128)}) custom-call(bf16[1024,1024]{1,0:T(8,128)(2,1)} %get-tuple-element.174.right_ref.ffn_ref, bf16[1024,4096]{1,0:T(8,128)(2,1)} %get-tuple-element.175.slope_ref, bf16[4096,1024]{1,0:T(8,128)(2,1)} %place.3.wdown_ref, ...), custom_call_target="tpu_custom_call" | custom-call | flops 9663676416 | bytes 23068672 | tf_op jit(solution)/shard_map/narrow/pallas_call | solution.py:301
  332.4 10.4 %resid_back.1 = (f32[1024,1024]{1,0:T(8,128)}, bf16[1024,1024]{1,0:T(8,128)(2,1)}, bf16[1024,1024]{1,0:T(8,128)(2,1)}, f32[3,1024]{1,0:T(4,128)}) custom-call(f32[1024,1024]{1,0:T(8,128)} %get-tuple-element.195.first_ref, f32[1024,1024]{1,0:T(8,128)} %get-tuple-element.172.normed_ref, f32[1024,1]{1,0:T(8,128)} %get-tuple-element.196.inverse_ref, ...), custom_call_target="tpu_custom_call" | custom-call | flops 4294967296 | bytes 18874368 | tf_op jit(solution)/shard_map/resid_back/pallas_call | solution.py:343
  342.8 20.8 %outer_wide.2 = (bf16[16,32,5120]{2,1,0:T(8,128)(2,1)}, bf16[16,32,5120]{2,1,0:T(8,128)(2,1)}) custom-call(bf16[1024,1024]{1,0:T(8,128)(2,1)} %get-tuple-element.164.low_ref.refs_0_.refs_1_.refs_2_, bf16[1024,1024]{1,0:T(8,128)(2,1)} %get-tuple-element.164.low_ref.refs_0_.refs_1_.refs_2_, ...), custom_call_target="tpu_custom_call" | custom-call | flops 10737418240 | bytes 29360128 | tf_op jit(solution)/shard_map/outer_wide/pallas_call | solution.py:410
  366.6 11.6 %collective-permute-done.38.came3_ref = bf16[4,128,512]{2,1,0:T(8,128)(2,1)S(1)} collective-permute-done((bf16[4,128,512]{2,1,0:T(8,128)(2,1)}, bf16[4,128,512]{2,1,0:T(8,128)(2,1)S(1)}, u32[]{:S(2)}, u32[]{:S(2)}) %collective-permute-start.38) | collective-permute-done | bytes 524320 | tf_op jit(solution)/shard_map/ppermute | solution.py:433
  382.1 13.6 %attend_back.2 = (bf16[1024,1024]{1,0:T(8,128)(2,1)}, bf16[1024,1024]{1,0:T(8,128)(2,1)}, bf16[1024,1024]{1,0:T(8,128)(2,1)}) custom-call(bf16[1024,1024]{1,0:T(8,128)(2,1)} %fusion.q_ref.refs_0_, bf16[1024,1024]{1,0:T(8,128)(2,1)} %convolution_convert_fusion.k_ref.refs_1_, bf16[1024,1024]{1,0:T(8,128)(2,1)} %add_convert_fusion.1.v_ref.refs_2_, ...), custom_call_target="tpu_custom_call" | custom-call | flops 12884901888 | bytes 15728640 | tf_op jit(solution)/shard_map/attend_back/pallas_call | solution.py:69
  407.1 13.5 %attend_back.3 = (bf16[1024,1024]{1,0:T(8,128)(2,1)}, bf16[1024,1024]{1,0:T(8,128)(2,1)}, bf16[1024,1024]{1,0:T(8,128)(2,1)}) custom-call(bf16[1024,1024]{1,0:T(8,128)(2,1)} %fusion.q_ref.refs_0_, bf16[1024,1024]{1,0:T(8,128)(2,1)} %convolution_convert_fusion.k_ref.refs_1_, ...), custom_call_target="tpu_custom_call", output_to_operand_aliasing={{0}: (5, {}), {1}: (6, {}), {2}: (7, {})} | custom-call | flops 12884901888 | bytes 15728640 | tf_op jit(solution)/shard_map/attend_back/pallas_call | solution.py:69
  420.7 14.4 %outer_wide.3 = (bf16[16,32,3072]{2,1,0:T(8,128)(2,1)}, bf16[16,32,3072]{2,1,0:T(8,128)(2,1)}) custom-call(bf16[1024,1024]{1,0:T(8,128)(2,1)} %refs_2_.1, bf16[1024,1024]{1,0:T(8,128)(2,1)} %refs_2_.1, bf16[1024,1024]{1,0:T(8,128)(2,1)} %refs_2_.1, bf16[1024,1024]{1,0:T(8,128)(2,1)} %get-tuple-element.239.refs_3_, ...), custom_call_target="tpu_custom_call" | custom-call | flops 6442450944 | bytes 18874368 | tf_op jit(solution)/shard_map/outer_wide/pallas_call | solution.py:410
  447.9 15.9 %collective-permute-done.42 = bf16[128,1024]{1,0:T(8,128)(2,1)} collective-permute-done((bf16[128,1024]{1,0:T(8,128)(2,1)}, bf16[128,1024]{1,0:T(8,128)(2,1)}, u32[]{:S(2)}, u32[]{:S(2)}) %collective-permute-start.42) | collective-permute-done | bytes 262176 | tf_op jit(solution)/shard_map/ppermute | solution.py:435
  514.2 13.5 %collective-permute-done.47.came1_ref = bf16[4,2,32,1536]{3,2,1,0:T(8,128)(2,1)S(1)} collective-permute-done((bf16[4,2,32,1536]{3,2,1,0:T(8,128)(2,1)}, bf16[4,2,32,1536]{3,2,1,0:T(8,128)(2,1)S(1)}, u32[]{:S(2)}, u32[]{:S(2)}) %collective-permute-start.47) | collective-permute-done | bytes 786464 | tf_op jit(solution)/shard_map/ppermute | solution.py:433
  550.4 16.4 %collective-permute-start.51 = (bf16[32,3072]{1,0:T(8,128)(2,1)}, bf16[32,3072]{1,0:T(8,128)(2,1)S(1)}, u32[]{:S(2)}, u32[]{:S(2)}) collective-permute-start(bf16[32,3072]{1,0:T(8,128)(2,1)} %get-tuple-element.253), channel_id=1, source_target_pairs={{0,8},{1,9},{2,10},{3,11},{4,12},{5,13},{6,14},{7,15},{8,16},{9,17... | collective-permute-start | bytes 589832 | tf_op jit(solution)/shard_map/ppermute | solution.py:435
  566.8 10.8 %collective-permute-done.57 = bf16[32,5120]{1,0:T(8,128)(2,1)S(1)} collective-permute-done((bf16[32,5120]{1,0:T(8,128)(2,1)}, bf16[32,5120]{1,0:T(8,128)(2,1)S(1)}, u32[]{:S(2)}, u32[]{:S(2)}) %collective-permute-start.57) | collective-permute-done | bytes 327712 | tf_op jit(solution)/shard_map/ppermute | solution.py:435
  (303 shorter events, 234.2 us)
Async XLA Ops:
  7.2 173.6 %all-gather.3.cloned.1.call-start = ((), (), s32[]{:S(2)}) async-start(), calls=%async_computation | async-start | bytes 2162688 | tf_op jit(solution)/shard_map/all_gather | solution.py:697
  7.9 181.1 %all-gather.5.cloned.1.call-start = ((), (), s32[]{:S(2)}) async-start(), calls=%async_computation.1 | async-start | bytes 8650752 | tf_op jit(solution)/shard_map/all_gather | solution.py:696
  57.3 23.5 %collective-permute-start.4 = (bf16[8,32,1024]{2,1,0:T(8,128)(2,1)S(1)}, bf16[8,32,1024]{2,1,0:T(8,128)(2,1)S(1)}, u32[]{:S(2)}, u32[]{:S(2)}) collective-permute-start(bf16[8,32,1024]{2,1,0:T(8,128)(2,1)S(1)} %constant_dynamic-update-slice_fusion.refs_0_), channel_id=1, source_target_pairs={{0,2},{1,3},{2,0},{3,1},{4,6},{5,7},{6,4},{7,5},{8,10},{9,11},{10,... | collective-permute-start | bytes 1572872 | tf_op jit(solution)/shard_map/ppermute | solution.py:433
  59.4 21.9 %collective-permute-start.11 = (bf16[8,32,1024]{2,1,0:T(8,128)(2,1)S(1)}, bf16[8,32,1024]{2,1,0:T(8,128)(2,1)S(1)}, u32[]{:S(2)}, u32[]{:S(2)}) collective-permute-start(bf16[8,32,1024]{2,1,0:T(8,128)(2,1)S(1)} %constant_dynamic-update-slice_fusion.5.refs_4_), channel_id=1, source_target_pairs={{0,4},{1,5},{2,6},{3,7},{4,0},{5,1},{6,2},{7,3},{8,12},{9,13},{10,... | collective-permute-start | bytes 1572872 | tf_op jit(solution)/shard_map/ppermute | solution.py:433
  60.5 22.2 %collective-permute-start.19 = (bf16[8,32,1152]{2,1,0:T(8,128)(2,1)S(1)}, bf16[8,32,1152]{2,1,0:T(8,128)(2,1)S(1)}, u32[]{:S(2)}, u32[]{:S(2)}) collective-permute-start(bf16[8,32,1152]{2,1,0:T(8,128)(2,1)S(1)} %constant_dynamic-update-slice_fusion.10.refs_8_), channel_id=1, source_target_pairs={{0,1},{1,0},{2,3},{3,2},{4,5},{5,4},{6,7},{7,6},{8,9},{9,8},{10,11... | collective-permute-start | bytes 1769480 | tf_op jit(solution)/shard_map/ppermute | solution.py:433
  139.0 26.0 %collective-permute-start.27 = (bf16[4,128,512]{2,1,0:T(8,128)(2,1)S(1)}, bf16[4,128,512]{2,1,0:T(8,128)(2,1)S(1)}, u32[]{:S(2)}, u32[]{:S(2)}) collective-permute-start(bf16[4,128,512]{2,1,0:T(8,128)(2,1)S(1)} %pad_maximum_fusion), channel_id=1, source_target_pairs={{0,4},{1,5},{2,6},{3,7},{4,0},{5,1},{6,2},{7,3},{8,12},{9,13},{10,... | collective-permute-start | bytes 1572872 | tf_op jit(solution)/shard_map/ppermute | solution.py:433
  163.4 25.5 %collective-permute-start.30 = (bf16[8,128,512]{2,1,0:T(8,128)(2,1)S(1)}, bf16[8,128,512]{2,1,0:T(8,128)(2,1)S(1)}, u32[]{:S(2)}, u32[]{:S(2)}) collective-permute-start(bf16[8,128,512]{2,1,0:T(8,128)(2,1)S(1)} %constant_dynamic-update-slice_fusion.20.refs_4_), channel_id=1, source_target_pairs={{0,4},{1,5},{2,6},{3,7},{4,0},{5,1},{6,2},{7,3},{8,12},{9,13},{10,... | collective-permute-start | bytes 3145736 | tf_op jit(solution)/shard_map/ppermute | solution.py:433
  165.0 24.0 %collective-permute-start.29 = (bf16[8,128,512]{2,1,0:T(8,128)(2,1)S(1)}, bf16[8,128,512]{2,1,0:T(8,128)(2,1)}, u32[]{:S(2)}, u32[]{:S(2)}) collective-permute-start(bf16[8,128,512]{2,1,0:T(8,128)(2,1)S(1)} %constant_dynamic-update-slice_fusion.15.refs_0_), channel_id=1, source_target_pairs={{0,2},{1,3},{2,0},{3,1},{4,6},{5,7},{6,4},{7,5},{8,10},{9,11},{10,... | collective-permute-start | bytes 3145736 | tf_op jit(solution)/shard_map/ppermute | solution.py:433
  291.7 35.2 %collective-permute-start.36 = (bf16[4,2,128,512]{3,2,1,0:T(8,128)(2,1)}, bf16[4,2,128,512]{3,2,1,0:T(8,128)(2,1)S(1)}, u32[]{:S(2)}, u32[]{:S(2)}) collective-permute-start(bf16[4,2,128,512]{3,2,1,0:T(8,128)(2,1)} %get-tuple-element.183), channel_id=1, source_target_pairs={{0,2},{1,3},{2,0},{3,1},{4,6},{5,7},{6,4},{7,5},{8,10},{9,11},{10,... | collective-permute-start | bytes 3145736 | tf_op jit(solution)/shard_map/ppermute | solution.py:433
  292.3 34.6 %collective-permute-start.37 = (bf16[4,2,128,512]{3,2,1,0:T(8,128)(2,1)}, bf16[4,2,128,512]{3,2,1,0:T(8,128)(2,1)S(1)}, u32[]{:S(2)}, u32[]{:S(2)}) collective-permute-start(bf16[4,2,128,512]{3,2,1,0:T(8,128)(2,1)} %get-tuple-element.184), channel_id=1, source_target_pairs={{0,4},{1,5},{2,6},{3,7},{4,0},{5,1},{6,2},{7,3},{8,12},{9,13},{10,... | collective-permute-start | bytes 3145736 | tf_op jit(solution)/shard_map/ppermute | solution.py:433
  363.6 32.0 %collective-permute-start.40 = (bf16[16,32,5120]{2,1,0:T(8,128)(2,1)}, bf16[16,32,5120]{2,1,0:T(8,128)(2,1)S(1)}, u32[]{:S(2)}, u32[]{:S(2)}) collective-permute-start(bf16[16,32,5120]{2,1,0:T(8,128)(2,1)} %get-tuple-element.204), channel_id=1, source_target_pairs={{0,1},{1,0},{2,3},{3,2},{4,5},{5,4},{6,7},{7,6},{8,9},{9,8},{10,11... | collective-permute-start | bytes 15728648 | tf_op jit(solution)/shard_map/ppermute | solution.py:433
  404.7 63.1 %collective-permute-start.44 = (bf16[4,2,32,2560]{3,2,1,0:T(8,128)(2,1)}, bf16[4,2,32,2560]{3,2,1,0:T(8,128)(2,1)}, u32[]{:S(2)}, u32[]{:S(2)}) collective-permute-start(bf16[4,2,32,2560]{3,2,1,0:T(8,128)(2,1)} %get-tuple-element.217), channel_id=1, source_target_pairs={{0,2},{1,3},{2,0},{3,1},{4,6},{5,7},{6,4},{7,5},{8,10},{9,11},{10,... | collective-permute-start | bytes 3932168 | tf_op jit(solution)/shard_map/ppermute | solution.py:433
  406.2 61.7 %collective-permute-start.45 = (bf16[4,2,32,2560]{3,2,1,0:T(8,128)(2,1)}, bf16[4,2,32,2560]{3,2,1,0:T(8,128)(2,1)}, u32[]{:S(2)}, u32[]{:S(2)}) collective-permute-start(bf16[4,2,32,2560]{3,2,1,0:T(8,128)(2,1)} %get-tuple-element.218), channel_id=1, source_target_pairs={{0,4},{1,5},{2,6},{3,7},{4,0},{5,1},{6,2},{7,3},{8,12},{9,13},{10,... | collective-permute-start | bytes 3932168 | tf_op jit(solution)/shard_map/ppermute | solution.py:433
  435.1 62.0 %collective-permute-start.46 = (bf16[16,32,3072]{2,1,0:T(8,128)(2,1)}, bf16[16,32,3072]{2,1,0:T(8,128)(2,1)S(1)}, u32[]{:S(2)}, u32[]{:S(2)}) collective-permute-start(bf16[16,32,3072]{2,1,0:T(8,128)(2,1)} %get-tuple-element.225), channel_id=1, source_target_pairs={{0,1},{1,0},{2,3},{3,2},{4,5},{5,4},{6,7},{7,6},{8,9},{9,8},{10,11... | collective-permute-start | bytes 9437192 | tf_op jit(solution)/shard_map/ppermute | solution.py:433
  439.4 24.4 %collective-permute-start.42 = (bf16[128,1024]{1,0:T(8,128)(2,1)}, bf16[128,1024]{1,0:T(8,128)(2,1)}, u32[]{:S(2)}, u32[]{:S(2)}) collective-permute-start(bf16[128,1024]{1,0:T(8,128)(2,1)} %get-tuple-element.212), channel_id=1, source_target_pairs={{0,16},{1,17},{2,18},{3,19},{4,20},{5,21},{6,22},{7,23},{8,24},{9,... | collective-permute-start | bytes 786440 | tf_op jit(solution)/shard_map/ppermute | solution.py:435
  486.9 48.1 %collective-permute-start.54 = (bf16[4,32,2560]{2,1,0:T(8,128)(2,1)}, bf16[4,32,2560]{2,1,0:T(8,128)(2,1)}, u32[]{:S(2)}, u32[]{:S(2)}) collective-permute-start(bf16[4,32,2560]{2,1,0:T(8,128)(2,1)} %get-tuple-element.237), channel_id=1, source_target_pairs={{0,4},{1,5},{2,6},{3,7},{4,0},{5,1},{6,2},{7,3},{8,12},{9,13},{10,... | collective-permute-start | bytes 1966088 | tf_op jit(solution)/shard_map/ppermute | solution.py:433
  496.5 38.5 %collective-permute-start.55 = (bf16[4,32,2560]{2,1,0:T(8,128)(2,1)}, bf16[4,32,2560]{2,1,0:T(8,128)(2,1)}, u32[]{:S(2)}, u32[]{:S(2)}) collective-permute-start(bf16[4,32,2560]{2,1,0:T(8,128)(2,1)} %get-tuple-element.238), channel_id=1, source_target_pairs={{0,2},{1,3},{2,0},{3,1},{4,6},{5,7},{6,4},{7,5},{8,10},{9,11},{10,... | collective-permute-start | bytes 1966088 | tf_op jit(solution)/shard_map/ppermute | solution.py:433
  503.9 23.8 %collective-permute-start.47 = (bf16[4,2,32,1536]{3,2,1,0:T(8,128)(2,1)}, bf16[4,2,32,1536]{3,2,1,0:T(8,128)(2,1)S(1)}, u32[]{:S(2)}, u32[]{:S(2)}) collective-permute-start(bf16[4,2,32,1536]{3,2,1,0:T(8,128)(2,1)} %get-tuple-element.241), channel_id=1, source_target_pairs={{0,2},{1,3},{2,0},{3,1},{4,6},{5,7},{6,4},{7,5},{8,10},{9,11},{10,... | collective-permute-start | bytes 2359304 | tf_op jit(solution)/shard_map/ppermute | solution.py:433
  505.4 22.3 %collective-permute-start.48 = (bf16[4,2,32,1536]{3,2,1,0:T(8,128)(2,1)}, bf16[4,2,32,1536]{3,2,1,0:T(8,128)(2,1)S(1)}, u32[]{:S(2)}, u32[]{:S(2)}) collective-permute-start(bf16[4,2,32,1536]{3,2,1,0:T(8,128)(2,1)} %get-tuple-element.242), channel_id=1, source_target_pairs={{0,4},{1,5},{2,6},{3,7},{4,0},{5,1},{6,2},{7,3},{8,12},{9,13},{10,... | collective-permute-start | bytes 2359304 | tf_op jit(solution)/shard_map/ppermute | solution.py:433
  540.2 37.4 %collective-permute-start.57 = (bf16[32,5120]{1,0:T(8,128)(2,1)}, bf16[32,5120]{1,0:T(8,128)(2,1)S(1)}, u32[]{:S(2)}, u32[]{:S(2)}) collective-permute-start(bf16[32,5120]{1,0:T(8,128)(2,1)} %get-tuple-element.262), channel_id=1, source_target_pairs={{0,16},{1,17},{2,18},{3,19},{4,20},{5,21},{6,22},{7,23},{8,24},{9,... | collective-permute-start | bytes 983048 | tf_op jit(solution)/shard_map/ppermute | solution.py:435
  540.2 37.4 %collective-permute-start.56 = (bf16[32,5120]{1,0:T(8,128)(2,1)}, bf16[32,5120]{1,0:T(8,128)(2,1)S(1)}, u32[]{:S(2)}, u32[]{:S(2)}) collective-permute-start(bf16[32,5120]{1,0:T(8,128)(2,1)} %get-tuple-element.261), channel_id=1, source_target_pairs={{0,8},{1,9},{2,10},{3,11},{4,12},{5,13},{6,14},{7,15},{8,16},{9,17... | collective-permute-start | bytes 983048 | tf_op jit(solution)/shard_map/ppermute | solution.py:435
  545.0 35.3 %collective-permute-start.53 = (bf16[32,3072]{1,0:T(8,128)(2,1)}, bf16[32,3072]{1,0:T(8,128)(2,1)S(1)}, u32[]{:S(2)}, u32[]{:S(2)}) collective-permute-start(bf16[32,3072]{1,0:T(8,128)(2,1)} %get-tuple-element.255), channel_id=1, source_target_pairs={{0,24},{1,25},{2,26},{3,27},{4,28},{5,29},{6,30},{7,31},{8,0},{9,1... | collective-permute-start | bytes 589832 | tf_op jit(solution)/shard_map/ppermute | solution.py:435
  548.0 33.9 %collective-permute-start.52 = (bf16[32,3072]{1,0:T(8,128)(2,1)}, bf16[32,3072]{1,0:T(8,128)(2,1)S(1)}, u32[]{:S(2)}, u32[]{:S(2)}) collective-permute-start(bf16[32,3072]{1,0:T(8,128)(2,1)} %get-tuple-element.254), channel_id=1, source_target_pairs={{0,16},{1,17},{2,18},{3,19},{4,20},{5,21},{6,22},{7,23},{8,24},{9,... | collective-permute-start | bytes 589832 | tf_op jit(solution)/shard_map/ppermute | solution.py:435
  550.4 31.4 %collective-permute-start.51 = (bf16[32,3072]{1,0:T(8,128)(2,1)}, bf16[32,3072]{1,0:T(8,128)(2,1)S(1)}, u32[]{:S(2)}, u32[]{:S(2)}) collective-permute-start(bf16[32,3072]{1,0:T(8,128)(2,1)} %get-tuple-element.253), channel_id=1, source_target_pairs={{0,8},{1,9},{2,10},{3,11},{4,12},{5,13},{6,14},{7,15},{8,16},{9,17... | collective-permute-start | bytes 589832 | tf_op jit(solution)/shard_map/ppermute | solution.py:435
  (86 other events, 1123.0 us)
Sparse Core Ops, SparseCore 0:
  10.9 66.3 all-gather.2
  80.1 92.2 all-gather.4
